TPU v7x, 256 devices: a whole 4x4x8 slice. The times are simulated.
256 devices in a mesh: ctx: 128 (over x_lo, y, z, core), head: 2 (over x_hi).
Axes of the slice: x: 4 (x_hi: 2, x_lo: 2; x = x_hi * 2 + x_lo), y: 4, z: 8, core: 2. Of those that a mesh axis runs over, the one named last changes fastest.
Arguments:
- block_order: int32 [256], replicated, may hold values from 0 to 255, as said below
- conv_input: bfloat16 [16384, 2048], P('ctx', 'head'), may hold values from -0.125 to 0.125
- conv_filter: float32 [2048, 128], P('head'), may hold values from -0.5 to 0.5
- query_rows: bfloat16 [16384, 256], P('ctx', 'head'), may hold values from -40 to 40
- key_rows: bfloat16 [16384, 256], P('ctx', 'head'), may hold values from -6 to 6
- value_rows: bfloat16 [16384, 256], P('ctx', 'head'), may hold values from -6 to 6
- out_grad: bfloat16 [16384, 256], P('ctx', 'head'), may hold values from -6 to 6
- qkv_weight: bfloat16 [3, 2048, 256], P(None, None, 'head'), may hold values from -0.21875 to 0.21875
Outputs:
- input_grad: bfloat16 [16384, 2048], P('ctx', 'head')
- filter_grad: float32 [2048, 128], P('head')
Inputs may be any that keep to these rules, and one draw needn't show every extreme that they name: `block_order`: A permutation of the 256 blocks of 64 positions; entries 2i and 2i + 1 name the blocks held by index i of ctx, either blocks 2i and 2i + 1 or blocks i and 255 - i, in either order.
All inputs are finite; a program needn't handle non-finite values.
Results may differ from a plain program's by a relative error of at most 0.0064.
Values may be sent and summed in bfloat16 or wider, within the bound.
No kernel may reach another device: no remote copies, remote signals or barrier semaphores. Data moves between devices by JAX's collectives and lax.ppermute only.
A program may use at most 128 MiB of HBM per device.

v0:
```python
import jax
import jax.numpy as jnp
from jax import lax
from jax.sharding import PartitionSpec as P

HD = 128


LOWEST = -1e30


def passed_along(block, axis, distance):
    devices = range(lax.axis_size(axis))
    route = [(i - distance, i) for i in devices if i - distance in devices]
    return lax.ppermute(block, axis, route)


def all_positions(block_order, block_len):
    offsets = jnp.arange(block_len, dtype=jnp.int32)
    return (block_order[:, None] * block_len + offsets[None, :]).reshape(-1)


def split_heads(matrix, head_dim):
    return matrix.reshape(matrix.shape[0], matrix.shape[1] // head_dim, head_dim)


def visible_mask(key_pos, query_pos):
    return key_pos[None, None, :] <= query_pos[None, :, None]


def score_block(left_rows, right_rows, factor):
    return (
        jnp.einsum("qhd,khd->hqk", left_rows, right_rows, preferred_element_type=jnp.float32)
        * factor
    )


def make_forward(queries, grads_out, query_pos, positions, head_dim, softmax_scale):

    def update(current, pieces, first_row):
        key_piece = split_heads(pieces[0], head_dim)
        value_piece = split_heads(pieces[1], head_dim)

        def compute(running):
            running_max, norm_sum, cross_sum = running
            visible = visible_mask(positions, query_pos)
            scores = jnp.where(visible, score_block(queries, key_piece, softmax_scale), LOWEST)
            new_max = jnp.maximum(running_max, jnp.max(scores, axis=2))
            weights = jnp.where(visible, jnp.exp(scores - new_max[:, :, None]), 0.0)
            dprobs = score_block(grads_out, value_piece, 1.0)
            return (new_max, jnp.sum(weights, axis=2), jnp.sum(weights * dprobs, axis=2))

        return compute(current)

    return update


def make_query_grads(
    queries, grads_out, query_pos, positions, lse_rows, delta_rows, head_dim, softmax_scale
):

    def update(current, pieces, first_row):
        key_piece = split_heads(pieces[0], head_dim)
        value_piece = split_heads(pieces[1], head_dim)

        def compute(running):
            visible = visible_mask(positions, query_pos)
            scores = score_block(queries, key_piece, softmax_scale)
            soft_probs = jnp.where(visible, jnp.exp(scores - lse_rows[:, :, None]), 0.0)
            dprobs = score_block(grads_out, value_piece, 1.0)
            dscores = (soft_probs * (dprobs - delta_rows[:, :, None])).astype(jnp.bfloat16)
            return jnp.einsum(
                "hqk,khd->qhd", dscores, key_piece, preferred_element_type=jnp.float32
            )

        return compute(current)

    return update


def key_core(
    query_piece,
    grad_piece,
    lse_piece,
    delta_piece,
    query_pos,
    key_piece,
    value_piece,
    key_pos,
    softmax_scale,
):
    visible = visible_mask(key_pos, query_pos)
    scores = score_block(query_piece, key_piece, softmax_scale)
    soft_probs = jnp.where(visible, jnp.exp(scores - lse_piece[:, :, None]), 0.0)
    dprobs = score_block(grad_piece, value_piece, 1.0)
    dscores = (soft_probs * (dprobs - delta_piece[:, :, None])).astype(jnp.bfloat16)
    key_sum = jnp.einsum("hqk,qhd->khd", dscores, query_piece, preferred_element_type=jnp.float32)
    value_sum = jnp.einsum(
        "hqk,qhd->khd",
        soft_probs.astype(jnp.bfloat16),
        grad_piece,
        preferred_element_type=jnp.float32,
    )
    return (key_sum, value_sum)


def make_key_grads(key_local, value_local, key_pos, positions, head_dim, softmax_scale):

    def update(current, pieces, first_row):
        query_piece = split_heads(pieces[0], head_dim)
        grad_piece = split_heads(pieces[1], head_dim)

        def compute(running):
            return key_core(
                query_piece,
                grad_piece,
                pieces[2].T,
                pieces[3].T,
                positions,
                key_local,
                value_local,
                key_pos,
                softmax_scale,
            )

        return compute(current)

    return update


def fold_keys(key_rows, value_rows, update, initial):
    return update(
        initial,
        (
            lax.all_gather(key_rows, "ctx", axis=0, tiled=True),
            lax.all_gather(value_rows, "ctx", axis=0, tiled=True),
        ),
        jnp.int32(0),
    )


def local(
    block_order, conv_input, conv_filter, query_rows, key_rows, value_rows, out_grad, qkv_weight
):
    head_dim = HD
    tok_rows = query_rows.shape[0]
    block_len = tok_rows // 2
    device = lax.axis_index("ctx")
    devices_ctx = lax.axis_size("ctx")
    positions = all_positions(block_order, block_len)
    query_pos = lax.dynamic_slice_in_dim(positions, device * tok_rows, tok_rows, 0)
    softmax_scale = head_dim ** (-0.5)
    queries = split_heads(query_rows, head_dim)
    grads_out = split_heads(out_grad, head_dim)
    keys_local = split_heads(key_rows, head_dim)
    values_local = split_heads(value_rows, head_dim)
    head_count = queries.shape[1]
    initial_stats = (
        jnp.full((head_count, tok_rows), LOWEST, jnp.float32),
        jnp.zeros((head_count, tok_rows), jnp.float32),
        jnp.zeros((head_count, tok_rows), jnp.float32),
    )
    zeros_grad = jnp.zeros((tok_rows, head_count, head_dim), jnp.float32)
    forward = make_forward(queries, grads_out, query_pos, positions, head_dim, softmax_scale)
    running_max, norm_sum, cross_sum = fold_keys(key_rows, value_rows, forward, initial_stats)
    lse_rows = running_max + jnp.log(norm_sum)
    delta_rows = cross_sum / norm_sum
    query_update = make_query_grads(
        queries, grads_out, query_pos, positions, lse_rows, delta_rows, head_dim, softmax_scale
    )
    query_acc = fold_keys(key_rows, value_rows, query_update, zeros_grad)
    key_update = make_key_grads(
        keys_local, values_local, query_pos, positions, head_dim, softmax_scale
    )
    key_acc, value_acc = key_update(
        (zeros_grad, zeros_grad),
        (
            lax.all_gather(query_rows.astype(jnp.float32), "ctx", axis=0, tiled=True).astype(
                jnp.bfloat16
            ),
            lax.all_gather(out_grad.astype(jnp.float32), "ctx", axis=0, tiled=True).astype(
                jnp.bfloat16
            ),
            lax.all_gather(lse_rows.T, "ctx", axis=0, tiled=True),
            lax.all_gather(delta_rows.T, "ctx", axis=0, tiled=True),
        ),
        jnp.int32(0),
    )
    query_grad = (softmax_scale * query_acc).astype(jnp.bfloat16).reshape(tok_rows, -1)
    key_grad = (softmax_scale * key_acc).astype(jnp.bfloat16).reshape(tok_rows, -1)
    value_grad = value_acc.astype(jnp.bfloat16).reshape(tok_rows, -1)
    stacked = jnp.stack((query_grad, key_grad, value_grad), axis=1)
    channel_terms = jnp.einsum(
        "tjf,jcf->tc", stacked, qkv_weight, preferred_element_type=jnp.float32
    )
    conv_grad = lax.psum_scatter(channel_terms, "head", scatter_dimension=1, tiled=True).astype(
        jnp.bfloat16
    )
    channels = conv_grad.shape[1]
    tap_count = conv_filter.shape[1]
    reach_blocks = -(-(tap_count - 1) // block_len)
    slots_in = conv_input.reshape(2, block_len, channels)
    slots_grad = conv_grad.reshape(2, block_len, channels)
    my_ids = lax.dynamic_slice_in_dim(block_order, device * 2, 2, 0)
    cand_in = [slots_in]
    cand_grad = [slots_grad]
    cand_ids = [my_ids]
    for offset in list(range(1, reach_blocks + 1)) + list(range(-reach_blocks, 0)):
        moved_in, moved_grad = passed_along((slots_in, slots_grad), "ctx", offset)
        source = device - offset
        in_range = jnp.logical_and(source >= 0, source < devices_ctx)
        source_ids = lax.dynamic_slice_in_dim(
            block_order, jnp.clip(source, 0, devices_ctx - 1) * 2, 2, 0
        )
        cand_in.append(moved_in)
        cand_grad.append(moved_grad)
        cand_ids.append(jnp.where(in_range, source_ids, -1000))
    all_in = jnp.concatenate(cand_in, axis=0)
    all_grad = jnp.concatenate(cand_grad, axis=0)
    all_ids = jnp.concatenate(cand_ids, axis=0)
    earlier_ids = my_ids[:, None] - jnp.arange(reach_blocks, 0, -1, dtype=jnp.int32)[None, :]
    later_ids = my_ids[:, None] + jnp.arange(1, reach_blocks + 1, dtype=jnp.int32)[None, :]
    pick_earlier = (earlier_ids[:, :, None] == all_ids[None, None, :]).astype(jnp.bfloat16)
    pick_later = (later_ids[:, :, None] == all_ids[None, None, :]).astype(jnp.bfloat16)
    rim_earlier = jnp.einsum(
        "srn,nbc->srbc", pick_earlier, all_in, preferred_element_type=jnp.float32
    ).astype(jnp.bfloat16)
    rim_later = jnp.einsum(
        "srn,nbc->srbc", pick_later, all_grad, preferred_element_type=jnp.float32
    ).astype(jnp.bfloat16)
    ext_in = jnp.concatenate(
        (rim_earlier.reshape(2, reach_blocks * block_len, channels), slots_in), axis=1
    )
    ext_in = ext_in[:, reach_blocks * block_len - (tap_count - 1) :]
    ext_grad = jnp.concatenate(
        (slots_grad, rim_later.reshape(2, reach_blocks * block_len, channels)), axis=1
    )
    ext_grad = ext_grad[:, : block_len + tap_count - 1]
    kernel = conv_filter.T[:, None, :]
    input_part = lax.conv_general_dilated(
        ext_grad.astype(jnp.float32),
        kernel,
        (1,),
        "VALID",
        dimension_numbers=("NWC", "WIO", "NWC"),
        feature_group_count=channels,
        precision=lax.Precision.HIGHEST,
    )
    input_grad = input_part.reshape(tok_rows, channels).astype(jnp.bfloat16)
    wide_in = jnp.transpose(ext_in.astype(jnp.float32), (1, 0, 2)).reshape(
        1, block_len + tap_count - 1, 2 * channels
    )
    wide_grad = jnp.transpose(slots_grad.astype(jnp.float32), (1, 0, 2)).reshape(
        block_len, 1, 2 * channels
    )
    lagged = lax.conv_general_dilated(
        wide_in,
        wide_grad,
        (1,),
        "VALID",
        dimension_numbers=("NWC", "WIO", "NWC"),
        feature_group_count=2 * channels,
        precision=lax.Precision.HIGHEST,
    )
    filter_part = jnp.sum(lagged.reshape(tap_count, 2, channels), axis=1)[::-1].T
    filter_grad = lax.psum(filter_part, "ctx")
    return (input_grad, filter_grad)


def solution(mesh):
    return jax.shard_map(
        local,
        mesh=mesh,
        in_specs=(
            P(),
            P("ctx", "head"),
            P("head", None),
            P("ctx", "head"),
            P("ctx", "head"),
            P("ctx", "head"),
            P("ctx", "head"),
            P(None, None, "head"),
        ),
        out_specs=(P("ctx", "head"), P("head", None)),
        check_vma=False,
    )
```

profile of v0, /device:TPU:6, one launch (start us, length us, event | category | flops | bytes accessed | tf_op | source)
XLA Modules:
  0.0 1969.0 jit_solution(9053537933328801559)
XLA Ops:
  7.2 0.0 all-gather.9.cloned.1.call-start
  7.2 0.7 all-gather.9.cloned.1.call-update
  7.9 0.0 all-gather.11.cloned.1.call-start
  8.0 0.7 all-gather.11.cloned.1.call-update
  8.7 0.0 all-gather.13.cloned.1.call-start
  8.7 0.7 all-gather.13.cloned.1.call-update
  9.4 0.0 all-gather.15.cloned.1.call-start
  9.4 0.5 all-gather.15.cloned.1.call-update
  10.0 0.0 reduce-scatter.2.cloned.1.call-start
  10.0 0.7 broadcast_multiply_fusion
  10.7 0.1 iota_add_fusion
  10.8 0.1 add.104
  10.9 0.1 dynamic_slice.18
  11.0 217.7 %all-gather.9.cloned.1.call-done = bf16[16384,128]{1,0:T(8,128)(2,1)} async-done(((bf16[128,128]{1,0:T(8,128)(2,1)}), bf16[16384,128]{1,0:T(8,128)(2,1)}) %all-gather.9.cloned.1.call-update) | async-done | bytes 4194320 | tf_op jit(solution)/shard_map/all_gather | solution.py:135
  228.7 6.8 fusion.7
  235.5 209.3 %all-gather.11.cloned.1.call-done = bf16[16384,128]{1,0:T(8,128)(2,1)} async-done(((bf16[128,128]{1,0:T(8,128)(2,1)}), bf16[16384,128]{1,0:T(8,128)(2,1)}) %all-gather.11.cloned.1.call-update) | async-done | bytes 4194320 | tf_op jit(solution)/shard_map/all_gather | solution.py:136
  444.8 11.0 multiply_reduce_fusion
  455.8 152.7 %all-gather.2 = f32[128,1,128]{2,1,0:T(1,128)S(1)} all-gather(f32[1,1,128]{2,1,0:T(1,128)S(1)} %bitcast.85), channel_id=2, replica_groups=mesh['ctx'=128,'head'=2] {'ctx'}, dimensions={0}, use_global_device_ids=true | all-gather | bytes 66048 | tf_op jit(solution)/shard_map/all_gather | solution.py:184
  608.6 150.4 %all-gather.3 = f32[128,1,128]{2,1,0:T(1,128)S(1)} all-gather(f32[1,1,128]{2,1,0:T(1,128)S(1)} %bitcast.84), channel_id=3, replica_groups=mesh['ctx'=128,'head'=2] {'ctx'}, dimensions={0}, use_global_device_ids=true | all-gather | bytes 66048 | tf_op jit(solution)/shard_map/all_gather | solution.py:185
  759.0 14.5 fusion.3
  773.5 6.3 fusion.51
  779.9 97.2 %all-gather.15.cloned.1.call-done = bf16[16384,128]{1,0:T(8,128)(2,1)} async-done(((bf16[128,128]{1,0:T(8,128)(2,1)}), bf16[16384,128]{1,0:T(8,128)(2,1)}) %all-gather.15.cloned.1.call-update) | async-done | bytes 4194320 | tf_op jit(solution)/shard_map/all_gather | solution.py:181
  877.1 5.9 fusion.59
  883.0 10.2 fusion.54
  893.2 1.6 convolution_bitcast_fusion
  894.8 0.0 reduce-scatter.2.cloned.1.call-update
  894.9 0.0 all-reduce.2.cloned.1.call-start
  894.9 0.3 copy.52
  895.2 1.9 collective-permute-start.4
  897.1 1.9 collective-permute-start.5
  899.1 8.1 collective-permute-start.6
  907.2 3.3 collective-permute-start.7
  910.6 0.1 broadcast_select_fusion
  910.7 1.0 copy.46
  911.7 0.1 concatenate.15
  911.8 0.1 broadcast_subtract_fusion
  911.9 0.7 collective-permute-done.5
  912.6 0.5 collective-permute-done.6
  913.1 2.8 collective-permute-done.7
  915.9 8.2 concatenate.18
  924.1 2.2 fusion.25
  926.3 0.1 copy.53
  926.5 0.2 fusion.64
  926.7 0.8 copy.54
  927.5 1.8 reshape.306
  929.2 1.1 convert_element_type.99
  930.3 0.3 copy.63
  930.6 1.9 collective-permute-start
  932.5 2.2 collective-permute-start.1
  934.8 8.3 collective-permute-start.2
  943.0 3.0 collective-permute-start.3
  946.0 0.2 reshape.307
  946.3 12.9 convolution_reduce_fusion
  959.2 2.1 reshape.292
  961.3 1.2 reduce_sum.29
  962.5 2.7 rev.3
  965.3 10.0 concatenate.16
  975.3 2.2 fusion.22
  977.5 0.1 copy.43
  977.6 0.5 copy.45
  978.2 5.3 convolution_convert_fusion
  983.5 0.8 copy.47
  984.3 975.8 %all-reduce.2.cloned.1.call-done = f32[1024,128]{0,1:T(8,128)} async-done(((f32[1024,128]{0,1:T(8,128)}), f32[1024,128]{0,1:T(8,128)}) %all-reduce.2.cloned.1.call-update) | async-done | bytes 524304 | tf_op jit(solution)/shard_map/psum | solution.py:266
  1960.1 2.0 copy.58
  (31 shorter events, 0.1 us)
Async XLA Ops:
  7.2 886.0 %copy-start = (bf16[3,2048,128]{2,1,0:T(8,128)(2,1)S(1)}, bf16[3,2048,128]{2,1,0:T(8,128)(2,1)}, u32[]{:S(2)}) copy-start(bf16[3,2048,128]{2,1,0:T(8,128)(2,1)} %param.15) | copy-start | bytes 4718596
  7.2 221.5 %all-gather.9.cloned.1.call-start = ((), (), s32[]{:S(2)}) async-start(), calls=%async_computation.1 | async-start | bytes 4227072 | tf_op jit(solution)/shard_map/all_gather | solution.py:135
  7.9 436.9 %all-gather.11.cloned.1.call-start = ((), (), s32[]{:S(2)}) async-start(), calls=%async_computation.2 | async-start | bytes 4227072 | tf_op jit(solution)/shard_map/all_gather | solution.py:136
  8.7 750.3 %all-gather.13.cloned.1.call-start = ((), (), s32[]{:S(2)}) async-start(), calls=%async_computation.3 | async-start | bytes 4227072 | tf_op jit(solution)/shard_map/all_gather | solution.py:178
  9.4 867.7 %all-gather.15.cloned.1.call-start = ((), (), s32[]{:S(2)}) async-start(), calls=%async_computation.4 | async-start | bytes 4227072 | tf_op jit(solution)/shard_map/all_gather | solution.py:181
  10.0 919.3 %reduce-scatter.2.cloned.1.call-start = ((), (), s32[]{:S(2)}) async-start(), calls=%async_computation.5 | async-start | bytes 1572864 | tf_op jit(solution)/shard_map/reduce_scatter | solution.py:196
  11.0 433.9 %copy-start.8 = (bf16[128,128]{1,0:T(8,128)(2,1)S(1)}, bf16[128,128]{1,0:T(8,128)(2,1)}, u32[]{:S(2)}) copy-start(bf16[128,128]{1,0:T(8,128)(2,1)} %param.14) | copy-start | bytes 98308
  444.8 314.2 %copy-start.7 = (bf16[128,128]{1,0:T(8,128)(2,1)S(1)}, bf16[128,128]{1,0:T(8,128)(2,1)}, u32[]{:S(2)}) copy-start(bf16[128,128]{1,0:T(8,128)(2,1)} %param.12) | copy-start | bytes 98308
  759.0 14.5 copy-start.1
  759.0 14.5 copy-start.2
  779.9 103.1 %copy-start.6 = (bf16[128,128]{1,0:T(8,128)(2,1)S(1)}, bf16[128,128]{1,0:T(8,128)(2,1)}, u32[]{:S(2)}) copy-start(bf16[128,128]{1,0:T(8,128)(2,1)} %param.13) | copy-start | bytes 98308
  882.9 12.0 copy-start.3
  893.2 17.3 copy-start.9
  893.2 17.4 copy-start.4
  894.9 1065.3 %all-reduce.2.cloned.1.call-start = ((), (), s32[]{:S(2)}) async-start(), calls=%async_computation.6 | async-start | bytes 1048576 | tf_op jit(solution)/shard_map/psum | solution.py:266
  895.2 16.6 collective-permute-start.4
  897.1 15.5 collective-permute-start.5
  899.1 14.0 collective-permute-start.6
  907.2 8.7 collective-permute-start.7
  930.6 34.6 %collective-permute-start = (bf16[2,64,1024]{2,0,1:T(2,128)(2,1)S(1)}, bf16[2,64,1024]{2,0,1:T(2,128)(2,1)}, u32[]{:S(2)}, u32[]{:S(2)}) collective-permute-start(bf16[2,64,1024]{2,0,1:T(2,128)(2,1)S(1)} %copy.63), channel_id=1, source_target_pairs={{0,2},{2,4},{4,6},{6,8},{8,10},{10,12},{12,14},{14,16},{16,18},{18... | collective-permute-start | bytes 786440 | tf_op jit(solution)/shard_map/ppermute | solution.py:15
  932.5 32.7 %collective-permute-start.1 = (bf16[2,64,1024]{2,0,1:T(2,128)(2,1)S(1)}, bf16[2,64,1024]{2,0,1:T(2,128)(2,1)}, u32[]{:S(2)}, u32[]{:S(2)}) collective-permute-start(bf16[2,64,1024]{2,0,1:T(2,128)(2,1)S(1)} %copy.63), channel_id=1, source_target_pairs={{0,4},{2,6},{4,8},{6,10},{8,12},{10,14},{12,16},{14,18},{16,20},{1... | collective-permute-start | bytes 786440 | tf_op jit(solution)/shard_map/ppermute | solution.py:15
  934.8 30.5 %collective-permute-start.2 = (bf16[2,64,1024]{2,0,1:T(2,128)(2,1)S(1)}, bf16[2,64,1024]{2,0,1:T(2,128)(2,1)}, u32[]{:S(2)}, u32[]{:S(2)}) collective-permute-start(bf16[2,64,1024]{2,0,1:T(2,128)(2,1)S(1)} %copy.63), channel_id=1, source_target_pairs={{4,0},{6,2},{8,4},{10,6},{12,8},{14,10},{16,12},{18,14},{20,16},{2... | collective-permute-start | bytes 786440 | tf_op jit(solution)/shard_map/ppermute | solution.py:15
  943.0 22.2 %collective-permute-start.3 = (bf16[2,64,1024]{2,0,1:T(2,128)(2,1)S(1)}, bf16[2,64,1024]{2,0,1:T(2,128)(2,1)}, u32[]{:S(2)}, u32[]{:S(2)}) collective-permute-start(bf16[2,64,1024]{2,0,1:T(2,128)(2,1)S(1)} %copy.63), channel_id=1, source_target_pairs={{2,0},{4,2},{6,4},{8,6},{10,8},{12,10},{14,12},{16,14},{18,16},{20... | collective-permute-start | bytes 786440 | tf_op jit(solution)/shard_map/ppermute | solution.py:15
  965.2 13.0 copy-start.5
Sparse Core Ops, SparseCore 0:
  9.9 218.7 all-gather.8
  230.5 214.2 all-gather.10
  446.7 214.4 all-gather.12
  662.9 214.0 all-gather.14
  895.0 23.7 reduce-scatter.1
  965.3 994.7 all-reduce.1
where the time goes:
time: 1970 us
  waiting for transfers between devices  1510 us (77%)
  blocking collectives  303 us (15%)
  matrix products  79 us (4%)
  local copies, waits for them, and re-layouts  31.3 us (2%)
  starting transfers between devices  30.9 us (2%)
    psum x1, waiting for transfers between devices, local(): filter_grad = lax.psum(filter_part, 'ctx')  976 us
    all_gather x1, waiting for transfers between devices, fold_keys(): lax.all_gather(key_rows, 'ctx', axis=0, tiled=True)  218 us
    all_gather x1, waiting for transfers between devices, fold_keys(): lax.all_gather(value_rows, 'ctx', axis=0, tiled=True)  209 us
    all_gather x1, blocking collectives, local(): lax.all_gather(lse_rows.T, 'ctx', axis=0, tiled=True)  153 us
    all_gather x1, blocking collectives, local(): lax.all_gather(delta_rows.T, 'ctx', axis=0, tiled=True)  150 us
    all_gather x1, waiting for transfers between devices, local(): lax.all_gather(out_grad.astype(jnp.float32), 'ctx', axis=0, tiled=True)  97.2 us
  transfers between devices with their start and end apart: 14, of which 7 were waited for; matrix products, arithmetic and copies ran while one was open for 5% of the time, Pallas kernels for 0%

commit v1 on v0

v1 whole, which is shorter than its diff:
```python
import functools

import jax
import jax.numpy as jnp
from jax import lax
from jax.experimental import pallas as pl
from jax.experimental.pallas import tpu as pltpu
from jax.sharding import Mesh
from jax.sharding import PartitionSpec as P

HD = 128
TAPS = 128
BLK = 64
XL, Y, Z, CORE, HEAD = 2, 4, 8, 2, 2
QSETS = XL * Y
KSETS = Z * CORE
ROWS = 2 * BLK
NQ = KSETS * ROWS
NK = QSETS * ROWS
CTX = ("xl", "y", "z", "core")
LOWEST = -1e30
LOG2E = 1.4426950408889634
SCALE = HD**-0.5
QB = 256
BF = jnp.bfloat16
F32 = jnp.float32
LANES = 128


def nt(a, b):
    return lax.dot_general(a, b, (((1,), (1,)), ((), ())), preferred_element_type=F32)


def tn(a, b):
    return lax.dot_general(a, b, (((0,), (0,)), ((), ())), preferred_element_type=F32)


def nn(a, b):
    return lax.dot_general(a, b, (((1,), (0,)), ((), ())), preferred_element_type=F32)


def scores_t(q, k, kpos, qpos):
    s = nt(k, q) * (SCALE * LOG2E)
    return jnp.where(kpos <= qpos, s, LOWEST)


def stats_kernel(core_ref, q_ref, g_ref, k_ref, v_ref, kpos_ref, qpos_ref, lse_ref, delta_ref):
    s = scores_t(q_ref[...], k_ref[...], kpos_ref[...], qpos_ref[...])
    dp = nt(v_ref[...], g_ref[...])
    top = jnp.max(s, axis=0, keepdims=True)
    w = jnp.exp2(s - top)
    norm = jnp.sum(w, axis=0, keepdims=True)
    cross = jnp.sum(w * dp, axis=0, keepdims=True)
    lse_ref[...] = top + jnp.log2(norm)
    delta_ref[...] = cross / norm


def grads_kernel(
    core_ref, q_ref, g_ref, k_ref, v_ref, kpos_ref, qpos_ref, lse_ref, delta_ref, dq_ref, dkv_ref, dk_acc, dv_acc
):
    step = pl.program_id(0)

    @pl.when(step == 0)
    def _():
        dk_acc[...] = jnp.zeros_like(dk_acc)
        dv_acc[...] = jnp.zeros_like(dv_acc)

    parts = lse_ref[:, 0, :]
    top = jnp.max(parts, axis=0, keepdims=True)
    lse = top + jnp.log2(jnp.sum(jnp.exp2(parts - top), axis=0, keepdims=True))
    delta = jnp.sum(jnp.exp2(parts - lse) * delta_ref[:, 0, :], axis=0, keepdims=True)
    q = q_ref[...]
    g = g_ref[...]
    s = scores_t(q, k_ref[...], kpos_ref[...], qpos_ref[...])
    p = jnp.exp2(s - lse)
    dp = nt(v_ref[...], g)
    ds = (p * (dp - delta)).astype(BF)
    dv_acc[...] += nn(p.astype(BF), g)
    dk_acc[...] += nn(ds, q)
    dq_ref[...] = (SCALE * tn(ds, k_ref[...])).astype(dq_ref.dtype)

    @pl.when(step == pl.num_programs(0) - 1)
    def _():
        dkv_ref[:, :HD] = (SCALE * dk_acc[...]).astype(dkv_ref.dtype)
        dkv_ref[:, HD:] = dv_acc[...].astype(dkv_ref.dtype)


def row_specs():
    half = NQ // 2 // QB
    rows = lambda col: pl.BlockSpec((QB, HD), lambda i, c: (i, col))
    keys = lambda col: pl.BlockSpec((NK, HD), lambda i, c: (0, col))
    ins = [
        rows(0),
        rows(1),
        keys(0),
        keys(1),
        pl.BlockSpec((NK, 1), lambda i, c: (0, 0)),
        pl.BlockSpec((1, QB), lambda i, c: (0, i)),
    ]
    place = lambda i, c: jnp.where(c[0] == 0, i, lax.rem(i + half, 2 * half))
    return ins, place


def attention_stats(core, qg, kv, kpos, qpos):
    ins, place = row_specs()
    stat = pl.BlockSpec((1, QB), lambda i, c: (0, place(i, c)))
    return pl.pallas_call(
        stats_kernel,
        grid_spec=pltpu.PrefetchScalarGridSpec(
            num_scalar_prefetch=1, grid=(NQ // QB,), in_specs=ins, out_specs=[stat, stat]
        ),
        out_shape=[jax.ShapeDtypeStruct((1, NQ), F32)] * 2,
        compiler_params=pltpu.CompilerParams(vmem_limit_bytes=40 << 20),
        name="attention_stats",
    )(core, qg, qg, kv, kv, kpos, qpos)


def attention_grads(core, qg, kv, kpos, qpos, lse_parts, delta_parts):
    ins, place = row_specs()
    stat = pl.BlockSpec((KSETS, 1, QB), lambda i, c: (0, 0, place(i, c)))
    return pl.pallas_call(
        grads_kernel,
        grid_spec=pltpu.PrefetchScalarGridSpec(
            num_scalar_prefetch=1,
            grid=(NQ // QB,),
            in_specs=ins + [stat, stat],
            out_specs=[
                pl.BlockSpec((QB, HD), lambda i, c: (i, 0)),
                pl.BlockSpec((NK, 2 * HD), lambda i, c: (0, 0)),
            ],
            scratch_shapes=[pltpu.VMEM((NK, HD), F32), pltpu.VMEM((NK, HD), F32)],
        ),
        out_shape=[jax.ShapeDtypeStruct((NQ, HD), BF), jax.ShapeDtypeStruct((NK, 2 * HD), BF)],
        compiler_params=pltpu.CompilerParams(vmem_limit_bytes=40 << 20),
        name="attention_grads",
    )(core, qg, qg, kv, kv, kpos, qpos, lse_parts, delta_parts)


def conv_kernel(n_grad, n_in, picks_ref, *refs):
    grads = refs[:n_grad]
    ins = refs[n_grad : n_grad + n_in]
    taps_ref, out_ref, filt_ref, gcand, xcand, gext, xext, lag = refs[n_grad + n_in :]

    def load(cands, stack):
        at = 0
        for ref in cands:
            for b in range(ref.shape[0] // BLK):
                stack[at] = ref[b * BLK : (b + 1) * BLK, :].astype(F32)
                at += 1
        stack[at] = jnp.zeros((BLK, LANES), F32)

    load(grads, gcand)
    load(ins, xcand)
    for slot in range(2):
        for part in range(3):
            gext[slot, part * BLK : (part + 1) * BLK, :] = gcand[picks_ref[slot * 3 + part]]
            xext[slot, part * BLK : (part + 1) * BLK, :] = xcand[picks_ref[6 + slot * 3 + part]]
    for slot in range(2):
        acc = jnp.zeros((BLK, LANES), F32)
        for j in range(TAPS):
            acc = acc + taps_ref[j : j + 1, :] * gext[slot, j : j + BLK, :]
        out_ref[slot * BLK : (slot + 1) * BLK, :] = acc.astype(BF)
    own = [gext[slot, :BLK, :] for slot in range(2)]
    for j in range(TAPS):
        total = None
        for slot in range(2):
            prod = own[slot] * xext[slot, 2 * BLK - j : 3 * BLK - j, :]
            prod = jnp.sum(prod.reshape(BLK // 8, 8, LANES), axis=0)
            total = prod if total is None else total + prod
        lag[j] = total
    filt_ref[0] = jnp.sum(lag[...], axis=1).T


def conv_grads(core, picks, grads, ins, taps):
    channels = taps.shape[1]
    tiles = channels // LANES
    half = tiles // 2
    column = lambda a: pl.BlockSpec((a.shape[0], LANES), lambda i, p: (0, i))
    which = lambda i, p: (jnp.where(i // half == p[12], 0, 1), lax.rem(i, half), 0)
    blocks = lambda arrays: sum(a.shape[0] // BLK for a in arrays) + 1
    return pl.pallas_call(
        functools.partial(conv_kernel, len(grads), len(ins)),
        grid_spec=pltpu.PrefetchScalarGridSpec(
            num_scalar_prefetch=1,
            grid=(tiles,),
            in_specs=[column(a) for a in grads] + [column(a) for a in ins] + [column(taps)],
            out_specs=[
                pl.BlockSpec((ROWS, LANES), lambda i, p: (0, i)),
                pl.BlockSpec((1, LANES, TAPS), which),
            ],
            scratch_shapes=[
                pltpu.VMEM((blocks(grads), BLK, LANES), F32),
                pltpu.VMEM((blocks(ins), BLK, LANES), F32),
                pltpu.VMEM((2, 3 * BLK, LANES), F32),
                pltpu.VMEM((2, 3 * BLK, LANES), F32),
                pltpu.VMEM((TAPS, 8, LANES), F32),
            ],
        ),
        out_shape=[
            jax.ShapeDtypeStruct((ROWS, channels), BF),
            jax.ShapeDtypeStruct((2, channels // 2, TAPS), F32),
        ],
        compiler_params=pltpu.CompilerParams(vmem_limit_bytes=40 << 20),
        name="conv_grads",
    )(jnp.concatenate((picks, core)), *grads, *ins, taps)


def to_all(x, axes, count):
    return lax.all_to_all(jnp.broadcast_to(x[None], (count,) + x.shape), axes, 0, 0, tiled=True)


def swap(x, axis):
    return lax.ppermute(x, axis, [(0, 1), (1, 0)])


def from_ctx(x, distance):
    n = XL * Y * Z * CORE
    return lax.ppermute(x, CTX, [(i + distance, i) for i in range(n) if 0 <= i + distance < n])


def local(block_order, conv_input, conv_filter, query_rows, key_rows, value_rows, out_grad, qkv_weight):
    core = lax.axis_index("core")
    core_arr = core.reshape(1).astype(jnp.int32)
    head = lax.axis_index("head")
    qset = lax.axis_index("xl") * Y + lax.axis_index("y")
    zi = lax.axis_index("z")
    device = (qset * Z + zi) * CORE + core
    channels = conv_input.shape[1]

    order = block_order.reshape(QSETS, Z, CORE, 2)
    mine = lax.dynamic_index_in_dim(order, qset, 0, keepdims=False)
    q_ids = jnp.stack(
        (
            lax.dynamic_index_in_dim(mine, core, 1, keepdims=False),
            lax.dynamic_index_in_dim(mine, 1 - core, 1, keepdims=False),
        )
    ).reshape(-1)
    k_ids = lax.dynamic_slice(order, (0, zi, core, 0), (QSETS, 1, 1, 2)).reshape(-1)
    offsets = jnp.arange(BLK, dtype=jnp.int32)
    qpos = (q_ids[:, None] * BLK + offsets[None, :]).reshape(1, NQ)
    kpos = (k_ids[:, None] * BLK + offsets[None, :]).reshape(NK, 1)

    kv = to_all(jnp.concatenate((key_rows, value_rows), axis=1), ("xl", "y"), QSETS).reshape(NK, 2 * HD)
    qg_own = to_all(jnp.concatenate((query_rows, out_grad), axis=1), "z", Z).reshape(NQ // 2, 2 * HD)
    qg = jnp.concatenate((qg_own, swap(qg_own, "core")), axis=0)

    lse, delta = attention_stats(core_arr, qg, kv, kpos, qpos)
    stats = to_all(jnp.concatenate((lse, delta), axis=0), ("z", "core"), KSETS)
    stats = stats.reshape(KSETS, 2, NQ)
    dq, dkv = attention_grads(core_arr, qg, kv, kpos, qpos, stats[:, :1], stats[:, 1:])

    dq_half = dq[: NQ // 2].astype(F32) + swap(dq[NQ // 2 :], "core").astype(F32)
    dq_parts = lax.all_to_all(dq_half.astype(BF).reshape(Z, ROWS, HD), "z", 0, 0, tiled=True)
    dkv_parts = lax.all_to_all(dkv.reshape(QSETS, ROWS, 2 * HD), ("xl", "y"), 0, 0, tiled=True)
    query_grad = jnp.sum(dq_parts.astype(F32), axis=0).astype(BF)
    kv_grad = jnp.sum(dkv_parts.astype(F32), axis=0).astype(BF)
    grads = jnp.concatenate((query_grad, kv_grad), axis=1)

    w_own = lax.dynamic_slice_in_dim(qkv_weight, head * channels, channels, 1)
    w_other = swap(lax.dynamic_slice_in_dim(qkv_weight, (1 - head) * channels, channels, 1), "head")
    grads_other = swap(grads, "head")
    conv_grad = jnp.zeros((ROWS, channels), F32)
    for which in range(3):
        cols = slice(which * HD, (which + 1) * HD)
        conv_grad = conv_grad + nt(grads[:, cols], w_own[which]) + nt(grads_other[:, cols], w_other[which])
    conv_grad = conv_grad.astype(BF)

    ids = lax.dynamic_slice_in_dim(block_order, device * 2, 2, 0)
    swapped = ids[0] > ids[1]
    blocks_of = lambda a: (a[:BLK], a[BLK:])

    def low_high(a):
        first, second = blocks_of(a)
        return jnp.where(swapped, second, first), jnp.where(swapped, first, second)

    g_low, g_high = low_high(conv_grad)
    x_low, x_high = low_high(conv_input)
    grad_list = [
        conv_grad,
        from_ctx(g_low, 1),
        from_ctx(g_high, 1),
        from_ctx(g_low, 2),
        from_ctx(g_high, -1),
        from_ctx(g_high, -2),
    ]
    in_list = [
        conv_input,
        from_ctx(x_low, -1),
        from_ctx(x_high, -1),
        from_ctx(x_low, -2),
        from_ctx(x_low, 1),
        from_ctx(x_high, 1),
        from_ctx(x_high, 2),
    ]
    padded = jnp.concatenate((jnp.full((4,), -1000, jnp.int32), block_order, jnp.full((4,), -1000, jnp.int32)))
    near = lax.dynamic_slice_in_dim(padded, device * 2, 10, 0).reshape(5, 2)
    low, high = jnp.min(near, axis=1), jnp.max(near, axis=1)
    grad_ids = jnp.stack((ids[0], ids[1], low[3], high[3], low[4], high[1], high[0]))
    in_ids = jnp.stack((ids[0], ids[1], low[1], high[1], low[0], low[3], high[3], high[4]))

    def pick(wanted, have):
        hit = wanted[:, None] == have[None, :]
        return jnp.where(jnp.any(hit, axis=1), jnp.argmax(hit, axis=1), have.shape[0]).astype(jnp.int32)

    steps = jnp.arange(3, dtype=jnp.int32)
    later = (ids[:, None] + steps[None, :]).reshape(-1)
    earlier = (ids[:, None] + steps[None, :] - 2).reshape(-1)
    picks = jnp.concatenate((pick(later, grad_ids), pick(earlier, in_ids)))
    input_grad, filter_part = conv_grads(core_arr, picks, grad_list, in_list, conv_filter.T)

    mine_sum = filter_part[0] + swap(filter_part[1], "core")
    chips = XL * Y * Z
    parts = lax.all_to_all(
        mine_sum.astype(BF).reshape(chips, channels // 2 // chips, TAPS), ("xl", "y", "z"), 0, 0, tiled=True
    )
    total = jnp.sum(parts.astype(F32), axis=0)
    half = to_all(total, ("xl", "y", "z"), chips).reshape(channels // 2, TAPS)
    other = swap(half, "core")
    filter_grad = jnp.concatenate(
        (jnp.where(core == 0, half, other), jnp.where(core == 0, other, half)), axis=0
    )
    return input_grad, filter_grad


def solution(mesh):
    fine = Mesh(mesh.devices.reshape(XL, Y, Z, CORE, HEAD), CTX + ("head",))
    rows = P(CTX, "head")
    return jax.shard_map(
        local,
        mesh=fine,
        in_specs=(P(), rows, P("head", None), rows, rows, rows, rows, P(None, None, "head")),
        out_specs=(rows, P("head", None)),
        check_vma=False,
    )
```

time: 1970 us -> 212 us (0.11)
  waiting for transfers between devices: 1510 us -> 45.6 us
  blocking collectives: 303 us -> 32.3 us
  matrix products: 79 us -> 4.28 us
  starting transfers between devices: 30.9 us -> 63.5 us
  Pallas kernels: 0 us -> 27.5 us
    psum x1 -> x0, waiting for transfers between devices: 976 us -> none  [local(): filter_grad = lax.psum(filter_part, 'ctx')]
    all_gather x4 -> x0, waiting for transfers between devices: 524 us -> none  [the longest x1 218 us: fold_keys(): lax.all_gather(key_rows, 'ctx', axis=0, tiled=True)]
    all_gather x2 -> x0, blocking collectives: 303 us -> none  [the longest x1 153 us: local(): lax.all_gather(lse_rows.T, 'ctx', axis=0, tiled=True)]
    dot_general x9 -> x6, matrix products: 60.8 us -> 4.28 us  [nt(): lax.dot_general(a, b, (((1,), (1,)), ((), ())), preferred_element_type=F32)]
    all_to_all x0 -> x5, waiting for transfers between devices: none -> 33.4 us  [the longest x3 15.5 us: to_all(): lax.all_to_all(jnp.broadcast_to(x[None], (count,) + x.shape), axes, 0, 0,...]
    all_to_all x0 -> x2, blocking collectives: none -> 32.3 us  [the longest x1 17.4 us: to_all(): lax.all_to_all(jnp.broadcast_to(x[None], (count,) + x.shape), axes, 0, 0,...]
    pallas_call x0 -> x3, Pallas kernels: none -> 27.5 us  [the longest x1 13.7 us: conv_grads(): pl.pallas_call(functools.partial(conv_kernel, len(grads), len(ins)), grid...]
    all_to_all x0 -> x5, starting transfers between devices: none -> 21.7 us  [the longest x3 13.2 us: to_all(): lax.all_to_all(jnp.broadcast_to(x[None], (count,) + x.shape), axes, 0, 0,...]
  transfers between devices with their start and end apart: 14 -> 22, of which waited for: 7 -> 10; matrix products, arithmetic and copies ran while one was open for 5% -> 15% of each run, Pallas kernels for 0% -> 7%
where the time goes in v1:
time: 212 us; the launch traced here: 209 us
  starting transfers between devices  63.5 us (30%)
  waiting for transfers between devices  45.6 us (22%)
  blocking collectives  32.3 us (15%)
  Pallas kernels  27.5 us (13%)
  local copies, waits for them, and re-layouts  21.3 us (10%)
  other arithmetic  12.5 us (6%)
  matrix products  4.28 us (2%)
  between operations  2.44 us (1%)
    ppermute x11, starting transfers between devices, from_ctx(): lax.ppermute(x, CTX, [(i + distance, i) for i in range(n) if 0 <= i + dis...  37.5 us
    all_to_all x1, blocking collectives, to_all(): lax.all_to_all(jnp.broadcast_to(x[None], (count,) + x.shape), axes, 0, 0,...  17.4 us
    all_to_all x3, waiting for transfers between devices, to_all(): lax.all_to_all(jnp.broadcast_to(x[None], (count,) + x.shape), axes, 0, 0,...  15.5 us
    all_to_all x1, blocking collectives, local(): lax.all_to_all(mine_sum.astype(BF).reshape(chips, channels // 2 // chips,...  14.9 us
    pallas_call x1, Pallas kernels, conv_grads(): pl.pallas_call(functools.partial(conv_kernel, len(grads), len(ins)), grid...  13.7 us
    all_to_all x3, starting transfers between devices, to_all(): lax.all_to_all(jnp.broadcast_to(x[None], (count,) + x.shape), axes, 0, 0,...  13.2 us
    all_to_all x1, waiting for transfers between devices, local(): lax.all_to_all(dq_half.astype(BF).reshape(Z, ROWS, HD), 'z', 0, 0, tiled=...  11.6 us
    pallas_call x1, Pallas kernels, attention_grads(): pl.pallas_call(grads_kernel, grid_spec=pltpu.PrefetchScalarGridSpec(num_s...  7.99 us
  transfers between devices with their start and end apart: 22, of which 10 were waited for; matrix products, arithmetic and copies ran while one was open for 15% of the time, Pallas kernels for 7%

profile of v1, /device:TPU:6, one launch (start us, length us, event | category | flops | bytes accessed | tf_op | source)
XLA Modules:
  0.0 209.4 jit_solution(9558247810862515758)
XLA Ops:
  0.7 0.9 dynamic_slice.24
  1.5 0.6 fusion.16
  3.4 1.7 broadcast_select_fusion.2
  5.1 3.8 %collective-permute-start.11 = (bf16[64,1024]{1,0:T(8,128)(2,1)}, bf16[64,1024]{1,0:T(8,128)(2,1)S(1)}, u32[]{:S(2)}, u32[]{:S(2)}) collective-permute-start(bf16[64,1024]{1,0:T(8,128)(2,1)} %get-tuple-element.23), channel_id=1, source_target_pairs={{0,4},{2,6},{4,8},{6,10},{8,12},{10,14},{12,16},{14,18},{16,20},{1... | collective-permute-start | bytes 393224 | tf_op jit(solution)/shard_map/ppermute | solution.py:218
  8.9 8.0 %collective-permute-start.12 = (bf16[64,1024]{1,0:T(8,128)(2,1)}, bf16[64,1024]{1,0:T(8,128)(2,1)S(1)}, u32[]{:S(2)}, u32[]{:S(2)}) collective-permute-start(bf16[64,1024]{1,0:T(8,128)(2,1)} %get-tuple-element.23), channel_id=1, source_target_pairs={{2,0},{4,2},{6,4},{8,6},{10,8},{12,10},{14,12},{16,14},{18,16},{20... | collective-permute-start | bytes 393224 | tf_op jit(solution)/shard_map/ppermute | solution.py:218
  16.9 0.8 pad_maximum_fusion.3
  17.7 0.8 broadcast_in_dim.16
  18.6 3.6 %all-to-all-start = ((bf16[8,128,256]{2,1,0:T(8,128)(2,1)}), bf16[8,128,256]{2,1,0:T(8,128)(2,1)S(1)}, u32[]{:S(2)}, u32[]{:S(2)}) async-start(bf16[8,128,256]{2,1,0:T(8,128)(2,1)} %broadcast_in_dim.16), calls=%async_computation | async-start | bytes 1048576 | tf_op jit(solution)/shard_map/all_to_all | solution.py:209
  22.2 1.0 constant_dynamic-slice_fusion
  23.2 1.1 collective-permute-start.3
  24.3 1.9 collective-permute-start.10
  27.1 1.3 add.177.kpos_ref
  28.4 11.3 %all-to-all-done = bf16[8,128,256]{2,1,0:T(8,128)(2,1)S(1)} async-done(((bf16[8,128,256]{2,1,0:T(8,128)(2,1)}), bf16[8,128,256]{2,1,0:T(8,128)(2,1)S(1)}, u32[]{:S(2)}, u32[]{:S(2)}) %all-to-all-start) | async-done | bytes 524320 | tf_op jit(solution)/shard_map/all_to_all | solution.py:209
  39.7 0.9 broadcast_in_dim.17
  40.6 5.3 %all-to-all-start.1 = ((bf16[8,128,256]{2,1,0:T(8,128)(2,1)}), bf16[8,128,256]{2,1,0:T(8,128)(2,1)S(1)}, u32[]{:S(2)}, u32[]{:S(2)}) async-start(bf16[8,128,256]{2,1,0:T(8,128)(2,1)} %broadcast_in_dim.17), calls=%async_computation.1 | async-start | bytes 1048576 | tf_op jit(solution)/shard_map/all_to_all | solution.py:209
  46.3 0.6 add.154
  47.0 0.7 fusion.17
  47.7 3.6 %stack.17 = s32[7]{0:T(128)} concatenate(s32[2]{0:T(128)S(1)} %dynamic_slice.24, s32[1]{0:T(128)} %get-tuple-element.39, s32[1]{0:T(128)} %get-tuple-element.34, s32[1]{0:T(128)} %get-tuple-element.42, s32[1]{0:T(128)} %get-tuple-element.33, s32[1]{0:T(128)} %get-tuple-element.32), dimensions={0} | concatenate | bytes 56 | tf_op jit(solution)/shard_map/stack | solution.py:298
  51.3 1.3 pad_maximum_fusion.q_ref.g_ref
  52.6 0.6 all-to-all-done.1
  53.2 1.0 copy-done.1
  54.2 5.8 %attention_stats.1 = (f32[1,2048]{1,0:T(1,128)S(1)}, f32[1,2048]{1,0:T(1,128)S(1)}) custom-call(s32[1]{0:T(128)} %bitcast.core_ref, bf16[2048,256]{1,0:T(8,128)(2,1)S(1)} %pad_maximum_fusion.q_ref.g_ref, bf16[2048,256]{1,0:T(8,128)(2,1)S(1)} %pad_maximum_fusion.q_ref.g_ref, bf16[1024,256]{1,0:T(8,128)(2,1)S(1)} %bitcast.41, bf16[1024,256]{1,0:T(8,128)(2,1)S(1)} %bitcast.42, ...), custom_call_target="tpu_custom_call" | custom-call | tf_op jit(solution)/shard_map/attention_stats/pallas_call | solution.py:107
  60.1 0.8 broadcast_in_dim.18
  60.9 4.2 %all-to-all-start.2 = ((f32[16,2,2048]{2,1,0:T(2,128)}), f32[16,2,2048]{2,1,0:T(2,128)}, u32[]{:S(2)}, u32[]{:S(2)}) async-start(f32[16,2,2048]{2,1,0:T(2,128)} %broadcast_in_dim.18), calls=%async_computation.2 | async-start | bytes 524288 | tf_op jit(solution)/shard_map/all_to_all | solution.py:209
  65.1 1.4 compare_reduce_fusion.3
  66.5 0.6 slice.110
  67.0 3.1 %stack.18 = s32[8]{0:T(128)S(1)} concatenate(s32[2]{0:T(128)S(1)} %dynamic_slice.24, s32[1]{0:T(128)} %get-tuple-element.40, s32[1]{0:T(128)} %get-tuple-element.33, s32[1]{0:T(128)} %get-tuple-element.41, s32[1]{0:T(128)} %get-tuple-element.39, s32[2]{0:T(128)} %slice.110), dimensions={0} | concatenate | bytes 64 | tf_op jit(solution)/shard_map/stack | solution.py:299
  70.2 1.1 broadcast_add_fusion
  71.3 1.3 compare_reduce_fusion.2
  72.6 3.5 %all-to-all-done.2 = f32[16,2,2048]{2,1,0:T(2,128)} async-done(((f32[16,2,2048]{2,1,0:T(2,128)}), f32[16,2,2048]{2,1,0:T(2,128)}, u32[]{:S(2)}, u32[]{:S(2)}) %all-to-all-start.2) | async-done | bytes 262176 | tf_op jit(solution)/shard_map/all_to_all | solution.py:209
  76.2 1.3 fusion.15
  77.5 1.0 copy-done.2
  78.5 8.0 %attention_grads.1 = (bf16[2048,128]{1,0:T(8,128)(2,1)S(1)}, bf16[1024,256]{1,0:T(8,128)(2,1)S(1)}) custom-call(s32[1]{0:T(128)} %bitcast.core_ref, bf16[2048,256]{1,0:T(8,128)(2,1)S(1)} %pad_maximum_fusion.q_ref.g_ref, bf16[2048,256]{1,0:T(8,128)(2,1)S(1)} %pad_maximum_fusion.q_ref.g_ref, bf16[1024,256]{1,0:T(8,128)(2,1)S(1)} %bitcast.43, ...), custom_call_target="tpu_custom_call" | custom-call | tf_op jit(solution)/shard_map/attention_grads/pallas_call | solution.py:121
  86.5 0.7 copy-done.4
  87.5 1.2 collective-permute-start.1
  88.8 5.1 %all-to-all-start.4 = ((bf16[8,128,256]{2,1,0:T(8,128)(2,1)}), bf16[8,128,256]{2,1,0:T(8,128)(2,1)S(1)}, u32[]{:S(2)}, u32[]{:S(2)}) async-start(bf16[8,128,256]{2,1,0:T(8,128)(2,1)} %bitcast.46), calls=%async_computation.4 | async-start | bytes 1048576 | tf_op jit(solution)/shard_map/all_to_all | solution.py:254
  93.9 0.7 compare_reduce_fusion
  94.6 1.7 add_convert_fusion
  96.3 6.4 %all-to-all-done.4 = bf16[8,128,256]{2,1,0:T(8,128)(2,1)S(1)} async-done(((bf16[8,128,256]{2,1,0:T(8,128)(2,1)}), bf16[8,128,256]{2,1,0:T(8,128)(2,1)S(1)}, u32[]{:S(2)}, u32[]{:S(2)}) %all-to-all-start.4) | async-done | bytes 524320 | tf_op jit(solution)/shard_map/all_to_all | solution.py:254
  102.7 3.4 %all-to-all-start.3 = ((bf16[8,128,128]{2,1,0:T(8,128)(2,1)}), bf16[8,128,128]{2,1,0:T(8,128)(2,1)S(1)}, u32[]{:S(2)}, u32[]{:S(2)}) async-start(bf16[8,128,128]{2,1,0:T(8,128)(2,1)} %bitcast.5), calls=%async_computation.3 | async-start | bytes 524288 | tf_op jit(solution)/shard_map/all_to_all | solution.py:253
  106.5 11.6 %all-to-all-done.3 = bf16[8,128,128]{2,1,0:T(8,128)(2,1)S(1)} async-done(((bf16[8,128,128]{2,1,0:T(8,128)(2,1)}), bf16[8,128,128]{2,1,0:T(8,128)(2,1)S(1)}, u32[]{:S(2)}, u32[]{:S(2)}) %all-to-all-start.3) | async-done | bytes 262176 | tf_op jit(solution)/shard_map/all_to_all | solution.py:253
  118.1 1.5 collective-permute-start.2
  119.8 1.9 collective-permute-start.13
  121.7 2.6 %collective-permute-done.2 = bf16[128,384]{1,0:T(8,128)(2,1)S(1)} collective-permute-done((bf16[128,384]{1,0:T(8,128)(2,1)S(1)}, bf16[128,384]{1,0:T(8,128)(2,1)S(1)}, u32[]{:S(2)}, u32[]{:S(2)}) %collective-permute-start.2) | collective-permute-done | bytes 98336 | tf_op jit(solution)/shard_map/ppermute | solution.py:213
  124.3 1.9 collective-permute-start.14
  126.2 1.2 convolution_add_fusion.3
  127.7 1.2 fusion
  128.9 1.2 fusion.1.refs_0_
  130.1 1.9 collective-permute-start.9
  132.0 0.7 broadcast_select_fusion.4
  132.8 7.8 %collective-permute-start.4 = (bf16[64,1024]{1,0:T(8,128)(2,1)}, bf16[64,1024]{1,0:T(8,128)(2,1)S(1)}, u32[]{:S(2)}, u32[]{:S(2)}) collective-permute-start(bf16[64,1024]{1,0:T(8,128)(2,1)} %get-tuple-element.25), channel_id=1, source_target_pairs={{2,0},{4,2},{6,4},{8,6},{10,8},{12,10},{14,12},{16,14},{18,16},{20... | collective-permute-start | bytes 393224 | tf_op jit(solution)/shard_map/ppermute | solution.py:218
  140.6 1.9 collective-permute-start.6
  142.6 1.9 collective-permute-start.5
  144.5 2.4 %collective-permute-start.7 = (bf16[64,1024]{1,0:T(8,128)(2,1)}, bf16[64,1024]{1,0:T(8,128)(2,1)}, u32[]{:S(2)}, u32[]{:S(2)}) collective-permute-start(bf16[64,1024]{1,0:T(8,128)(2,1)} %get-tuple-element.24), channel_id=1, source_target_pairs={{0,2},{2,4},{4,6},{6,8},{8,10},{10,12},{12,14},{14,16},{16,18},{18... | collective-permute-start | bytes 393224 | tf_op jit(solution)/shard_map/ppermute | solution.py:218
  146.9 3.9 %collective-permute-start.8 = (bf16[64,1024]{1,0:T(8,128)(2,1)}, bf16[64,1024]{1,0:T(8,128)(2,1)}, u32[]{:S(2)}, u32[]{:S(2)}) collective-permute-start(bf16[64,1024]{1,0:T(8,128)(2,1)} %get-tuple-element.24), channel_id=1, source_target_pairs={{0,4},{2,6},{4,8},{6,10},{8,12},{10,14},{12,16},{14,18},{16,20},{1... | collective-permute-start | bytes 393224 | tf_op jit(solution)/shard_map/ppermute | solution.py:218
  150.9 1.2 copy.23
  152.2 3.1 %collective-permute-done.7.refs_4_ = bf16[64,1024]{1,0:T(8,128)(2,1)} collective-permute-done((bf16[64,1024]{1,0:T(8,128)(2,1)}, bf16[64,1024]{1,0:T(8,128)(2,1)}, u32[]{:S(2)}, u32[]{:S(2)}) %collective-permute-start.7) | collective-permute-done | bytes 131104 | tf_op jit(solution)/shard_map/ppermute | solution.py:218
  155.3 3.8 %collective-permute-done.8.refs_5_ = bf16[64,1024]{1,0:T(8,128)(2,1)} collective-permute-done((bf16[64,1024]{1,0:T(8,128)(2,1)}, bf16[64,1024]{1,0:T(8,128)(2,1)}, u32[]{:S(2)}, u32[]{:S(2)}) %collective-permute-start.8) | collective-permute-done | bytes 131104 | tf_op jit(solution)/shard_map/ppermute | solution.py:218
  159.1 13.7 %conv_grads.1 = (bf16[128,1024]{1,0:T(8,128)(2,1)}, f32[2,512,128]{2,1,0:T(8,128)S(1)}) custom-call(s32[13]{0:T(128)S(1)} %pad_add_fusion.1.picks_ref, bf16[128,1024]{1,0:T(8,128)(2,1)S(1)} %fusion.1.refs_0_, bf16[64,1024]{1,0:T(8,128)(2,1)S(1)} %collective-permute-done.4.refs_1_, bf16[64,1024]{1,0:T(8,128)(2,1)} %collective-permute-done.5.refs_2_, ...), custom_call_target="tpu_custom_call" | custom-call | tf_op jit(solution)/shard_map/conv_grads/pallas_call | solution.py:181
  173.4 1.2 collective-permute-done.15
  174.6 14.9 %all_to_all.35 = bf16[64,8,128]{2,1,0:T(8,128)(2,1)S(1)} all-to-all(bf16[64,8,128]{2,1,0:T(8,128)(2,1)S(1)} %fusion.5), channel_id=1, replica_groups=mesh['xl'=2,'y'=4,'z'=8,'core'=2,'head'=2] {'xl','y','z'}, dimensions={0} | all-to-all | bytes 262144 | tf_op jit(solution)/shard_map/all_to_all | solution.py:313
  189.6 17.4 %all_to_all.36 = f32[64,8,128]{2,1,0:T(8,128)S(1)} all-to-all(f32[64,8,128]{2,1,0:T(8,128)S(1)} %broadcast_in_dim.19), channel_id=1, replica_groups=mesh['xl'=2,'y'=4,'z'=8,'core'=2,'head'=2] {'xl','y','z'}, dimensions={0} | all-to-all | bytes 524288 | tf_op jit(solution)/shard_map/all_to_all | solution.py:209
  207.0 1.5 collective-permute-done.16
  208.5 0.8 pad_maximum_fusion.1
  (74 shorter events, 3.4 us)
Async XLA Ops:
  0.6 21.6 %copy-start = (bf16[3,2048,128]{2,1,0:T(8,128)(2,1)S(1)}, bf16[3,2048,128]{2,1,0:T(8,128)(2,1)}, u32[]{:S(2)}) copy-start(bf16[3,2048,128]{2,1,0:T(8,128)(2,1)} %param.15) | copy-start | bytes 4718596
  5.1 127.7 %collective-permute-start.11 = (bf16[64,1024]{1,0:T(8,128)(2,1)}, bf16[64,1024]{1,0:T(8,128)(2,1)S(1)}, u32[]{:S(2)}, u32[]{:S(2)}) collective-permute-start(bf16[64,1024]{1,0:T(8,128)(2,1)} %get-tuple-element.23), channel_id=1, source_target_pairs={{0,4},{2,6},{4,8},{6,10},{8,12},{10,14},{12,16},{14,18},{16,20},{1... | collective-permute-start | bytes 393224 | tf_op jit(solution)/shard_map/ppermute | solution.py:218
  8.9 131.7 %collective-permute-start.12 = (bf16[64,1024]{1,0:T(8,128)(2,1)}, bf16[64,1024]{1,0:T(8,128)(2,1)S(1)}, u32[]{:S(2)}, u32[]{:S(2)}) collective-permute-start(bf16[64,1024]{1,0:T(8,128)(2,1)} %get-tuple-element.23), channel_id=1, source_target_pairs={{2,0},{4,2},{6,4},{8,6},{10,8},{12,10},{14,12},{16,14},{18,16},{20... | collective-permute-start | bytes 393224 | tf_op jit(solution)/shard_map/ppermute | solution.py:218
  17.7 8.5 %copy-start.9 = (s32[256]{0:T(256)S(1)}, s32[256]{0:T(256)}, u32[]{:S(2)}) copy-start(s32[256]{0:T(256)} %param.8) | copy-start | bytes 3076
  18.6 9.8 %copy-start.7 = (bf16[128,128]{1,0:T(8,128)(2,1)S(1)}, bf16[128,128]{1,0:T(8,128)(2,1)}, u32[]{:S(2)}) copy-start(bf16[128,128]{1,0:T(8,128)(2,1)} %param.13) | copy-start | bytes 98308
  18.6 9.8 %copy-start.8 = (bf16[128,128]{1,0:T(8,128)(2,1)S(1)}, bf16[128,128]{1,0:T(8,128)(2,1)}, u32[]{:S(2)}) copy-start(bf16[128,128]{1,0:T(8,128)(2,1)} %param.12) | copy-start | bytes 98308
  18.6 21.2 %all-to-all-start = ((bf16[8,128,256]{2,1,0:T(8,128)(2,1)}), bf16[8,128,256]{2,1,0:T(8,128)(2,1)S(1)}, u32[]{:S(2)}, u32[]{:S(2)}) async-start(bf16[8,128,256]{2,1,0:T(8,128)(2,1)} %broadcast_in_dim.16), calls=%async_computation | async-start | bytes 1048576 | tf_op jit(solution)/shard_map/all_to_all | solution.py:209
  23.2 96.6 %collective-permute-start.3 = (bf16[3,1024,128]{2,1,0:T(8,128)(2,1)}, bf16[3,1024,128]{2,1,0:T(8,128)(2,1)}, u32[]{:S(2)}, u32[]{:S(2)}) collective-permute-start(bf16[3,1024,128]{2,1,0:T(8,128)(2,1)} %constant_dynamic-slice_fusion), channel_id=1, source_target_pairs={{0,1},{1,0},{2,3},{3,2},{4,5},{5,4},{6,7},{7,6},{8,9},{9,8},{10,11... | collective-permute-start | bytes 2359304 | tf_op jit(solution)/shard_map/ppermute | solution.py:213
  24.3 105.8 %collective-permute-start.10 = (bf16[64,1024]{1,0:T(8,128)(2,1)}, bf16[64,1024]{1,0:T(8,128)(2,1)S(1)}, u32[]{:S(2)}, u32[]{:S(2)}) collective-permute-start(bf16[64,1024]{1,0:T(8,128)(2,1)} %get-tuple-element.22), channel_id=1, source_target_pairs={{0,2},{2,4},{4,6},{6,8},{8,10},{10,12},{12,14},{14,16},{16,18},{18... | collective-permute-start | bytes 393224 | tf_op jit(solution)/shard_map/ppermute | solution.py:218
  39.7 11.6 %copy-start.6 = (bf16[8,128,256]{2,1,0:T(8,128)(2,1)}, bf16[8,128,256]{2,1,0:T(8,128)(2,1)S(1)}, u32[]{:S(2)}) copy-start(bf16[8,128,256]{2,1,0:T(8,128)(2,1)S(1)} %all-to-all-done) | copy-start | bytes 1572868
  40.6 12.6 %all-to-all-start.1 = ((bf16[8,128,256]{2,1,0:T(8,128)(2,1)}), bf16[8,128,256]{2,1,0:T(8,128)(2,1)S(1)}, u32[]{:S(2)}, u32[]{:S(2)}) async-start(bf16[8,128,256]{2,1,0:T(8,128)(2,1)} %broadcast_in_dim.17), calls=%async_computation.1 | async-start | bytes 1048576 | tf_op jit(solution)/shard_map/all_to_all | solution.py:209
  46.0 5.4 %collective-permute-start = (bf16[1024,256]{1,0:T(8,128)(2,1)S(1)}, bf16[1024,256]{1,0:T(8,128)(2,1)}, u32[]{:S(2)}, u32[]{:S(2)}) collective-permute-start(bf16[1024,256]{1,0:T(8,128)(2,1)S(1)} %bitcast.47), channel_id=1, source_target_pairs={{0,2},{2,0},{1,3},{3,1},{4,6},{6,4},{5,7},{7,5},{8,10},{10,8},{9,1... | collective-permute-start | bytes 1572872 | tf_op jit(solution)/shard_map/ppermute | solution.py:213
  53.2 1.0 copy-start.1
  60.9 15.2 %all-to-all-start.2 = ((f32[16,2,2048]{2,1,0:T(2,128)}), f32[16,2,2048]{2,1,0:T(2,128)}, u32[]{:S(2)}, u32[]{:S(2)}) async-start(f32[16,2,2048]{2,1,0:T(2,128)} %broadcast_in_dim.18), calls=%async_computation.2 | async-start | bytes 524288 | tf_op jit(solution)/shard_map/all_to_all | solution.py:209
  77.4 1.0 copy-start.2
  78.5 10.1 %copy-start.10 = (s32[6]{0:T(128)S(1)}, s32[6]{0:T(128)}, u32[]{:S(2)}) copy-start(s32[6]{0:T(128)} %broadcast_add_fusion) | copy-start | bytes 76
  86.5 0.8 copy-start.4
  86.5 1.0 copy-start.5
  86.5 7.4 %copy-start.11 = (s32[6]{0:T(128)S(1)}, s32[6]{0:T(128)}, u32[]{:S(2)}) copy-start(s32[6]{0:T(128)} %broadcast_add_fusion) | copy-start | bytes 76
  86.5 19.6 %copy-start.12 = (pred[6]{0:T(512)(128)(4,1)S(1)}, pred[6]{0:T(512)(128)(4,1)}, u32[]{:S(2)}) copy-start(pred[6]{0:T(512)(128)(4,1)} %compare_reduce_fusion.3) | copy-start | bytes 22
  87.5 7.2 %collective-permute-start.1 = (bf16[1024,128]{1,0:T(8,128)(2,1)S(1)}, bf16[1024,128]{1,0:T(8,128)(2,1)S(1)}, u32[]{:S(2)}, u32[]{:S(2)}) collective-permute-start(bf16[1024,128]{1,0:T(8,128)(2,1)S(1)} %slice.114), channel_id=1, source_target_pairs={{0,2},{2,0},{1,3},{3,1},{4,6},{6,4},{5,7},{7,5},{8,10},{10,8},{9,1... | collective-permute-start | bytes 786440 | tf_op jit(solution)/shard_map/ppermute | solution.py:213
  88.8 13.9 %all-to-all-start.4 = ((bf16[8,128,256]{2,1,0:T(8,128)(2,1)}), bf16[8,128,256]{2,1,0:T(8,128)(2,1)S(1)}, u32[]{:S(2)}, u32[]{:S(2)}) async-start(bf16[8,128,256]{2,1,0:T(8,128)(2,1)} %bitcast.46), calls=%async_computation.4 | async-start | bytes 1048576 | tf_op jit(solution)/shard_map/all_to_all | solution.py:254
  102.7 15.3 %all-to-all-start.3 = ((bf16[8,128,128]{2,1,0:T(8,128)(2,1)}), bf16[8,128,128]{2,1,0:T(8,128)(2,1)S(1)}, u32[]{:S(2)}, u32[]{:S(2)}) async-start(bf16[8,128,128]{2,1,0:T(8,128)(2,1)} %bitcast.5), calls=%async_computation.3 | async-start | bytes 524288 | tf_op jit(solution)/shard_map/all_to_all | solution.py:253
  118.1 6.2 %collective-permute-start.2 = (bf16[128,384]{1,0:T(8,128)(2,1)S(1)}, bf16[128,384]{1,0:T(8,128)(2,1)S(1)}, u32[]{:S(2)}, u32[]{:S(2)}) collective-permute-start(bf16[128,384]{1,0:T(8,128)(2,1)S(1)} %pad_maximum_fusion.2), channel_id=1, source_target_pairs={{0,1},{1,0},{2,3},{3,2},{4,5},{5,4},{6,7},{7,6},{8,9},{9,8},{10,11... | collective-permute-start | bytes 294920 | tf_op jit(solution)/shard_map/ppermute | solution.py:213
  119.8 22.7 %collective-permute-start.13 = (bf16[64,1024]{1,0:T(8,128)(2,1)}, bf16[64,1024]{1,0:T(8,128)(2,1)S(1)}, u32[]{:S(2)}, u32[]{:S(2)}) collective-permute-start(bf16[64,1024]{1,0:T(8,128)(2,1)} %get-tuple-element.22), channel_id=1, source_target_pairs={{2,0},{4,2},{6,4},{8,6},{10,8},{12,10},{14,12},{16,14},{18,16},{20... | collective-permute-start | bytes 393224 | tf_op jit(solution)/shard_map/ppermute | solution.py:218
  124.3 20.2 %collective-permute-start.14 = (bf16[64,1024]{1,0:T(8,128)(2,1)}, bf16[64,1024]{1,0:T(8,128)(2,1)S(1)}, u32[]{:S(2)}, u32[]{:S(2)}) collective-permute-start(bf16[64,1024]{1,0:T(8,128)(2,1)} %get-tuple-element.22), channel_id=1, source_target_pairs={{4,0},{6,2},{8,4},{10,6},{12,8},{14,10},{16,12},{18,14},{20,16},{2... | collective-permute-start | bytes 393224 | tf_op jit(solution)/shard_map/ppermute | solution.py:218
  128.9 30.3 %copy-start.3 = (bf16[128,1024]{1,0:T(8,128)(2,1)S(1)}, bf16[128,1024]{1,0:T(8,128)(2,1)}, u32[]{:S(2)}) copy-start(bf16[128,1024]{1,0:T(8,128)(2,1)} %refs_6_.1) | copy-start | bytes 786436
  130.1 16.8 %collective-permute-start.9 = (bf16[64,1024]{1,0:T(8,128)(2,1)}, bf16[64,1024]{1,0:T(8,128)(2,1)S(1)}, u32[]{:S(2)}, u32[]{:S(2)}) collective-permute-start(bf16[64,1024]{1,0:T(8,128)(2,1)} %get-tuple-element.23), channel_id=1, source_target_pairs={{0,2},{2,4},{4,6},{6,8},{8,10},{10,12},{12,14},{14,16},{16,18},{18... | collective-permute-start | bytes 393224 | tf_op jit(solution)/shard_map/ppermute | solution.py:218
  132.8 19.4 %collective-permute-start.4 = (bf16[64,1024]{1,0:T(8,128)(2,1)}, bf16[64,1024]{1,0:T(8,128)(2,1)S(1)}, u32[]{:S(2)}, u32[]{:S(2)}) collective-permute-start(bf16[64,1024]{1,0:T(8,128)(2,1)} %get-tuple-element.25), channel_id=1, source_target_pairs={{2,0},{4,2},{6,4},{8,6},{10,8},{12,10},{14,12},{16,14},{18,16},{20... | collective-permute-start | bytes 393224 | tf_op jit(solution)/shard_map/ppermute | solution.py:218
  140.6 11.6 %collective-permute-start.6 = (bf16[64,1024]{1,0:T(8,128)(2,1)}, bf16[64,1024]{1,0:T(8,128)(2,1)}, u32[]{:S(2)}, u32[]{:S(2)}) collective-permute-start(bf16[64,1024]{1,0:T(8,128)(2,1)} %get-tuple-element.25), channel_id=1, source_target_pairs={{4,0},{6,2},{8,4},{10,6},{12,8},{14,10},{16,12},{18,14},{20,16},{2... | collective-permute-start | bytes 393224 | tf_op jit(solution)/shard_map/ppermute | solution.py:218
  142.6 9.6 %collective-permute-start.5 = (bf16[64,1024]{1,0:T(8,128)(2,1)}, bf16[64,1024]{1,0:T(8,128)(2,1)}, u32[]{:S(2)}, u32[]{:S(2)}) collective-permute-start(bf16[64,1024]{1,0:T(8,128)(2,1)} %get-tuple-element.24), channel_id=1, source_target_pairs={{2,0},{4,2},{6,4},{8,6},{10,8},{12,10},{14,12},{16,14},{18,16},{20... | collective-permute-start | bytes 393224 | tf_op jit(solution)/shard_map/ppermute | solution.py:218
  144.5 10.8 %collective-permute-start.7 = (bf16[64,1024]{1,0:T(8,128)(2,1)}, bf16[64,1024]{1,0:T(8,128)(2,1)}, u32[]{:S(2)}, u32[]{:S(2)}) collective-permute-start(bf16[64,1024]{1,0:T(8,128)(2,1)} %get-tuple-element.24), channel_id=1, source_target_pairs={{0,2},{2,4},{4,6},{6,8},{8,10},{10,12},{12,14},{14,16},{16,18},{18... | collective-permute-start | bytes 393224 | tf_op jit(solution)/shard_map/ppermute | solution.py:218
  146.9 12.2 %collective-permute-start.8 = (bf16[64,1024]{1,0:T(8,128)(2,1)}, bf16[64,1024]{1,0:T(8,128)(2,1)}, u32[]{:S(2)}, u32[]{:S(2)}) collective-permute-start(bf16[64,1024]{1,0:T(8,128)(2,1)} %get-tuple-element.24), channel_id=1, source_target_pairs={{0,4},{2,6},{4,8},{6,10},{8,12},{10,14},{12,16},{14,18},{16,20},{1... | collective-permute-start | bytes 393224 | tf_op jit(solution)/shard_map/ppermute | solution.py:218
  172.9 1.7 collective-permute-start.15
  207.0 1.5 collective-permute-start.16

commit v2 on v1

v2 whole, which is shorter than its diff:
```python
import functools

import jax
import jax.numpy as jnp
from jax import lax
from jax.experimental import pallas as pl
from jax.experimental.pallas import tpu as pltpu
from jax.sharding import Mesh
from jax.sharding import PartitionSpec as P

HD = 128
TAPS = 128
BLK = 64
XL, Y, Z, CORE, HEAD = 2, 4, 8, 2, 2
ROWS = 2 * BLK
NQ = Z * ROWS
NK = XL * Y * CORE * ROWS
CTX = ("xl", "y", "z", "core")
LOWEST = -1e30
LOG2E = 1.4426950408889634
SCALE = HD**-0.5
QB = 256
BF = jnp.bfloat16
F32 = jnp.float32
LANES = 128


def nt(a, b):
    return lax.dot_general(a, b, (((1,), (1,)), ((), ())), preferred_element_type=F32)


def tn(a, b):
    return lax.dot_general(a, b, (((0,), (0,)), ((), ())), preferred_element_type=F32)


def nn(a, b):
    return lax.dot_general(a, b, (((1,), (0,)), ((), ())), preferred_element_type=F32)


def block_of(order_ref, xl, y, z, core, slot):
    return order_ref[(((xl * Y + y) * Z + z) * CORE + core) * 2 + slot]


def fill_key_positions(place_ref, order_ref, kpos):
    row = lax.broadcasted_iota(jnp.int32, (BLK, LANES), 0)
    at = 0
    for c in range(CORE):
        for b in range(Y):
            for a in range(XL):
                xl = lax.rem(place_ref[0] + a, XL)
                y = lax.rem(place_ref[1] + b, Y)
                core = lax.rem(place_ref[3] + c, CORE)
                for slot in range(2):
                    block = block_of(order_ref, xl, y, place_ref[2], core, slot)
                    kpos[at : at + BLK, :] = row + block * BLK
                    at += BLK


def query_positions(place_ref, order_ref, step):
    lane = lax.broadcasted_iota(jnp.int32, (1, QB), 1)
    pos = jnp.zeros((1, QB), jnp.int32)
    for b in range(QB // BLK):
        at = step * (QB // BLK) + b
        block = block_of(order_ref, place_ref[0], place_ref[1], at // 2, place_ref[3], at % 2)
        pos = jnp.where(lane // BLK == b, block * BLK + lane % BLK, pos)
    return pos


def scores_t(q, k, kpos, qpos):
    s = nt(k, q) * (SCALE * LOG2E)
    seen = jnp.concatenate([kpos[...]] * (QB // LANES), axis=1) <= qpos
    return jnp.where(seen, s, LOWEST)


def stats_kernel(place_ref, order_ref, q_ref, g_ref, k_ref, v_ref, stat_ref, kpos):
    step = pl.program_id(0)

    @pl.when(step == 0)
    def _():
        fill_key_positions(place_ref, order_ref, kpos)

    s = scores_t(q_ref[...], k_ref[...], kpos, query_positions(place_ref, order_ref, step))
    dp = nt(v_ref[...], g_ref[...])
    top = jnp.max(s, axis=0, keepdims=True)
    w = jnp.exp2(s - top)
    norm = jnp.sum(w, axis=0, keepdims=True)
    cross = jnp.sum(w * dp, axis=0, keepdims=True)
    stat = jnp.concatenate((top + jnp.log2(norm), cross / norm), axis=0)
    stat_ref[...] = jnp.broadcast_to(stat[None], stat_ref.shape)


def grads_kernel(
    place_ref, order_ref, q_ref, g_ref, k_ref, v_ref, stat_ref, dq_ref, own_ref, other_ref, dk_acc, dv_acc, kpos
):
    step = pl.program_id(0)

    @pl.when(step == 0)
    def _():
        fill_key_positions(place_ref, order_ref, kpos)
        dk_acc[...] = jnp.zeros_like(dk_acc)
        dv_acc[...] = jnp.zeros_like(dv_acc)

    parts = stat_ref[:, 0, :]
    top = jnp.max(parts, axis=0, keepdims=True)
    lse = top + jnp.log2(jnp.sum(jnp.exp2(parts - top), axis=0, keepdims=True))
    delta = jnp.sum(jnp.exp2(parts - lse) * stat_ref[:, 1, :], axis=0, keepdims=True)
    q = q_ref[...]
    g = g_ref[...]
    s = scores_t(q, k_ref[...], kpos, query_positions(place_ref, order_ref, step))
    p = jnp.exp2(s - lse)
    dp = nt(v_ref[...], g)
    ds = (p * (dp - delta)).astype(BF)
    dv_acc[...] += nn(p.astype(BF), g)
    dk_acc[...] += nn(ds, q)
    dq_ref[...] = (SCALE * tn(ds, k_ref[...])).astype(dq_ref.dtype)

    @pl.when(step == pl.num_programs(0) - 1)
    def _():
        for at, ref in ((0, own_ref), (NK // 2, other_ref)):
            for b in range(Y):
                for a in range(XL):
                    owner = lax.rem(place_ref[0] + a, XL) * Y + lax.rem(place_ref[1] + b, Y)
                    here = pl.ds(at + (b * XL + a) * ROWS, ROWS)
                    there = pl.ds(pl.multiple_of(owner * ROWS, ROWS), ROWS)
                    ref[there, :HD] = SCALE * dk_acc[here, :]
                    ref[there, HD:] = dv_acc[here, :]


def attention_specs():
    rows = lambda col: pl.BlockSpec((QB, HD), lambda i, *_: (i, col))
    keys = lambda col: pl.BlockSpec((NK, HD), lambda i, *_: (0, col))
    return [
        rows(0),
        rows(1),
        keys(0),
        keys(1),
    ]


STAT = pl.BlockSpec((Z, 2, QB), lambda i, *_: (0, 0, i))


def attention_stats(place, order, qg, kv):
    return pl.pallas_call(
        stats_kernel,
        grid_spec=pltpu.PrefetchScalarGridSpec(
            num_scalar_prefetch=2,
            grid=(NQ // QB,),
            in_specs=attention_specs(),
            out_specs=STAT,
            scratch_shapes=[pltpu.VMEM((NK, LANES), jnp.int32)],
        ),
        out_shape=jax.ShapeDtypeStruct((Z, 2, NQ), F32),
        compiler_params=pltpu.CompilerParams(vmem_limit_bytes=40 << 20),
        cost_estimate=pl.CostEstimate(flops=4 * NQ * NK * HD, bytes_accessed=4 << 20, transcendentals=NQ * NK),
        name="attention_stats",
    )(place, order, qg, qg, kv, kv)


def attention_grads(place, order, qg, kv, stats):
    half = pl.BlockSpec((NK // 2, 2 * HD), lambda i, *_: (0, 0))
    return pl.pallas_call(
        grads_kernel,
        grid_spec=pltpu.PrefetchScalarGridSpec(
            num_scalar_prefetch=2,
            grid=(NQ // QB,),
            in_specs=attention_specs() + [STAT],
            out_specs=[pl.BlockSpec((QB, HD), lambda i, *_: (i, 0)), half, half],
            scratch_shapes=[
                pltpu.VMEM((NK, HD), F32),
                pltpu.VMEM((NK, HD), F32),
                pltpu.VMEM((NK, LANES), jnp.int32),
            ],
        ),
        out_shape=[
            jax.ShapeDtypeStruct((NQ, HD), BF),
            jax.ShapeDtypeStruct((NK // 2, 2 * HD), F32),
            jax.ShapeDtypeStruct((NK // 2, 2 * HD), F32),
        ],
        compiler_params=pltpu.CompilerParams(vmem_limit_bytes=40 << 20),
        cost_estimate=pl.CostEstimate(flops=10 * NQ * NK * HD, bytes_accessed=4 << 20, transcendentals=NQ * NK),
        name="attention_grads",
    )(place, order, qg, qg, kv, kv, stats)


def pack_kernel(q_ref, g_ref, k_ref, v_ref, qg_ref, kv_ref):
    kv_ref[:, :HD] = k_ref[...]
    kv_ref[:, HD:] = v_ref[...]
    for i in range(Z):
        qg_ref[i, :, :HD] = q_ref[...]
        qg_ref[i, :, HD:] = g_ref[...]


def pack(q, g, k, v):
    return pl.pallas_call(
        pack_kernel,
        out_shape=[jax.ShapeDtypeStruct((Z, ROWS, 2 * HD), BF), jax.ShapeDtypeStruct((ROWS, 2 * HD), BF)],
        name="pack",
    )(q, g, k, v)


def stack_blocks(refs, stack):
    at = 0
    for ref in refs:
        for b in range(ref.shape[0] // BLK):
            stack[at] = ref[b * BLK : (b + 1) * BLK, :].astype(F32)
            at += 1
    stack[at] = jnp.zeros((BLK, LANES), F32)


def low_high(place_ref, order_ref, distance):
    at = ((place_ref[0] * Y + place_ref[1]) * Z + place_ref[2]) * CORE + place_ref[3] + distance
    inside = jnp.logical_and(at >= 0, at < XL * Y * Z * CORE)
    at = jnp.where(inside, at, 0)
    first, second = order_ref[2 * at], order_ref[2 * at + 1]
    low = jnp.where(inside, jnp.minimum(first, second), -1000)
    high = jnp.where(inside, jnp.maximum(first, second), -1000)
    return low, high


def extend(place_ref, order_ref, have, shift, cand, ext):
    at = ((place_ref[0] * Y + place_ref[1]) * Z + place_ref[2]) * CORE + place_ref[3]
    for slot in range(2):
        own = order_ref[2 * at + slot]
        for part in range(3):
            place = jnp.int32(len(have))
            for i, block in enumerate(have):
                place = jnp.where(block == own + (part + shift), i, place)
            ext[slot, part * BLK : (part + 1) * BLK, :] = cand[place]


def filter_kernel(
    n_in, place_ref, order_ref, q_own, kv_own, q_other, kv_other, w_own, w_other, *refs
):
    ins = refs[:n_in]
    pair_ref, low_ref, high_ref, filt_ref, cand, grad, ext, lag = refs[n_in:]
    cg = jnp.zeros((ROWS, LANES), F32)
    for q_ref, kv_ref, w_ref in ((q_own, kv_own, w_own), (q_other, kv_other, w_other)):
        cg = cg + nt(q_ref[...], w_ref[0])
        cg = cg + nt(kv_ref[:, :HD], w_ref[1])
        cg = cg + nt(kv_ref[:, HD:], w_ref[2])
    grad[...] = cg.astype(BF).astype(F32)
    device = ((place_ref[0] * Y + place_ref[1]) * Z + place_ref[2]) * CORE + place_ref[3]
    first, second = order_ref[2 * device], order_ref[2 * device + 1]
    swapped = (first > second).astype(jnp.int32)
    low = grad[pl.ds(pl.multiple_of(swapped * BLK, BLK), BLK), :].astype(BF)
    high = grad[pl.ds(pl.multiple_of((1 - swapped) * BLK, BLK), BLK), :].astype(BF)
    low_ref[...] = low
    high_ref[...] = high
    pair_ref[:BLK, :] = low
    pair_ref[BLK:, :] = high
    stack_blocks(ins, cand)
    near = [low_high(place_ref, order_ref, d) for d in (-2, -1, 1, 2)]
    device_of = lambda d: 2 * jnp.clip(device + d, 0, XL * Y * Z * CORE - 1)
    inside = lambda d, block: jnp.where(
        jnp.logical_and(device + d >= 0, device + d < XL * Y * Z * CORE), block, -1000
    )
    have = [first, second, near[0][0]]
    have += [inside(-1, order_ref[device_of(-1) + s]) for s in range(2)]
    have += [inside(1, order_ref[device_of(1) + s]) for s in range(2)]
    have += [near[3][1]]
    extend(place_ref, order_ref, have, -2, cand, ext)
    for r in range(8):
        for slot in range(2):
            rows = [grad[slot * BLK + 8 * m : slot * BLK + 8 * m + 8, :] for m in range(BLK // 8)]
            last = 2 * BLK - r
            shifted = [ext[slot, last - TAPS + 8 + 8 * n : last - TAPS + 16 + 8 * n, :] for n in range(23)]
            for a in range(TAPS // 8):
                total = rows[0] * shifted[15 - a]
                for m in range(1, BLK // 8):
                    total = total + rows[m] * shifted[15 - a + m]
                j = 8 * a + r
                lag[j] = total if slot == 0 else lag[j] + total
    filt_ref[0] = jnp.sum(lag[...], axis=1).T


def project_and_filter(place, order, q_own, kv_own, q_other, kv_other, weight, w_other, ins):
    channels = ins[0].shape[1]
    tiles = channels // LANES
    half = tiles // 2
    whole = lambda a: pl.BlockSpec(a.shape, lambda i, p, o: (0, 0))
    column = lambda a: pl.BlockSpec((a.shape[0], LANES), lambda i, p, o: (0, i))
    which = lambda i, p, o: (jnp.where(i // half == p[3], 0, 1), lax.rem(i, half), 0)
    block = lambda rows: pl.BlockSpec((rows, LANES), lambda i, p, o: (0, i))
    blocks = sum(a.shape[0] // BLK for a in ins) + 1
    return pl.pallas_call(
        functools.partial(filter_kernel, len(ins)),
        grid_spec=pltpu.PrefetchScalarGridSpec(
            num_scalar_prefetch=2,
            grid=(tiles,),
            in_specs=[whole(a) for a in (q_own, kv_own, q_other, kv_other)]
            + [
                pl.BlockSpec((3, LANES, HD), lambda i, p, o: (0, p[4] * tiles + i, 0)),
                pl.BlockSpec((3, LANES, HD), lambda i, p, o: (0, i, 0)),
            ]
            + [column(a) for a in ins],
            out_specs=[block(ROWS), block(BLK), block(BLK), pl.BlockSpec((1, LANES, TAPS), which)],
            scratch_shapes=[
                pltpu.VMEM((blocks, BLK, LANES), F32),
                pltpu.VMEM((ROWS, LANES), F32),
                pltpu.VMEM((2, 3 * BLK, LANES), F32),
                pltpu.VMEM((TAPS, 8, LANES), F32),
            ],
        ),
        out_shape=[
            jax.ShapeDtypeStruct((ROWS, channels), BF),
            jax.ShapeDtypeStruct((BLK, channels), BF),
            jax.ShapeDtypeStruct((BLK, channels), BF),
            jax.ShapeDtypeStruct((2, channels // 2, TAPS), F32),
        ],
        compiler_params=pltpu.CompilerParams(vmem_limit_bytes=40 << 20),
        cost_estimate=pl.CostEstimate(flops=4 << 30, bytes_accessed=8 << 20, transcendentals=0),
        name="project_and_filter",
    )(place, order, q_own, kv_own, q_other, kv_other, weight, w_other, *ins)


def conv_kernel(n_grad, place_ref, order_ref, *refs):
    grads = refs[:n_grad]
    filter_ref, out_ref, cand, ext, taps_ref = refs[n_grad:]
    taps_ref[...] = filter_ref[...].T
    stack_blocks(grads, cand)
    near = [low_high(place_ref, order_ref, d) for d in (0, 1, 2, -1, -2)]
    have = [near[0][0], near[0][1], near[1][0], near[1][1], near[2][0], near[3][1], near[4][1]]
    extend(place_ref, order_ref, have, 0, cand, ext)
    for slot in range(2):
        acc = [jnp.zeros((8, LANES), F32) for _ in range(BLK // 8)]
        for r in range(8):
            shifted = [ext[slot, r + 8 * n : r + 8 * n + 8, :] for n in range(23)]
            for a in range(TAPS // 8):
                tap = taps_ref[8 * a + r : 8 * a + r + 1, :]
                for m in range(BLK // 8):
                    acc[m] = acc[m] + tap * shifted[m + a]
        out_ref[slot * BLK : (slot + 1) * BLK, :] = jnp.concatenate(acc, axis=0).astype(BF)


def input_conv(place, order, grads, taps):
    channels = taps.shape[0]
    column = lambda a: pl.BlockSpec((a.shape[0], LANES), lambda i, p, o: (0, i))
    blocks = sum(a.shape[0] // BLK for a in grads) + 1
    return pl.pallas_call(
        functools.partial(conv_kernel, len(grads)),
        grid_spec=pltpu.PrefetchScalarGridSpec(
            num_scalar_prefetch=2,
            grid=(channels // LANES,),
            in_specs=[column(a) for a in grads] + [pl.BlockSpec((LANES, TAPS), lambda i, p, o: (i, 0))],
            out_specs=pl.BlockSpec((ROWS, LANES), lambda i, p, o: (0, i)),
            scratch_shapes=[
                pltpu.VMEM((blocks, BLK, LANES), F32),
                pltpu.VMEM((2, 3 * BLK, LANES), F32),
                pltpu.VMEM((TAPS, LANES), F32),
            ],
        ),
        out_shape=jax.ShapeDtypeStruct((ROWS, channels), BF),
        compiler_params=pltpu.CompilerParams(vmem_limit_bytes=40 << 20),
        cost_estimate=pl.CostEstimate(flops=1 << 20, bytes_accessed=1 << 20, transcendentals=0),
        name="input_conv",
    )(place, order, *grads, taps)


def to_all(x, axes, count):
    return lax.all_to_all(jnp.broadcast_to(x[None], (count,) + x.shape), axes, 0, 0, tiled=True)


def swap(x, axis):
    return lax.ppermute(x, axis, [(0, 1), (1, 0)])


def from_ctx(x, distance):
    n = XL * Y * Z * CORE
    return lax.ppermute(x, CTX, [(i + distance, i) for i in range(n) if 0 <= i + distance < n])


def around(x, step, size, axis):
    return lax.ppermute(x, axis, [((i + step) % size, i) for i in range(size)])


def local(block_order, conv_input, conv_filter, query_rows, key_rows, value_rows, out_grad, qkv_weight):
    coords = [lax.axis_index(axis) for axis in CTX + ("head",)]
    core, head = coords[3], coords[4]
    channels = conv_input.shape[1]
    chips = XL * Y * Z
    entry = lax.iota(jnp.int32, 8)
    place = jnp.zeros((8,), jnp.int32)
    for i, coord in enumerate(coords):
        place = jnp.where(entry == i, coord, place)

    qg, kv = pack(query_rows, out_grad, key_rows, value_rows)
    qg = lax.all_to_all(qg, "z", 0, 0, tiled=True).reshape(NQ, 2 * HD)
    kv_xl = swap(kv, "xl")
    kv = jnp.concatenate((kv, kv_xl), axis=0)
    kv = jnp.concatenate([kv] + [around(kv, s, Y, "y") for s in range(1, Y)], axis=0)
    kv = jnp.concatenate((kv, swap(kv, "core")), axis=0)

    device = ((coords[0] * Y + coords[1]) * Z + coords[2]) * CORE + core
    ids = lax.dynamic_slice_in_dim(block_order, device * 2, 2, 0)
    swapped = (ids[0] > ids[1]).astype(jnp.int32)
    x_low = lax.dynamic_slice_in_dim(conv_input, swapped * BLK, BLK, 0)
    x_high = lax.dynamic_slice_in_dim(conv_input, (1 - swapped) * BLK, BLK, 0)
    w_sent = lax.dynamic_slice_in_dim(qkv_weight, (1 - head) * channels, channels, 1)
    w_sent, x_low, x_high, kv_xl = lax.optimization_barrier((w_sent, x_low, x_high, kv_xl))
    w_other = swap(w_sent, "head")

    stats = attention_stats(place, block_order, qg, kv)
    stats = lax.all_to_all(stats, "z", 0, 0, tiled=True)
    stats, w_other = lax.optimization_barrier((stats, w_other))
    dq, dkv_own, dkv_other = attention_grads(place, block_order, qg, kv, stats)

    dq, x_low, x_high = lax.optimization_barrier((dq, x_low, x_high))
    moved_far = [from_ctx(x_low, -2), from_ctx(x_high, 2)]
    dq_parts = lax.all_to_all(dq.reshape(Z, ROWS, HD), "z", 0, 0, tiled=True)
    dkv = (dkv_own + swap(dkv_other, "core")).astype(BF).reshape(XL * Y, ROWS, 2 * HD)
    dq_parts, dkv, x_near, moved_far = lax.optimization_barrier((dq_parts, dkv, conv_input, moved_far))
    dkv_parts = lax.all_to_all(dkv, ("xl", "y"), 0, 0, tiled=True)
    moved_near = [from_ctx(x_near, -1), from_ctx(x_near, 1)]
    dkv_parts, moved_near = lax.optimization_barrier((dkv_parts, moved_near))
    query_grad = jnp.sum(dq_parts.astype(F32), axis=0).astype(BF)
    q_other = swap(query_grad, "head")
    kv_grad = jnp.sum(dkv_parts.astype(F32), axis=0).astype(BF)
    kv_other = swap(kv_grad, "head")

    ins = [conv_input, moved_far[0], *moved_near, moved_far[1]]
    g_pair, g_low, g_high, filter_part = project_and_filter(
        place, block_order, query_grad, kv_grad, q_other, kv_other, qkv_weight, w_other, ins
    )

    mine_sum = filter_part[0] + swap(filter_part[1], "core")
    far = [from_ctx(g_low, 2), from_ctx(g_high, -2)]
    parts = lax.all_to_all(
        mine_sum.reshape(chips, channels // 2 // chips, TAPS), ("xl", "y", "z"), 0, 0, tiled=True
    )
    parts, far, g_pair, g_high = lax.optimization_barrier((parts, far, g_pair, g_high))
    total = jnp.sum(parts, axis=0)
    total, g_pair, g_high = lax.optimization_barrier((total, g_pair, g_high))
    grads = [g_pair, from_ctx(g_pair, 1), far[0], from_ctx(g_high, -1), far[1]]
    half = to_all(total, ("xl", "y", "z"), chips)
    input_grad = input_conv(place, block_order, grads, conv_filter)
    half, input_grad = lax.optimization_barrier((half, input_grad))
    half = half.reshape(channels // 2, TAPS)
    other = swap(half, "core")
    filter_grad = jnp.concatenate(
        (jnp.where(core == 0, half, other), jnp.where(core == 0, other, half)), axis=0
    )
    return input_grad, filter_grad


def solution(mesh):
    fine = Mesh(mesh.devices.reshape(XL, Y, Z, CORE, HEAD), CTX + ("head",))
    rows = P(CTX, "head")
    return jax.shard_map(
        local,
        mesh=fine,
        in_specs=(P(), rows, P("head", None), rows, rows, rows, rows, P(None, None, "head")),
        out_specs=(rows, P("head", None)),
        check_vma=False,
    )
```

time: 212 us -> 183 us (0.86)
  blocking collectives: 32.3 us -> 0 us
  starting transfers between devices: 63.5 us -> 76.5 us
  Pallas kernels: 27.5 us -> 35.2 us
  other arithmetic: 12.5 us -> 4.9 us
  local copies, waits for them, and re-layouts: 21.3 us -> 14 us
  matrix products: 4.28 us -> 0 us
  waiting for transfers between devices: 45.6 us -> 47.8 us
    all_to_all x2 -> x0, blocking collectives: 32.3 us -> none  [the longest x1 17.4 us: to_all(): lax.all_to_all(jnp.broadcast_to(x[None], (count,) + x.shape), axes, 0, 0,...]
    ppermute x11 -> x8, waiting for transfers between devices: 6.93 us -> 29 us  [from_ctx(): lax.ppermute(x, CTX, [(i + distance, i) for i in range(n) if 0 <= i + dis...]
    all_to_all x2 -> x5, starting transfers between devices: 8.54 us -> 28.2 us  [the longest x1 8.6 us: local(): qg = lax.all_to_all(qg, 'z', 0, 0, tiled=True).reshape(NQ, 2 * HD)]
    all_to_all x2 -> x5, waiting for transfers between devices: 17.9 us -> 2.12 us  [the longest x1 2.11 us: local(): stats = lax.all_to_all(stats, 'z', 0, 0, tiled=True)]
    all_to_all x3 -> x1, waiting for transfers between devices: 15.5 us -> 0.01 us  [to_all(): lax.all_to_all(jnp.broadcast_to(x[None], (count,) + x.shape), axes, 0, 0,...]
    all_to_all x3 -> x1, starting transfers between devices: 13.2 us -> 4.19 us  [to_all(): lax.all_to_all(jnp.broadcast_to(x[None], (count,) + x.shape), axes, 0, 0,...]
    ppermute x6 -> x8, waiting for transfers between devices: 5.27 us -> 12.6 us  [swap(): return lax.ppermute(x, axis, [(0, 1), (1, 0)])]
    another operation x3 -> x0, local copies, waits for them, and re-layouts: 6.79 us -> none  [the longest x1 3.64 us: local(): jnp.stack((ids[0], ids[1], low[3], high[3], low[4], high[1], high[0]))]
  transfers between devices with their start and end apart: 22 -> 25, of which waited for: 10 -> 14; matrix products, arithmetic and copies ran while one was open for 15% -> 6% of each run, Pallas kernels for 7% -> 8%
where the time goes in v2:
time: 183 us; the launch traced here: 180 us
  starting transfers between devices  76.5 us (42%)
  waiting for transfers between devices  47.8 us (26%)
  Pallas kernels  35.2 us (19%)
  local copies, waits for them, and re-layouts  14 us (8%)
  other arithmetic  4.9 us (3%)
  between operations  2.11 us (1%)
    ppermute x8, starting transfers between devices, from_ctx(): lax.ppermute(x, CTX, [(i + distance, i) for i in range(n) if 0 <= i + dis...  33.5 us
    ppermute x8, waiting for transfers between devices, from_ctx(): lax.ppermute(x, CTX, [(i + distance, i) for i in range(n) if 0 <= i + dis...  29 us
    ppermute x8, waiting for transfers between devices, swap(): return lax.ppermute(x, axis, [(0, 1), (1, 0)])  12.6 us
    pallas_call x1, Pallas kernels, project_and_filter(): pl.pallas_call(functools.partial(filter_kernel, len(ins)), grid_spec=pltp...  10.9 us
    unnamed x36, local copies, waits for them, and re-layouts  10.2 us
    all_to_all x1, starting transfers between devices, local(): qg = lax.all_to_all(qg, 'z', 0, 0, tiled=True).reshape(NQ, 2 * HD)  8.6 us
    pallas_call x1, Pallas kernels, attention_grads(): pl.pallas_call(grads_kernel, grid_spec=pltpu.PrefetchScalarGridSpec(num_s...  8.57 us
    pallas_call x1, Pallas kernels, attention_stats(): pl.pallas_call(stats_kernel, grid_spec=pltpu.PrefetchScalarGridSpec(num_s...  7.13 us
  transfers between devices with their start and end apart: 25, of which 14 were waited for; matrix products, arithmetic and copies ran while one was open for 6% of the time, Pallas kernels for 8%

profile of v2, /device:TPU:6, one launch (start us, length us, event | category | flops | bytes accessed | tf_op | source)
XLA Modules:
  0.0 180.5 jit_solution(7427830781931579021)
XLA Ops:
  0.6 1.8 pack.1
  2.4 0.8 collective-permute-start
  3.3 8.6 %all-to-all-start = ((bf16[8,128,256]{2,1,0:T(8,128)(2,1)}), bf16[8,128,256]{2,1,0:T(8,128)(2,1)S(1)}, u32[]{:S(2)}, u32[]{:S(2)}) async-start(bf16[8,128,256]{2,1,0:T(8,128)(2,1)} %get-tuple-element.37), calls=%async_computation | async-start | bytes 1048576 | tf_op jit(solution)/shard_map/all_to_all | solution.py:388
  11.9 1.5 constant_dynamic-update-slice_fusion.6
  13.4 0.7 constant_dynamic-update-slice_fusion.5
  14.0 3.0 %collective-permute-start.1 = (bf16[256,256]{1,0:T(8,128)(2,1)}, bf16[256,256]{1,0:T(8,128)(2,1)S(1)}, u32[]{:S(2)}, u32[]{:S(2)}) collective-permute-start(bf16[256,256]{1,0:T(8,128)(2,1)} %get-tuple-element.84), channel_id=1, source_target_pairs={{32,0},{64,32},{96,64},{0,96},{33,1},{65,33},{97,65},{1,97},{34,2}... | collective-permute-start | bytes 393224 | tf_op jit(solution)/shard_map/ppermute | solution.py:374
  17.1 0.9 constant_dynamic-slice_fusion.2
  18.0 0.1 dynamic_slice.13
  18.1 0.7 collective-permute-start.2
  18.7 0.6 fusion.1
  20.6 1.0 collective-permute-start.3
  21.6 1.1 collective-permute-done.1
  22.7 0.7 constant_dynamic-update-slice_fusion.4
  23.4 3.0 %collective-permute-done.2 = bf16[256,256]{1,0:T(8,128)(2,1)} collective-permute-done((bf16[256,256]{1,0:T(8,128)(2,1)}, bf16[256,256]{1,0:T(8,128)(2,1)}, u32[]{:S(2)}, u32[]{:S(2)}) %collective-permute-start.2) | collective-permute-done | bytes 131104 | tf_op jit(solution)/shard_map/ppermute | solution.py:374
  26.3 1.6 constant_dynamic-update-slice_fusion.3
  27.9 0.7 constant_dynamic-update-slice_fusion.2
  28.6 0.7 constant_dynamic-slice_fusion
  29.3 1.1 collective-permute-start.5
  30.4 0.3 collective-permute-done.4
  30.8 7.1 %attention_stats.1 = f32[8,2,1024]{2,1,0:T(2,128)} custom-call(s32[8]{0:T(128)S(1)} %compare_select_fusion.4.place_ref, s32[256]{0:T(256)S(1)} %copy-done.6, bf16[1024,256]{1,0:T(8,128)(2,1)S(1)} %bitcast.16, bf16[1024,256]{1,0:T(8,128)(2,1)S(1)} %bitcast.17, bf16[2048,256]{1,0:T(8,128)(2,1)S(1)} %constant_dynamic-update-slice_fusion.7.k_ref.v_ref, ...), custom_call_target="tpu_custom_call" | custom-call | flops 1073741824 | bytes 4194304 | tf_op jit(solution)/shard_map/attention_stats/pallas_call | solution.py:144
  37.9 6.9 %all-to-all-start.1 = ((f32[8,2,1024]{2,1,0:T(2,128)}), f32[8,2,1024]{2,1,0:T(2,128)S(1)}, u32[]{:S(2)}, u32[]{:S(2)}) async-start(f32[8,2,1024]{2,1,0:T(2,128)} %attention_stats.1), calls=%async_computation.1 | async-start | bytes 131072 | tf_op jit(solution)/shard_map/all_to_all | solution.py:404
  44.8 6.3 %collective-permute-done.5.w_other = bf16[3,1024,128]{2,1,0:T(8,128)(2,1)} collective-permute-done((bf16[3,1024,128]{2,1,0:T(8,128)(2,1)}, bf16[3,1024,128]{2,1,0:T(8,128)(2,1)}, u32[]{:S(2)}, u32[]{:S(2)}) %collective-permute-start.5) | collective-permute-done | bytes 786464 | tf_op jit(solution)/shard_map/ppermute | solution.py:365
  51.1 2.1 %all-to-all-done.1.stat_ref = f32[8,2,1024]{2,1,0:T(2,128)S(1)} async-done(((f32[8,2,1024]{2,1,0:T(2,128)}), f32[8,2,1024]{2,1,0:T(2,128)S(1)}, u32[]{:S(2)}, u32[]{:S(2)}) %all-to-all-start.1) | async-done | bytes 65568 | tf_op jit(solution)/shard_map/all_to_all | solution.py:404
  53.2 1.2 copy-done.5
  54.4 8.6 %attention_grads.1 = (bf16[1024,128]{1,0:T(8,128)(2,1)S(1)}, f32[1024,256]{1,0:T(8,128)S(1)}, f32[1024,256]{1,0:T(8,128)}) custom-call(s32[8]{0:T(128)S(1)} %compare_select_fusion.4.place_ref, s32[256]{0:T(256)S(1)} %copy-done.6, bf16[1024,256]{1,0:T(8,128)(2,1)S(1)} %bitcast.18, bf16[1024,256]{1,0:T(8,128)(2,1)S(1)} %bitcast.19, ...), custom_call_target="tpu_custom_call" | custom-call | flops 2684354560 | bytes 4194304 | tf_op jit(solution)/shard_map/attention_grads/pallas_call | solution.py:162
  63.0 0.7 copy-done.3
  63.7 4.8 %all-to-all-start.2 = ((bf16[8,128,128]{2,1,0:T(8,128)(2,1)}), bf16[8,128,128]{2,1,0:T(8,128)(2,1)S(1)}, u32[]{:S(2)}, u32[]{:S(2)}) async-start(bf16[8,128,128]{2,1,0:T(8,128)(2,1)} %bitcast.20), calls=%async_computation.2 | async-start | bytes 524288 | tf_op jit(solution)/shard_map/all_to_all | solution.py:410
  68.5 3.9 %collective-permute-start.7 = (bf16[64,1024]{1,0:T(8,128)(2,1)}, bf16[64,1024]{1,0:T(8,128)(2,1)S(1)}, u32[]{:S(2)}, u32[]{:S(2)}) collective-permute-start(bf16[64,1024]{1,0:T(8,128)(2,1)} %get-tuple-element.47), channel_id=1, source_target_pairs={{0,4},{2,6},{4,8},{6,10},{8,12},{10,14},{12,16},{14,18},{16,20},{1... | collective-permute-start | bytes 393224 | tf_op jit(solution)/shard_map/ppermute | solution.py:370
  72.4 6.1 %collective-permute-start.8 = (bf16[64,1024]{1,0:T(8,128)(2,1)}, bf16[64,1024]{1,0:T(8,128)(2,1)S(1)}, u32[]{:S(2)}, u32[]{:S(2)}) collective-permute-start(bf16[64,1024]{1,0:T(8,128)(2,1)} %get-tuple-element.48), channel_id=1, source_target_pairs={{4,0},{6,2},{8,4},{10,6},{12,8},{14,10},{16,12},{18,14},{20,16},{2... | collective-permute-start | bytes 393224 | tf_op jit(solution)/shard_map/ppermute | solution.py:370
  78.6 2.2 %add_convert_fusion = bf16[1024,256]{1,0:T(8,128)(2,1)} fusion(f32[1024,256]{1,0:T(8,128)S(1)} %get-tuple-element.45, f32[1024,256]{1,0:T(8,128)} %collective-permute-done.6), kind=kLoop, calls=%fused_computation | loop fusion | flops 524288 | bytes 2621440 | tf_op jit(solution)/shard_map/convert_element_type | solution.py:411
  80.7 1.2 collective-permute-done.7.refs_1_
  82.0 0.7 copy-done.15
  82.7 3.7 %all-to-all-start.3 = ((bf16[8,128,256]{2,1,0:T(8,128)(2,1)}), bf16[8,128,256]{2,1,0:T(8,128)(2,1)S(1)}, u32[]{:S(2)}, u32[]{:S(2)}) async-start(bf16[8,128,256]{2,1,0:T(8,128)(2,1)} %bitcast.21), calls=%async_computation.3 | async-start | bytes 1048576 | tf_op jit(solution)/shard_map/all_to_all | solution.py:413
  86.4 7.2 %collective-permute-start.10 = (bf16[128,1024]{1,0:T(8,128)(2,1)S(1)}, bf16[128,1024]{1,0:T(8,128)(2,1)S(1)}, u32[]{:S(2)}, u32[]{:S(2)}) collective-permute-start(bf16[128,1024]{1,0:T(8,128)(2,1)S(1)} %copy-done.2), channel_id=1, source_target_pairs={{2,0},{4,2},{6,4},{8,6},{10,8},{12,10},{14,12},{16,14},{18,16},{20... | collective-permute-start | bytes 786440 | tf_op jit(solution)/shard_map/ppermute | solution.py:370
  93.6 1.9 %collective-permute-start.9 = (bf16[128,1024]{1,0:T(8,128)(2,1)S(1)}, bf16[128,1024]{1,0:T(8,128)(2,1)S(1)}, u32[]{:S(2)}, u32[]{:S(2)}) collective-permute-start(bf16[128,1024]{1,0:T(8,128)(2,1)S(1)} %copy-done.2), channel_id=1, source_target_pairs={{0,2},{2,4},{4,6},{6,8},{8,10},{10,12},{12,14},{14,16},{16,18},{18... | collective-permute-start | bytes 786440 | tf_op jit(solution)/shard_map/ppermute | solution.py:370
  95.6 1.9 %collective-permute-done.10.refs_3_ = bf16[128,1024]{1,0:T(8,128)(2,1)S(1)} collective-permute-done((bf16[128,1024]{1,0:T(8,128)(2,1)S(1)}, bf16[128,1024]{1,0:T(8,128)(2,1)S(1)}, u32[]{:S(2)}, u32[]{:S(2)}) %collective-permute-start.10) | collective-permute-done | bytes 262176 | tf_op jit(solution)/shard_map/ppermute | solution.py:370
  97.5 8.1 %collective-permute-done.9.refs_2_ = bf16[128,1024]{1,0:T(8,128)(2,1)S(1)} collective-permute-done((bf16[128,1024]{1,0:T(8,128)(2,1)S(1)}, bf16[128,1024]{1,0:T(8,128)(2,1)S(1)}, u32[]{:S(2)}, u32[]{:S(2)}) %collective-permute-start.9) | collective-permute-done | bytes 262176 | tf_op jit(solution)/shard_map/ppermute | solution.py:370
  105.7 0.1 reduce_sum.34.kv_own
  105.7 1.2 collective-permute-start.12
  106.9 1.0 reduce_sum.33.q_own
  107.9 2.7 %collective-permute-start.11 = (bf16[128,128]{1,0:T(8,128)(2,1)S(1)}, bf16[128,128]{1,0:T(8,128)(2,1)S(1)}, u32[]{:S(2)}, u32[]{:S(2)}) collective-permute-start(bf16[128,128]{1,0:T(8,128)(2,1)S(1)} %reduce_sum.33.q_own), channel_id=1, source_target_pairs={{0,1},{1,0},{2,3},{3,2},{4,5},{5,4},{6,7},{7,6},{8,9},{9,8},{10,11... | collective-permute-start | bytes 98312 | tf_op jit(solution)/shard_map/ppermute | solution.py:365
  110.6 3.0 %collective-permute-done.11.q_other = bf16[128,128]{1,0:T(8,128)(2,1)S(1)} collective-permute-done((bf16[128,128]{1,0:T(8,128)(2,1)S(1)}, bf16[128,128]{1,0:T(8,128)(2,1)S(1)}, u32[]{:S(2)}, u32[]{:S(2)}) %collective-permute-start.11) | collective-permute-done | bytes 32800 | tf_op jit(solution)/shard_map/ppermute | solution.py:365
  113.6 0.9 copy-done.8
  114.5 0.9 copy-done.10
  115.4 10.9 %project_and_filter.1 = (bf16[128,1024]{1,0:T(8,128)(2,1)S(1)}, bf16[64,1024]{1,0:T(8,128)(2,1)S(1)}, bf16[64,1024]{1,0:T(8,128)(2,1)S(1)}, f32[2,512,128]{2,1,0:T(8,128)S(1)}) custom-call(s32[8]{0:T(128)S(1)} %compare_select_fusion.4.place_ref, s32[256]{0:T(256)S(1)} %copy-done.6, bf16[128,128]{1,0:T(8,128)(2,1)S(1)} %reduce_sum.33.q_own, ...), custom_call_target="tpu_custom_call" | custom-call | flops 4294967296 | bytes 8388608 | tf_op jit(solution)/shard_map/project_and_filter/pallas_call | solution.py:286
  126.3 0.6 copy-done.11
  127.0 0.7 copy-done.13
  127.7 0.1 collective-permute-start.13
  127.8 1.5 collective-permute-done.13
  129.3 0.7 fusion
  130.0 4.2 %all-to-all-start.4 = ((f32[64,8,128]{2,1,0:T(8,128)}), f32[64,8,128]{2,1,0:T(8,128)S(1)}, u32[]{:S(2)}, u32[]{:S(2)}) async-start(f32[64,8,128]{2,1,0:T(8,128)} %fusion), calls=%async_computation.4 | async-start | bytes 524288 | tf_op jit(solution)/shard_map/all_to_all | solution.py:428
  134.2 6.4 %collective-permute-start.14 = (bf16[64,1024]{1,0:T(8,128)(2,1)S(1)}, bf16[64,1024]{1,0:T(8,128)(2,1)S(1)}, u32[]{:S(2)}, u32[]{:S(2)}) collective-permute-start(bf16[64,1024]{1,0:T(8,128)(2,1)S(1)} %copy-done.14), channel_id=1, source_target_pairs={{4,0},{6,2},{8,4},{10,6},{12,8},{14,10},{16,12},{18,14},{20,16},{2... | collective-permute-start | bytes 393224 | tf_op jit(solution)/shard_map/ppermute | solution.py:370
  140.7 1.9 %collective-permute-start.15 = (bf16[64,1024]{1,0:T(8,128)(2,1)S(1)}, bf16[64,1024]{1,0:T(8,128)(2,1)S(1)}, u32[]{:S(2)}, u32[]{:S(2)}) collective-permute-start(bf16[64,1024]{1,0:T(8,128)(2,1)S(1)} %copy-done.12), channel_id=1, source_target_pairs={{0,4},{2,6},{4,8},{6,10},{8,12},{10,14},{12,16},{14,18},{16,20},{1... | collective-permute-start | bytes 393224 | tf_op jit(solution)/shard_map/ppermute | solution.py:370
  142.6 1.5 collective-permute-done.14.refs_2_
  144.1 7.6 %collective-permute-done.15.refs_4_ = bf16[64,1024]{1,0:T(8,128)(2,1)S(1)} collective-permute-done((bf16[64,1024]{1,0:T(8,128)(2,1)S(1)}, bf16[64,1024]{1,0:T(8,128)(2,1)S(1)}, u32[]{:S(2)}, u32[]{:S(2)}) %collective-permute-start.15) | collective-permute-done | bytes 131104 | tf_op jit(solution)/shard_map/ppermute | solution.py:370
  151.8 0.1 reduce_sum.35
  151.8 0.7 broadcast_in_dim.27
  152.6 4.2 %all-to-all-start.5 = ((f32[64,8,128]{2,1,0:T(8,128)}), f32[64,8,128]{2,1,0:T(8,128)S(1)}, u32[]{:S(2)}, u32[]{:S(2)}) async-start(f32[64,8,128]{2,1,0:T(8,128)} %broadcast_in_dim.27), calls=%async_computation.5 | async-start | bytes 524288 | tf_op jit(solution)/shard_map/all_to_all | solution.py:361
  156.8 4.0 %collective-permute-start.16 = (bf16[128,1024]{1,0:T(8,128)(2,1)S(1)}, bf16[128,1024]{1,0:T(8,128)(2,1)S(1)}, u32[]{:S(2)}, u32[]{:S(2)}) collective-permute-start(bf16[128,1024]{1,0:T(8,128)(2,1)S(1)} %get-tuple-element.66.refs_0_), channel_id=1, source_target_pairs={{2,0},{4,2},{6,4},{8,6},{10,8},{12,10},{14,12},{16,14},{18,16},{20... | collective-permute-start | bytes 786440 | tf_op jit(solution)/shard_map/ppermute | solution.py:370
  160.8 1.9 %collective-permute-start.17 = (bf16[64,1024]{1,0:T(8,128)(2,1)S(1)}, bf16[64,1024]{1,0:T(8,128)(2,1)S(1)}, u32[]{:S(2)}, u32[]{:S(2)}) collective-permute-start(bf16[64,1024]{1,0:T(8,128)(2,1)S(1)} %copy-done.12), channel_id=1, source_target_pairs={{0,2},{2,4},{4,6},{6,8},{8,10},{10,12},{12,14},{14,16},{16,18},{18... | collective-permute-start | bytes 393224 | tf_op jit(solution)/shard_map/ppermute | solution.py:370
  162.7 8.6 %collective-permute-done.17.refs_3_ = bf16[64,1024]{1,0:T(8,128)(2,1)S(1)} collective-permute-done((bf16[64,1024]{1,0:T(8,128)(2,1)S(1)}, bf16[64,1024]{1,0:T(8,128)(2,1)S(1)}, u32[]{:S(2)}, u32[]{:S(2)}) %collective-permute-start.17) | collective-permute-done | bytes 131104 | tf_op jit(solution)/shard_map/ppermute | solution.py:370
  171.3 6.8 %input_conv.1 = bf16[128,1024]{1,0:T(8,128)(2,1)} custom-call(s32[8]{0:T(128)S(1)} %compare_select_fusion.4.place_ref, s32[256]{0:T(256)S(1)} %copy-done.6, bf16[128,1024]{1,0:T(8,128)(2,1)S(1)} %get-tuple-element.66.refs_0_, bf16[128,1024]{1,0:T(8,128)(2,1)S(1)} %collective-permute-done.16.refs_1_, bf16[64,1024]{1,0:T(8,128)(2,1)S(1)} %collective-permute-done.14.refs_2_, ...), custom_call_target="tpu_custom_call" | custom-call | flops 1048576 | bytes 1048576 | tf_op jit(solution)/shard_map/input_conv/pallas_call | solution.py:340
  178.1 1.5 collective-permute-done.18
  179.7 0.8 pad_maximum_fusion
  (43 shorter events, 0.2 us)
Async XLA Ops:
  0.6 16.4 %copy-start.1 = (bf16[3,2048,128]{2,1,0:T(8,128)(2,1)S(1)}, bf16[3,2048,128]{2,1,0:T(8,128)(2,1)}, u32[]{:S(2)}) copy-start(bf16[3,2048,128]{2,1,0:T(8,128)(2,1)} %w_own.1) | copy-start | bytes 4718596
  2.4 10.9 %collective-permute-start = (bf16[128,256]{1,0:T(8,128)(2,1)}, bf16[128,256]{1,0:T(8,128)(2,1)S(1)}, u32[]{:S(2)}, u32[]{:S(2)}) collective-permute-start(bf16[128,256]{1,0:T(8,128)(2,1)} %get-tuple-element.38), channel_id=1, source_target_pairs={{0,128},{128,0},{1,129},{129,1},{2,130},{130,2},{3,131},{131,3},{4... | collective-permute-start | bytes 196616 | tf_op jit(solution)/shard_map/ppermute | solution.py:365
  3.3 14.7 %copy-start.6 = (s32[256]{0:T(256)S(1)}, s32[256]{0:T(256)}, u32[]{:S(2)}) copy-start(s32[256]{0:T(256)} %order_ref.7) | copy-start | bytes 3076
  3.3 27.5 %all-to-all-start = ((bf16[8,128,256]{2,1,0:T(8,128)(2,1)}), bf16[8,128,256]{2,1,0:T(8,128)(2,1)S(1)}, u32[]{:S(2)}, u32[]{:S(2)}) async-start(bf16[8,128,256]{2,1,0:T(8,128)(2,1)} %get-tuple-element.37), calls=%async_computation | async-start | bytes 1048576 | tf_op jit(solution)/shard_map/all_to_all | solution.py:388
  13.4 15.2 %copy-start.2 = (bf16[128,1024]{1,0:T(8,128)(2,1)S(1)}, bf16[128,1024]{1,0:T(8,128)(2,1)}, u32[]{:S(2)}) copy-start(bf16[128,1024]{1,0:T(8,128)(2,1)} %refs_0_.1) | copy-start | bytes 786436
  14.0 8.7 %collective-permute-start.1 = (bf16[256,256]{1,0:T(8,128)(2,1)}, bf16[256,256]{1,0:T(8,128)(2,1)S(1)}, u32[]{:S(2)}, u32[]{:S(2)}) collective-permute-start(bf16[256,256]{1,0:T(8,128)(2,1)} %get-tuple-element.84), channel_id=1, source_target_pairs={{32,0},{64,32},{96,64},{0,96},{33,1},{65,33},{97,65},{1,97},{34,2}... | collective-permute-start | bytes 393224 | tf_op jit(solution)/shard_map/ppermute | solution.py:374
  18.1 8.3 %collective-permute-start.2 = (bf16[256,256]{1,0:T(8,128)(2,1)}, bf16[256,256]{1,0:T(8,128)(2,1)}, u32[]{:S(2)}, u32[]{:S(2)}) collective-permute-start(bf16[256,256]{1,0:T(8,128)(2,1)} %get-tuple-element.84), channel_id=1, source_target_pairs={{64,0},{96,32},{0,64},{32,96},{65,1},{97,33},{1,65},{33,97},{66,2}... | collective-permute-start | bytes 393224 | tf_op jit(solution)/shard_map/ppermute | solution.py:374
  20.6 7.3 %collective-permute-start.3 = (bf16[256,256]{1,0:T(8,128)(2,1)}, bf16[256,256]{1,0:T(8,128)(2,1)S(1)}, u32[]{:S(2)}, u32[]{:S(2)}) collective-permute-start(bf16[256,256]{1,0:T(8,128)(2,1)} %get-tuple-element.84), channel_id=1, source_target_pairs={{96,0},{0,32},{32,64},{64,96},{97,1},{1,33},{33,65},{65,97},{98,2}... | collective-permute-start | bytes 393224 | tf_op jit(solution)/shard_map/ppermute | solution.py:374
  28.6 2.1 %collective-permute-start.4 = (bf16[1024,256]{1,0:T(8,128)(2,1)}, bf16[1024,256]{1,0:T(8,128)(2,1)S(1)}, u32[]{:S(2)}, u32[]{:S(2)}) collective-permute-start(bf16[1024,256]{1,0:T(8,128)(2,1)} %get-tuple-element.76), channel_id=1, source_target_pairs={{0,2},{2,0},{1,3},{3,1},{4,6},{6,4},{5,7},{7,5},{8,10},{10,8},{9,1... | collective-permute-start | bytes 1572872 | tf_op jit(solution)/shard_map/ppermute | solution.py:365
  29.3 21.8 %collective-permute-start.5 = (bf16[3,1024,128]{2,1,0:T(8,128)(2,1)}, bf16[3,1024,128]{2,1,0:T(8,128)(2,1)}, u32[]{:S(2)}, u32[]{:S(2)}) collective-permute-start(bf16[3,1024,128]{2,1,0:T(8,128)(2,1)} %constant_dynamic-slice_fusion.2), channel_id=1, source_target_pairs={{0,1},{1,0},{2,3},{3,2},{4,5},{5,4},{6,7},{7,6},{8,9},{9,8},{10,11... | collective-permute-start | bytes 2359304 | tf_op jit(solution)/shard_map/ppermute | solution.py:365
  30.8 7.2 %copy-start.4 = (bf16[2048,256]{1,0:T(8,128)(2,1)}, bf16[2048,256]{1,0:T(8,128)(2,1)S(1)}, u32[]{:S(2)}) copy-start(bf16[2048,256]{1,0:T(8,128)(2,1)S(1)} %constant_dynamic-update-slice_fusion.7.k_ref.v_ref) | copy-start | bytes 3145732
  37.9 15.3 %all-to-all-start.1 = ((f32[8,2,1024]{2,1,0:T(2,128)}), f32[8,2,1024]{2,1,0:T(2,128)S(1)}, u32[]{:S(2)}, u32[]{:S(2)}) async-start(f32[8,2,1024]{2,1,0:T(2,128)} %attention_stats.1), calls=%async_computation.1 | async-start | bytes 131072 | tf_op jit(solution)/shard_map/all_to_all | solution.py:404
  53.2 1.2 copy-start.5
  63.0 0.7 copy-start.3
  63.7 14.9 %collective-permute-start.6 = (f32[1024,256]{1,0:T(8,128)}, f32[1024,256]{1,0:T(8,128)}, u32[]{:S(2)}, u32[]{:S(2)}) collective-permute-start(f32[1024,256]{1,0:T(8,128)} %get-tuple-element.46), channel_id=1, source_target_pairs={{0,2},{2,0},{1,3},{3,1},{4,6},{6,4},{5,7},{7,5},{8,10},{10,8},{9,1... | collective-permute-start | bytes 3145736 | tf_op jit(solution)/shard_map/ppermute | solution.py:365
  63.7 18.3 %all-to-all-start.2 = ((bf16[8,128,128]{2,1,0:T(8,128)(2,1)}), bf16[8,128,128]{2,1,0:T(8,128)(2,1)S(1)}, u32[]{:S(2)}, u32[]{:S(2)}) async-start(bf16[8,128,128]{2,1,0:T(8,128)(2,1)} %bitcast.20), calls=%async_computation.2 | async-start | bytes 524288 | tf_op jit(solution)/shard_map/all_to_all | solution.py:410
  68.5 13.5 %collective-permute-start.7 = (bf16[64,1024]{1,0:T(8,128)(2,1)}, bf16[64,1024]{1,0:T(8,128)(2,1)S(1)}, u32[]{:S(2)}, u32[]{:S(2)}) collective-permute-start(bf16[64,1024]{1,0:T(8,128)(2,1)} %get-tuple-element.47), channel_id=1, source_target_pairs={{0,4},{2,6},{4,8},{6,10},{8,12},{10,14},{12,16},{14,18},{16,20},{1... | collective-permute-start | bytes 393224 | tf_op jit(solution)/shard_map/ppermute | solution.py:370
  72.4 9.5 %collective-permute-start.8 = (bf16[64,1024]{1,0:T(8,128)(2,1)}, bf16[64,1024]{1,0:T(8,128)(2,1)S(1)}, u32[]{:S(2)}, u32[]{:S(2)}) collective-permute-start(bf16[64,1024]{1,0:T(8,128)(2,1)} %get-tuple-element.48), channel_id=1, source_target_pairs={{4,0},{6,2},{8,4},{10,6},{12,8},{14,10},{16,12},{18,14},{20,16},{2... | collective-permute-start | bytes 393224 | tf_op jit(solution)/shard_map/ppermute | solution.py:370
  82.0 31.6 %copy-start.7 = (bf16[64,1024]{1,0:T(8,128)(2,1)}, bf16[64,1024]{1,0:T(8,128)(2,1)S(1)}, u32[]{:S(2)}) copy-start(bf16[64,1024]{1,0:T(8,128)(2,1)S(1)} %collective-permute-done.7.refs_1_) | copy-start | bytes 393220
  82.0 31.6 %copy-start.9 = (bf16[64,1024]{1,0:T(8,128)(2,1)}, bf16[64,1024]{1,0:T(8,128)(2,1)S(1)}, u32[]{:S(2)}) copy-start(bf16[64,1024]{1,0:T(8,128)(2,1)S(1)} %collective-permute-done.8.refs_4_) | copy-start | bytes 393220
  82.0 0.8 copy-start.15
  82.7 22.9 %all-to-all-start.3 = ((bf16[8,128,256]{2,1,0:T(8,128)(2,1)}), bf16[8,128,256]{2,1,0:T(8,128)(2,1)S(1)}, u32[]{:S(2)}, u32[]{:S(2)}) async-start(bf16[8,128,256]{2,1,0:T(8,128)(2,1)} %bitcast.21), calls=%async_computation.3 | async-start | bytes 1048576 | tf_op jit(solution)/shard_map/all_to_all | solution.py:413
  86.4 11.1 %collective-permute-start.10 = (bf16[128,1024]{1,0:T(8,128)(2,1)S(1)}, bf16[128,1024]{1,0:T(8,128)(2,1)S(1)}, u32[]{:S(2)}, u32[]{:S(2)}) collective-permute-start(bf16[128,1024]{1,0:T(8,128)(2,1)S(1)} %copy-done.2), channel_id=1, source_target_pairs={{2,0},{4,2},{6,4},{8,6},{10,8},{12,10},{14,12},{16,14},{18,16},{20... | collective-permute-start | bytes 786440 | tf_op jit(solution)/shard_map/ppermute | solution.py:370
  93.6 12.0 %collective-permute-start.9 = (bf16[128,1024]{1,0:T(8,128)(2,1)S(1)}, bf16[128,1024]{1,0:T(8,128)(2,1)S(1)}, u32[]{:S(2)}, u32[]{:S(2)}) collective-permute-start(bf16[128,1024]{1,0:T(8,128)(2,1)S(1)} %copy-done.2), channel_id=1, source_target_pairs={{0,2},{2,4},{4,6},{6,8},{8,10},{10,12},{12,14},{14,16},{16,18},{18... | collective-permute-start | bytes 786440 | tf_op jit(solution)/shard_map/ppermute | solution.py:370
  105.7 7.9 %collective-permute-start.12 = (bf16[128,256]{1,0:T(8,128)(2,1)S(1)}, bf16[128,256]{1,0:T(8,128)(2,1)S(1)}, u32[]{:S(2)}, u32[]{:S(2)}) collective-permute-start(bf16[128,256]{1,0:T(8,128)(2,1)S(1)} %reduce_sum.34.kv_own), channel_id=1, source_target_pairs={{0,1},{1,0},{2,3},{3,2},{4,5},{5,4},{6,7},{7,6},{8,9},{9,8},{10,11... | collective-permute-start | bytes 196616 | tf_op jit(solution)/shard_map/ppermute | solution.py:365
  107.9 5.7 %collective-permute-start.11 = (bf16[128,128]{1,0:T(8,128)(2,1)S(1)}, bf16[128,128]{1,0:T(8,128)(2,1)S(1)}, u32[]{:S(2)}, u32[]{:S(2)}) collective-permute-start(bf16[128,128]{1,0:T(8,128)(2,1)S(1)} %reduce_sum.33.q_own), channel_id=1, source_target_pairs={{0,1},{1,0},{2,3},{3,2},{4,5},{5,4},{6,7},{7,6},{8,9},{9,8},{10,11... | collective-permute-start | bytes 98312 | tf_op jit(solution)/shard_map/ppermute | solution.py:365
  113.6 0.9 copy-start.8
  114.5 0.9 copy-start.10
  126.3 0.7 copy-start.11
  127.0 0.7 copy-start.13
  127.6 43.7 %copy-start = (f32[1024,128]{1,0:T(8,128)S(1)}, f32[1024,128]{1,0:T(8,128)}, u32[]{:S(2)}) copy-start(f32[1024,128]{1,0:T(8,128)} %refs_5_.1) | copy-start | bytes 1572868
  127.6 6.6 %copy-start.14 = (bf16[64,1024]{1,0:T(8,128)(2,1)S(1)}, bf16[64,1024]{1,0:T(8,128)(2,1)}, u32[]{:S(2)}) copy-start(bf16[64,1024]{1,0:T(8,128)(2,1)} %copy-done.13) | copy-start | bytes 393220
  127.6 13.0 %copy-start.12 = (bf16[64,1024]{1,0:T(8,128)(2,1)S(1)}, bf16[64,1024]{1,0:T(8,128)(2,1)}, u32[]{:S(2)}) copy-start(bf16[64,1024]{1,0:T(8,128)(2,1)} %copy-done.11) | copy-start | bytes 393220
  127.7 1.6 collective-permute-start.13
  130.0 21.8 %all-to-all-start.4 = ((f32[64,8,128]{2,1,0:T(8,128)}), f32[64,8,128]{2,1,0:T(8,128)S(1)}, u32[]{:S(2)}, u32[]{:S(2)}) async-start(f32[64,8,128]{2,1,0:T(8,128)} %fusion), calls=%async_computation.4 | async-start | bytes 524288 | tf_op jit(solution)/shard_map/all_to_all | solution.py:428
  134.2 9.9 %collective-permute-start.14 = (bf16[64,1024]{1,0:T(8,128)(2,1)S(1)}, bf16[64,1024]{1,0:T(8,128)(2,1)S(1)}, u32[]{:S(2)}, u32[]{:S(2)}) collective-permute-start(bf16[64,1024]{1,0:T(8,128)(2,1)S(1)} %copy-done.14), channel_id=1, source_target_pairs={{4,0},{6,2},{8,4},{10,6},{12,8},{14,10},{16,12},{18,14},{20,16},{2... | collective-permute-start | bytes 393224 | tf_op jit(solution)/shard_map/ppermute | solution.py:370
  140.7 11.1 %collective-permute-start.15 = (bf16[64,1024]{1,0:T(8,128)(2,1)S(1)}, bf16[64,1024]{1,0:T(8,128)(2,1)S(1)}, u32[]{:S(2)}, u32[]{:S(2)}) collective-permute-start(bf16[64,1024]{1,0:T(8,128)(2,1)S(1)} %copy-done.12), channel_id=1, source_target_pairs={{0,4},{2,6},{4,8},{6,10},{8,12},{10,14},{12,16},{14,18},{16,20},{1... | collective-permute-start | bytes 393224 | tf_op jit(solution)/shard_map/ppermute | solution.py:370
  152.6 25.5 %all-to-all-start.5 = ((f32[64,8,128]{2,1,0:T(8,128)}), f32[64,8,128]{2,1,0:T(8,128)S(1)}, u32[]{:S(2)}, u32[]{:S(2)}) async-start(f32[64,8,128]{2,1,0:T(8,128)} %broadcast_in_dim.27), calls=%async_computation.5 | async-start | bytes 524288 | tf_op jit(solution)/shard_map/all_to_all | solution.py:361
  156.8 14.5 %collective-permute-start.16 = (bf16[128,1024]{1,0:T(8,128)(2,1)S(1)}, bf16[128,1024]{1,0:T(8,128)(2,1)S(1)}, u32[]{:S(2)}, u32[]{:S(2)}) collective-permute-start(bf16[128,1024]{1,0:T(8,128)(2,1)S(1)} %get-tuple-element.66.refs_0_), channel_id=1, source_target_pairs={{2,0},{4,2},{6,4},{8,6},{10,8},{12,10},{14,12},{16,14},{18,16},{20... | collective-permute-start | bytes 786440 | tf_op jit(solution)/shard_map/ppermute | solution.py:370
  160.8 10.5 %collective-permute-start.17 = (bf16[64,1024]{1,0:T(8,128)(2,1)S(1)}, bf16[64,1024]{1,0:T(8,128)(2,1)S(1)}, u32[]{:S(2)}, u32[]{:S(2)}) collective-permute-start(bf16[64,1024]{1,0:T(8,128)(2,1)S(1)} %copy-done.12), channel_id=1, source_target_pairs={{0,2},{2,4},{4,6},{6,8},{8,10},{10,12},{12,14},{14,16},{16,18},{18... | collective-permute-start | bytes 393224 | tf_op jit(solution)/shard_map/ppermute | solution.py:370
  178.1 1.5 collective-permute-start.18

commit v3 on v2

--- a/solution.py
+++ b/solution.py
@@ -208,18 +208,23 @@
     stack[at] = jnp.zeros((BLK, LANES), F32)
 
 
-def low_high(place_ref, order_ref, distance):
-    at = ((place_ref[0] * Y + place_ref[1]) * Z + place_ref[2]) * CORE + place_ref[3] + distance
+def device_at(place_ref):
+    return ((place_ref[0] * Y + place_ref[1]) * Z + place_ref[2]) * CORE + place_ref[3]
+
+
+def blocks_at(order_ref, at):
     inside = jnp.logical_and(at >= 0, at < XL * Y * Z * CORE)
     at = jnp.where(inside, at, 0)
-    first, second = order_ref[2 * at], order_ref[2 * at + 1]
-    low = jnp.where(inside, jnp.minimum(first, second), -1000)
-    high = jnp.where(inside, jnp.maximum(first, second), -1000)
-    return low, high
+    return [jnp.where(inside, order_ref[2 * at + slot], -1000) for slot in range(2)]
+
+
+def low_high(order_ref, at):
+    first, second = blocks_at(order_ref, at)
+    return [jnp.minimum(first, second), jnp.maximum(first, second)]
 
 
 def extend(place_ref, order_ref, have, shift, cand, ext):
-    at = ((place_ref[0] * Y + place_ref[1]) * Z + place_ref[2]) * CORE + place_ref[3]
+    at = device_at(place_ref)
     for slot in range(2):
         own = order_ref[2 * at + slot]
         for part in range(3):
@@ -233,32 +238,26 @@
     n_in, place_ref, order_ref, q_own, kv_own, q_other, kv_other, w_own, w_other, *refs
 ):
     ins = refs[:n_in]
-    pair_ref, low_ref, high_ref, filt_ref, cand, grad, ext, lag = refs[n_in:]
+    pair_ref, high_ref, filt_ref, cand, grad, ext, lag = refs[n_in:]
     cg = jnp.zeros((ROWS, LANES), F32)
     for q_ref, kv_ref, w_ref in ((q_own, kv_own, w_own), (q_other, kv_other, w_other)):
         cg = cg + nt(q_ref[...], w_ref[0])
         cg = cg + nt(kv_ref[:, :HD], w_ref[1])
         cg = cg + nt(kv_ref[:, HD:], w_ref[2])
     grad[...] = cg.astype(BF).astype(F32)
-    device = ((place_ref[0] * Y + place_ref[1]) * Z + place_ref[2]) * CORE + place_ref[3]
+    device = device_at(place_ref)
+    partner = device + 1 - 2 * place_ref[3]
     first, second = order_ref[2 * device], order_ref[2 * device + 1]
     swapped = (first > second).astype(jnp.int32)
     low = grad[pl.ds(pl.multiple_of(swapped * BLK, BLK), BLK), :].astype(BF)
     high = grad[pl.ds(pl.multiple_of((1 - swapped) * BLK, BLK), BLK), :].astype(BF)
-    low_ref[...] = low
     high_ref[...] = high
     pair_ref[:BLK, :] = low
     pair_ref[BLK:, :] = high
     stack_blocks(ins, cand)
-    near = [low_high(place_ref, order_ref, d) for d in (-2, -1, 1, 2)]
-    device_of = lambda d: 2 * jnp.clip(device + d, 0, XL * Y * Z * CORE - 1)
-    inside = lambda d, block: jnp.where(
-        jnp.logical_and(device + d >= 0, device + d < XL * Y * Z * CORE), block, -1000
-    )
-    have = [first, second, near[0][0]]
-    have += [inside(-1, order_ref[device_of(-1) + s]) for s in range(2)]
-    have += [inside(1, order_ref[device_of(1) + s]) for s in range(2)]
-    have += [near[3][1]]
+    have = [first, second] + blocks_at(order_ref, partner)
+    have += blocks_at(order_ref, device - 2) + blocks_at(order_ref, partner - 2)
+    have += low_high(order_ref, device + 2)[1:] + low_high(order_ref, partner + 2)[1:]
     extend(place_ref, order_ref, have, -2, cand, ext)
     for r in range(8):
         for slot in range(2):
@@ -270,8 +269,12 @@
                 for m in range(1, BLK // 8):
                     total = total + rows[m] * shifted[15 - a + m]
                 j = 8 * a + r
-                lag[j] = total if slot == 0 else lag[j] + total
-    filt_ref[0] = jnp.sum(lag[...], axis=1).T
+                here = slice(8 * j, 8 * j + 8)
+                lag[here, :] = total if slot == 0 else lag[here, :] + total
+    taps = lag[pl.ds(0, TAPS, stride=8), :]
+    for s in range(1, 8):
+        taps = taps + lag[pl.ds(s, TAPS, stride=8), :]
+    filt_ref[0] = taps.T
 
 
 def project_and_filter(place, order, q_own, kv_own, q_other, kv_other, weight, w_other, ins):
@@ -294,17 +297,16 @@
                 pl.BlockSpec((3, LANES, HD), lambda i, p, o: (0, i, 0)),
             ]
             + [column(a) for a in ins],
-            out_specs=[block(ROWS), block(BLK), block(BLK), pl.BlockSpec((1, LANES, TAPS), which)],
+            out_specs=[block(ROWS), block(BLK), pl.BlockSpec((1, LANES, TAPS), which)],
             scratch_shapes=[
                 pltpu.VMEM((blocks, BLK, LANES), F32),
                 pltpu.VMEM((ROWS, LANES), F32),
                 pltpu.VMEM((2, 3 * BLK, LANES), F32),
-                pltpu.VMEM((TAPS, 8, LANES), F32),
+                pltpu.VMEM((8 * TAPS, LANES), F32),
             ],
         ),
         out_shape=[
             jax.ShapeDtypeStruct((ROWS, channels), BF),
-            jax.ShapeDtypeStruct((BLK, channels), BF),
             jax.ShapeDtypeStruct((BLK, channels), BF),
             jax.ShapeDtypeStruct((2, channels // 2, TAPS), F32),
         ],
@@ -319,8 +321,11 @@
     filter_ref, out_ref, cand, ext, taps_ref = refs[n_grad:]
     taps_ref[...] = filter_ref[...].T
     stack_blocks(grads, cand)
-    near = [low_high(place_ref, order_ref, d) for d in (0, 1, 2, -1, -2)]
-    have = [near[0][0], near[0][1], near[1][0], near[1][1], near[2][0], near[3][1], near[4][1]]
+    device = device_at(place_ref)
+    partner = device + 1 - 2 * place_ref[3]
+    have = low_high(order_ref, device) + low_high(order_ref, partner)
+    have += low_high(order_ref, device + 2) + low_high(order_ref, partner + 2)
+    have += low_high(order_ref, device - 2)[1:] + low_high(order_ref, partner - 2)[1:]
     extend(place_ref, order_ref, have, 0, cand, ext)
     for slot in range(2):
         acc = [jnp.zeros((8, LANES), F32) for _ in range(BLK // 8)]
@@ -394,10 +399,9 @@
     device = ((coords[0] * Y + coords[1]) * Z + coords[2]) * CORE + core
     ids = lax.dynamic_slice_in_dim(block_order, device * 2, 2, 0)
     swapped = (ids[0] > ids[1]).astype(jnp.int32)
-    x_low = lax.dynamic_slice_in_dim(conv_input, swapped * BLK, BLK, 0)
     x_high = lax.dynamic_slice_in_dim(conv_input, (1 - swapped) * BLK, BLK, 0)
     w_sent = lax.dynamic_slice_in_dim(qkv_weight, (1 - head) * channels, channels, 1)
-    w_sent, x_low, x_high, kv_xl = lax.optimization_barrier((w_sent, x_low, x_high, kv_xl))
+    w_sent, x_high, kv_xl = lax.optimization_barrier((w_sent, x_high, kv_xl))
     w_other = swap(w_sent, "head")
 
     stats = attention_stats(place, block_order, qg, kv)
@@ -405,33 +409,34 @@
     stats, w_other = lax.optimization_barrier((stats, w_other))
     dq, dkv_own, dkv_other = attention_grads(place, block_order, qg, kv, stats)
 
-    dq, x_low, x_high = lax.optimization_barrier((dq, x_low, x_high))
-    moved_far = [from_ctx(x_low, -2), from_ctx(x_high, 2)]
+    dq, x_pair, x_high = lax.optimization_barrier((dq, conv_input, x_high))
+    x_far = [from_ctx(x_pair, -2), from_ctx(x_high, 2)]
     dq_parts = lax.all_to_all(dq.reshape(Z, ROWS, HD), "z", 0, 0, tiled=True)
     dkv = (dkv_own + swap(dkv_other, "core")).astype(BF).reshape(XL * Y, ROWS, 2 * HD)
-    dq_parts, dkv, x_near, moved_far = lax.optimization_barrier((dq_parts, dkv, conv_input, moved_far))
+    dq_parts, dkv, x_far, x_pair = lax.optimization_barrier((dq_parts, dkv, x_far, x_pair))
     dkv_parts = lax.all_to_all(dkv, ("xl", "y"), 0, 0, tiled=True)
-    moved_near = [from_ctx(x_near, -1), from_ctx(x_near, 1)]
-    dkv_parts, moved_near = lax.optimization_barrier((dkv_parts, moved_near))
+    x_swapped = [swap(x, "core") for x in [x_pair] + x_far]
+    dkv_parts, x_swapped = lax.optimization_barrier((dkv_parts, x_swapped))
     query_grad = jnp.sum(dq_parts.astype(F32), axis=0).astype(BF)
     q_other = swap(query_grad, "head")
     kv_grad = jnp.sum(dkv_parts.astype(F32), axis=0).astype(BF)
     kv_other = swap(kv_grad, "head")
 
-    ins = [conv_input, moved_far[0], *moved_near, moved_far[1]]
-    g_pair, g_low, g_high, filter_part = project_and_filter(
+    ins = [conv_input, x_swapped[0], x_far[0], x_swapped[1], x_far[1], x_swapped[2]]
+    g_pair, g_high, filter_part = project_and_filter(
         place, block_order, query_grad, kv_grad, q_other, kv_other, qkv_weight, w_other, ins
     )
 
     mine_sum = filter_part[0] + swap(filter_part[1], "core")
-    far = [from_ctx(g_low, 2), from_ctx(g_high, -2)]
+    far = [from_ctx(g_pair, 2), from_ctx(g_high, -2)]
+    g_partner = swap(g_pair, "core")
     parts = lax.all_to_all(
         mine_sum.reshape(chips, channels // 2 // chips, TAPS), ("xl", "y", "z"), 0, 0, tiled=True
     )
-    parts, far, g_pair, g_high = lax.optimization_barrier((parts, far, g_pair, g_high))
+    parts, far, g_partner = lax.optimization_barrier((parts, far, g_partner))
     total = jnp.sum(parts, axis=0)
-    total, g_pair, g_high = lax.optimization_barrier((total, g_pair, g_high))
-    grads = [g_pair, from_ctx(g_pair, 1), far[0], from_ctx(g_high, -1), far[1]]
+    total, far = lax.optimization_barrier((total, far))
+    grads = [g_pair, g_partner, far[0], swap(far[0], "core"), far[1], swap(far[1], "core")]
     half = to_all(total, ("xl", "y", "z"), chips)
     input_grad = input_conv(place, block_order, grads, conv_filter)
     half, input_grad = lax.optimization_barrier((half, input_grad))

time: 183 us -> 169 us (0.923)
  starting transfers between devices: 76.5 us -> 69.1 us
  local copies, waits for them, and re-layouts: 14 us -> 9.39 us
  waiting for transfers between devices: 47.8 us -> 45.9 us
    ppermute x8 -> x4, waiting for transfers between devices: 29 us -> 14.1 us  [from_ctx(): lax.ppermute(x, CTX, [(i + distance, i) for i in range(n) if 0 <= i + dis...]
    ppermute x8 -> x4, starting transfers between devices: 33.5 us -> 18.7 us  [from_ctx(): lax.ppermute(x, CTX, [(i + distance, i) for i in range(n) if 0 <= i + dis...]
    all_to_all x1, waiting for transfers between devices: 0.01 us -> 5.78 us  [local(): dkv_parts = lax.all_to_all(dkv, ('xl', 'y'), 0, 0, tiled=True)]
    all_to_all x1, starting transfers between devices: 4.19 us -> 9.34 us  [local(): lax.all_to_all(mine_sum.reshape(chips, channels // 2 // chips, TAPS), ('x...]
    unnamed x36 -> x16, local copies, waits for them, and re-layouts: 10.2 us -> 5.67 us
    all_to_all x1, waiting for transfers between devices: 0.01 us -> 4.39 us  [to_all(): lax.all_to_all(jnp.broadcast_to(x[None], (count,) + x.shape), axes, 0, 0,...]
    ppermute x8 -> x14, waiting for transfers between devices: 12.6 us -> 15.5 us  [swap(): return lax.ppermute(x, axis, [(0, 1), (1, 0)])]
    ppermute x8 -> x14, starting transfers between devices: 5.92 us -> 7.3 us  [swap(): return lax.ppermute(x, axis, [(0, 1), (1, 0)])]
  transfers between devices with their start and end apart: 25 -> 27, of which waited for: 14 -> 15; matrix products, arithmetic and copies ran while one was open for 6% -> 6% of each run, Pallas kernels for 8% -> 8%
where the time goes in v3:
time: 169 us; the launch traced here: 167 us
  starting transfers between devices  69.1 us (41%)
  waiting for transfers between devices  45.9 us (27%)
  Pallas kernels  35.3 us (21%)
  local copies, waits for them, and re-layouts  9.39 us (6%)
  other arithmetic  4.97 us (3%)
  between operations  2.13 us (1%)
    ppermute x4, starting transfers between devices, from_ctx(): lax.ppermute(x, CTX, [(i + distance, i) for i in range(n) if 0 <= i + dis...  18.7 us
    ppermute x14, waiting for transfers between devices, swap(): return lax.ppermute(x, axis, [(0, 1), (1, 0)])  15.5 us
    ppermute x4, waiting for transfers between devices, from_ctx(): lax.ppermute(x, CTX, [(i + distance, i) for i in range(n) if 0 <= i + dis...  14.1 us
    pallas_call x1, Pallas kernels, project_and_filter(): pl.pallas_call(functools.partial(filter_kernel, len(ins)), grid_spec=pltp...  10.8 us
    all_to_all x1, starting transfers between devices, local(): lax.all_to_all(mine_sum.reshape(chips, channels // 2 // chips, TAPS), ('x...  9.34 us
    pallas_call x1, Pallas kernels, attention_grads(): pl.pallas_call(grads_kernel, grid_spec=pltpu.PrefetchScalarGridSpec(num_s...  8.62 us
    all_to_all x1, starting transfers between devices, local(): qg = lax.all_to_all(qg, 'z', 0, 0, tiled=True).reshape(NQ, 2 * HD)  8.6 us
    ppermute x14, starting transfers between devices, swap(): return lax.ppermute(x, axis, [(0, 1), (1, 0)])  7.3 us
  transfers between devices with their start and end apart: 27, of which 15 were waited for; matrix products, arithmetic and copies ran while one was open for 6% of the time, Pallas kernels for 8%

profile of v3, /device:TPU:6, one launch (start us, length us, event | category | flops | bytes accessed | tf_op | source)
XLA Modules:
  0.0 166.8 jit_solution(2432280241799588850)
XLA Ops:
  0.6 1.8 %pack.1 = (bf16[8,128,256]{2,1,0:T(8,128)(2,1)}, bf16[128,256]{1,0:T(8,128)(2,1)}) custom-call(bf16[128,128]{1,0:T(8,128)(2,1)} %q_ref.1, bf16[128,128]{1,0:T(8,128)(2,1)} %g_ref.1, bf16[128,128]{1,0:T(8,128)(2,1)} %k_ref.1, bf16[128,128]{1,0:T(8,128)(2,1)} %v_ref.1), custom_call_target="tpu_custom_call" | custom-call | tf_op jit(solution)/shard_map/pack/pallas_call | solution.py:195
  2.4 0.8 collective-permute-start
  3.3 8.6 %all-to-all-start = ((bf16[8,128,256]{2,1,0:T(8,128)(2,1)}), bf16[8,128,256]{2,1,0:T(8,128)(2,1)S(1)}, u32[]{:S(2)}, u32[]{:S(2)}) async-start(bf16[8,128,256]{2,1,0:T(8,128)(2,1)} %get-tuple-element.35), calls=%async_computation | async-start | bytes 1048576 | tf_op jit(solution)/shard_map/all_to_all | solution.py:393
  11.9 1.5 constant_dynamic-update-slice_fusion.6
  13.4 0.0 collective-permute-done
  13.4 0.7 constant_dynamic-update-slice_fusion.5
  14.0 3.0 %collective-permute-start.1 = (bf16[256,256]{1,0:T(8,128)(2,1)}, bf16[256,256]{1,0:T(8,128)(2,1)S(1)}, u32[]{:S(2)}, u32[]{:S(2)}) collective-permute-start(bf16[256,256]{1,0:T(8,128)(2,1)} %get-tuple-element.78), channel_id=1, source_target_pairs={{32,0},{64,32},{96,64},{0,96},{33,1},{65,33},{97,65},{1,97},{34,2}... | collective-permute-start | bytes 393224 | tf_op jit(solution)/shard_map/ppermute | solution.py:379
  17.1 0.9 constant_dynamic-slice_fusion.1
  18.0 0.1 dynamic_slice.10
  18.1 0.7 collective-permute-start.2
  18.7 0.6 fusion.1
  20.6 1.0 collective-permute-start.3
  21.7 1.0 collective-permute-done.1
  22.7 0.7 constant_dynamic-update-slice_fusion.4
  23.4 2.9 %collective-permute-done.2 = bf16[256,256]{1,0:T(8,128)(2,1)} collective-permute-done((bf16[256,256]{1,0:T(8,128)(2,1)}, bf16[256,256]{1,0:T(8,128)(2,1)}, u32[]{:S(2)}, u32[]{:S(2)}) %collective-permute-start.2) | collective-permute-done | bytes 131104 | tf_op jit(solution)/shard_map/ppermute | solution.py:379
  26.3 1.6 constant_dynamic-update-slice_fusion.3
  27.9 0.0 collective-permute-done.3
  27.9 0.7 constant_dynamic-update-slice_fusion.2
  28.5 0.7 constant_dynamic-slice_fusion
  29.2 1.1 collective-permute-start.5
  30.3 0.3 collective-permute-done.4
  30.7 7.1 %attention_stats.1 = f32[8,2,1024]{2,1,0:T(2,128)} custom-call(s32[8]{0:T(128)S(1)} %compare_select_fusion.4.place_ref, s32[256]{0:T(256)S(1)} %copy-done.5, bf16[1024,256]{1,0:T(8,128)(2,1)S(1)} %bitcast.15, bf16[1024,256]{1,0:T(8,128)(2,1)S(1)} %bitcast.16, bf16[2048,256]{1,0:T(8,128)(2,1)S(1)} %constant_dynamic-update-slice_fusion.7.k_ref.v_ref, ...), custom_call_target="tpu_custom_call" | custom-call | flops 1073741824 | bytes 4194304 | tf_op jit(solution)/shard_map/attention_stats/pallas_call | solution.py:144
  37.8 7.0 %all-to-all-start.1 = ((f32[8,2,1024]{2,1,0:T(2,128)}), f32[8,2,1024]{2,1,0:T(2,128)S(1)}, u32[]{:S(2)}, u32[]{:S(2)}) async-start(f32[8,2,1024]{2,1,0:T(2,128)} %attention_stats.1), calls=%async_computation.1 | async-start | bytes 131072 | tf_op jit(solution)/shard_map/all_to_all | solution.py:408
  44.9 6.1 %collective-permute-done.5.w_other = bf16[3,1024,128]{2,1,0:T(8,128)(2,1)} collective-permute-done((bf16[3,1024,128]{2,1,0:T(8,128)(2,1)}, bf16[3,1024,128]{2,1,0:T(8,128)(2,1)}, u32[]{:S(2)}, u32[]{:S(2)}) %collective-permute-start.5) | collective-permute-done | bytes 786464 | tf_op jit(solution)/shard_map/ppermute | solution.py:370
  51.0 2.3 %all-to-all-done.1.stat_ref = f32[8,2,1024]{2,1,0:T(2,128)S(1)} async-done(((f32[8,2,1024]{2,1,0:T(2,128)}), f32[8,2,1024]{2,1,0:T(2,128)S(1)}, u32[]{:S(2)}, u32[]{:S(2)}) %all-to-all-start.1) | async-done | bytes 65568 | tf_op jit(solution)/shard_map/all_to_all | solution.py:408
  53.3 1.2 copy-done.4
  54.5 8.6 %attention_grads.1 = (bf16[1024,128]{1,0:T(8,128)(2,1)}, f32[1024,256]{1,0:T(8,128)S(1)}, f32[1024,256]{1,0:T(8,128)}) custom-call(s32[8]{0:T(128)S(1)} %compare_select_fusion.4.place_ref, s32[256]{0:T(256)S(1)} %copy-done.5, bf16[1024,256]{1,0:T(8,128)(2,1)S(1)} %bitcast.17, bf16[1024,256]{1,0:T(8,128)(2,1)S(1)} %bitcast.18, ...), custom_call_target="tpu_custom_call" | custom-call | flops 2684354560 | bytes 4194304 | tf_op jit(solution)/shard_map/attention_grads/pallas_call | solution.py:162
  63.1 0.0 collective-permute-start.6
  63.1 4.8 %all-to-all-start.2 = ((bf16[8,128,128]{2,1,0:T(8,128)(2,1)}), bf16[8,128,128]{2,1,0:T(8,128)(2,1)S(1)}, u32[]{:S(2)}, u32[]{:S(2)}) async-start(bf16[8,128,128]{2,1,0:T(8,128)(2,1)} %bitcast.2), calls=%async_computation.2 | async-start | bytes 524288 | tf_op jit(solution)/shard_map/all_to_all | solution.py:414
  67.9 3.9 %collective-permute-start.7 = (bf16[128,1024]{1,0:T(8,128)(2,1)S(1)}, bf16[128,1024]{1,0:T(8,128)(2,1)S(1)}, u32[]{:S(2)}, u32[]{:S(2)}) collective-permute-start(bf16[128,1024]{1,0:T(8,128)(2,1)S(1)} %copy-done.2), channel_id=1, source_target_pairs={{0,4},{2,6},{4,8},{6,10},{8,12},{10,14},{12,16},{14,18},{16,20},{1... | collective-permute-start | bytes 786440 | tf_op jit(solution)/shard_map/ppermute | solution.py:375
  71.8 6.1 %collective-permute-start.8 = (bf16[64,1024]{1,0:T(8,128)(2,1)}, bf16[64,1024]{1,0:T(8,128)(2,1)S(1)}, u32[]{:S(2)}, u32[]{:S(2)}) collective-permute-start(bf16[64,1024]{1,0:T(8,128)(2,1)} %constant_dynamic-slice_fusion), channel_id=1, source_target_pairs={{4,0},{6,2},{8,4},{10,6},{12,8},{14,10},{16,12},{18,14},{20,16},{2... | collective-permute-start | bytes 393224 | tf_op jit(solution)/shard_map/ppermute | solution.py:375
  77.9 2.1 %add_convert_fusion = bf16[1024,256]{1,0:T(8,128)(2,1)} fusion(f32[1024,256]{1,0:T(8,128)S(1)} %get-tuple-element.42, f32[1024,256]{1,0:T(8,128)} %collective-permute-done.6), kind=kLoop, calls=%fused_computation | loop fusion | flops 524288 | bytes 2621440 | tf_op jit(solution)/shard_map/convert_element_type | solution.py:415
  80.1 1.0 collective-permute-done.8.refs_4_
  81.1 3.0 %collective-permute-done.7.refs_2_ = bf16[128,1024]{1,0:T(8,128)(2,1)S(1)} collective-permute-done((bf16[128,1024]{1,0:T(8,128)(2,1)S(1)}, bf16[128,1024]{1,0:T(8,128)(2,1)S(1)}, u32[]{:S(2)}, u32[]{:S(2)}) %collective-permute-start.7) | collective-permute-done | bytes 262176 | tf_op jit(solution)/shard_map/ppermute | solution.py:375
  84.1 4.1 %all-to-all-start.3 = ((bf16[8,128,256]{2,1,0:T(8,128)(2,1)}), bf16[8,128,256]{2,1,0:T(8,128)(2,1)}, u32[]{:S(2)}, u32[]{:S(2)}) async-start(bf16[8,128,256]{2,1,0:T(8,128)(2,1)} %bitcast.19), calls=%async_computation.3 | async-start | bytes 1048576 | tf_op jit(solution)/shard_map/all_to_all | solution.py:417
  88.2 0.1 collective-permute-start.10
  88.3 0.5 collective-permute-start.9
  88.8 0.1 collective-permute-start.11
  88.9 1.5 collective-permute-done.11.refs_5_
  90.4 5.8 %all-to-all-done.3 = bf16[8,128,256]{2,1,0:T(8,128)(2,1)} async-done(((bf16[8,128,256]{2,1,0:T(8,128)(2,1)}), bf16[8,128,256]{2,1,0:T(8,128)(2,1)}, u32[]{:S(2)}, u32[]{:S(2)}) %all-to-all-start.3) | async-done | bytes 524320 | tf_op jit(solution)/shard_map/all_to_all | solution.py:417
  96.2 1.1 reduce_sum.34.kv_own
  97.3 1.5 collective-permute-start.13
  98.8 2.4 %collective-permute-start.12 = (bf16[128,128]{1,0:T(8,128)(2,1)S(1)}, bf16[128,128]{1,0:T(8,128)(2,1)S(1)}, u32[]{:S(2)}, u32[]{:S(2)}) collective-permute-start(bf16[128,128]{1,0:T(8,128)(2,1)S(1)} %reduce_sum.33.q_own), channel_id=1, source_target_pairs={{0,1},{1,0},{2,3},{3,2},{4,5},{5,4},{6,7},{7,6},{8,9},{9,8},{10,11... | collective-permute-start | bytes 98312 | tf_op jit(solution)/shard_map/ppermute | solution.py:370
  101.2 3.3 %collective-permute-done.12.q_other = bf16[128,128]{1,0:T(8,128)(2,1)S(1)} collective-permute-done((bf16[128,128]{1,0:T(8,128)(2,1)S(1)}, bf16[128,128]{1,0:T(8,128)(2,1)S(1)}, u32[]{:S(2)}, u32[]{:S(2)}) %collective-permute-start.12) | collective-permute-done | bytes 32800 | tf_op jit(solution)/shard_map/ppermute | solution.py:370
  104.5 10.8 %project_and_filter.1 = (bf16[128,1024]{1,0:T(8,128)(2,1)S(1)}, bf16[64,1024]{1,0:T(8,128)(2,1)S(1)}, f32[2,512,128]{2,1,0:T(8,128)S(1)}) custom-call(s32[8]{0:T(128)S(1)} %compare_select_fusion.4.place_ref, s32[256]{0:T(256)S(1)} %copy-done.5, bf16[128,128]{1,0:T(8,128)(2,1)S(1)} %reduce_sum.33.q_own, bf16[128,256]{1,0:T(8,128)(2,1)S(1)} %reduce_sum.34.kv_own, ...), custom_call_target="tpu_custom_call" | custom-call | flops 4294967296 | bytes 8388608 | tf_op jit(solution)/shard_map/project_and_filter/pallas_call | solution.py:289
  115.3 0.0 copy-start
  115.3 0.1 collective-permute-start.14
  115.4 1.5 collective-permute-done.14
  116.9 0.7 fusion
  117.7 9.3 %all-to-all-start.4 = ((f32[64,8,128]{2,1,0:T(8,128)}), f32[64,8,128]{2,1,0:T(8,128)S(1)}, u32[]{:S(2)}, u32[]{:S(2)}) async-start(f32[64,8,128]{2,1,0:T(8,128)} %fusion), calls=%async_computation.4 | async-start | bytes 524288 | tf_op jit(solution)/shard_map/all_to_all | solution.py:433
  127.0 6.7 %collective-permute-start.15 = (bf16[128,1024]{1,0:T(8,128)(2,1)S(1)}, bf16[128,1024]{1,0:T(8,128)(2,1)S(1)}, u32[]{:S(2)}, u32[]{:S(2)}) collective-permute-start(bf16[128,1024]{1,0:T(8,128)(2,1)S(1)} %get-tuple-element.57.refs_0_), channel_id=1, source_target_pairs={{4,0},{6,2},{8,4},{10,6},{12,8},{14,10},{16,12},{18,14},{20,16},{2... | collective-permute-start | bytes 786440 | tf_op jit(solution)/shard_map/ppermute | solution.py:375
  133.7 0.1 collective-permute-start.17
  133.8 1.9 %collective-permute-start.16 = (bf16[64,1024]{1,0:T(8,128)(2,1)S(1)}, bf16[64,1024]{1,0:T(8,128)(2,1)S(1)}, u32[]{:S(2)}, u32[]{:S(2)}) collective-permute-start(bf16[64,1024]{1,0:T(8,128)(2,1)S(1)} %get-tuple-element.58), channel_id=1, source_target_pairs={{0,4},{2,6},{4,8},{6,10},{8,12},{10,14},{12,16},{14,18},{16,20},{1... | collective-permute-start | bytes 393224 | tf_op jit(solution)/shard_map/ppermute | solution.py:375
  135.7 10.1 %collective-permute-done.16.refs_4_ = bf16[64,1024]{1,0:T(8,128)(2,1)S(1)} collective-permute-done((bf16[64,1024]{1,0:T(8,128)(2,1)S(1)}, bf16[64,1024]{1,0:T(8,128)(2,1)S(1)}, u32[]{:S(2)}, u32[]{:S(2)}) %collective-permute-start.16) | collective-permute-done | bytes 131104 | tf_op jit(solution)/shard_map/ppermute | solution.py:375
  145.8 0.1 reduce_sum.35
  145.9 0.7 broadcast_in_dim.27
  146.6 4.6 %all-to-all-start.5 = ((f32[64,8,128]{2,1,0:T(8,128)}), f32[64,8,128]{2,1,0:T(8,128)S(1)}, u32[]{:S(2)}, u32[]{:S(2)}) async-start(f32[64,8,128]{2,1,0:T(8,128)} %broadcast_in_dim.27), calls=%async_computation.5 | async-start | bytes 524288 | tf_op jit(solution)/shard_map/all_to_all | solution.py:366
  151.2 0.1 collective-permute-start.18
  151.3 0.5 collective-permute-start.19
  151.8 1.2 collective-permute-done.19.refs_5_
  153.0 7.0 %input_conv.1 = bf16[128,1024]{1,0:T(8,128)(2,1)} custom-call(s32[8]{0:T(128)S(1)} %compare_select_fusion.4.place_ref, s32[256]{0:T(256)S(1)} %copy-done.5, bf16[128,1024]{1,0:T(8,128)(2,1)S(1)} %get-tuple-element.57.refs_0_, bf16[128,1024]{1,0:T(8,128)(2,1)S(1)} %collective-permute-done.17.refs_1_, bf16[128,1024]{1,0:T(8,128)(2,1)S(1)} %collective-permute-done.15.refs_2_, ...), custom_call_target="tpu_custom_call" | custom-call | flops 1048576 | bytes 1048576 | tf_op jit(solution)/shard_map/input_conv/pallas_call | solution.py:345
  160.0 4.4 %all-to-all-done.5 = f32[64,8,128]{2,1,0:T(8,128)S(1)} async-done(((f32[64,8,128]{2,1,0:T(8,128)}), f32[64,8,128]{2,1,0:T(8,128)S(1)}, u32[]{:S(2)}, u32[]{:S(2)}) %all-to-all-start.5) | async-done | bytes 262176 | tf_op jit(solution)/shard_map/all_to_all | solution.py:366
  164.4 1.5 collective-permute-done.20
  165.9 0.8 pad_maximum_fusion
  (27 shorter events, 0.2 us)
Async XLA Ops:
  0.6 16.4 %copy-start.1 = (bf16[3,2048,128]{2,1,0:T(8,128)(2,1)S(1)}, bf16[3,2048,128]{2,1,0:T(8,128)(2,1)}, u32[]{:S(2)}) copy-start(bf16[3,2048,128]{2,1,0:T(8,128)(2,1)} %w_own.1) | copy-start | bytes 4718596
  2.4 10.9 %collective-permute-start = (bf16[128,256]{1,0:T(8,128)(2,1)}, bf16[128,256]{1,0:T(8,128)(2,1)S(1)}, u32[]{:S(2)}, u32[]{:S(2)}) collective-permute-start(bf16[128,256]{1,0:T(8,128)(2,1)} %get-tuple-element.36), channel_id=1, source_target_pairs={{0,128},{128,0},{1,129},{129,1},{2,130},{130,2},{3,131},{131,3},{4... | collective-permute-start | bytes 196616 | tf_op jit(solution)/shard_map/ppermute | solution.py:370
  3.3 14.7 %copy-start.5 = (s32[256]{0:T(256)S(1)}, s32[256]{0:T(256)}, u32[]{:S(2)}) copy-start(s32[256]{0:T(256)} %order_ref.7) | copy-start | bytes 3076
  3.3 27.4 %all-to-all-start = ((bf16[8,128,256]{2,1,0:T(8,128)(2,1)}), bf16[8,128,256]{2,1,0:T(8,128)(2,1)S(1)}, u32[]{:S(2)}, u32[]{:S(2)}) async-start(bf16[8,128,256]{2,1,0:T(8,128)(2,1)} %get-tuple-element.35), calls=%async_computation | async-start | bytes 1048576 | tf_op jit(solution)/shard_map/all_to_all | solution.py:393
  13.4 15.2 %copy-start.2 = (bf16[128,1024]{1,0:T(8,128)(2,1)S(1)}, bf16[128,1024]{1,0:T(8,128)(2,1)}, u32[]{:S(2)}) copy-start(bf16[128,1024]{1,0:T(8,128)(2,1)} %refs_0_.1) | copy-start | bytes 786436
  14.0 8.7 %collective-permute-start.1 = (bf16[256,256]{1,0:T(8,128)(2,1)}, bf16[256,256]{1,0:T(8,128)(2,1)S(1)}, u32[]{:S(2)}, u32[]{:S(2)}) collective-permute-start(bf16[256,256]{1,0:T(8,128)(2,1)} %get-tuple-element.78), channel_id=1, source_target_pairs={{32,0},{64,32},{96,64},{0,96},{33,1},{65,33},{97,65},{1,97},{34,2}... | collective-permute-start | bytes 393224 | tf_op jit(solution)/shard_map/ppermute | solution.py:379
  18.1 8.2 %collective-permute-start.2 = (bf16[256,256]{1,0:T(8,128)(2,1)}, bf16[256,256]{1,0:T(8,128)(2,1)}, u32[]{:S(2)}, u32[]{:S(2)}) collective-permute-start(bf16[256,256]{1,0:T(8,128)(2,1)} %get-tuple-element.78), channel_id=1, source_target_pairs={{64,0},{96,32},{0,64},{32,96},{65,1},{97,33},{1,65},{33,97},{66,2}... | collective-permute-start | bytes 393224 | tf_op jit(solution)/shard_map/ppermute | solution.py:379
  20.6 7.2 %collective-permute-start.3 = (bf16[256,256]{1,0:T(8,128)(2,1)}, bf16[256,256]{1,0:T(8,128)(2,1)S(1)}, u32[]{:S(2)}, u32[]{:S(2)}) collective-permute-start(bf16[256,256]{1,0:T(8,128)(2,1)} %get-tuple-element.78), channel_id=1, source_target_pairs={{96,0},{0,32},{32,64},{64,96},{97,1},{1,33},{33,65},{65,97},{98,2}... | collective-permute-start | bytes 393224 | tf_op jit(solution)/shard_map/ppermute | solution.py:379
  28.5 2.1 %collective-permute-start.4 = (bf16[1024,256]{1,0:T(8,128)(2,1)}, bf16[1024,256]{1,0:T(8,128)(2,1)S(1)}, u32[]{:S(2)}, u32[]{:S(2)}) collective-permute-start(bf16[1024,256]{1,0:T(8,128)(2,1)} %get-tuple-element.70), channel_id=1, source_target_pairs={{0,2},{2,0},{1,3},{3,1},{4,6},{6,4},{5,7},{7,5},{8,10},{10,8},{9,1... | collective-permute-start | bytes 1572872 | tf_op jit(solution)/shard_map/ppermute | solution.py:370
  29.2 21.8 %collective-permute-start.5 = (bf16[3,1024,128]{2,1,0:T(8,128)(2,1)}, bf16[3,1024,128]{2,1,0:T(8,128)(2,1)}, u32[]{:S(2)}, u32[]{:S(2)}) collective-permute-start(bf16[3,1024,128]{2,1,0:T(8,128)(2,1)} %constant_dynamic-slice_fusion.1), channel_id=1, source_target_pairs={{0,1},{1,0},{2,3},{3,2},{4,5},{5,4},{6,7},{7,6},{8,9},{9,8},{10,11... | collective-permute-start | bytes 2359304 | tf_op jit(solution)/shard_map/ppermute | solution.py:370
  30.7 7.2 %copy-start.3 = (bf16[2048,256]{1,0:T(8,128)(2,1)}, bf16[2048,256]{1,0:T(8,128)(2,1)S(1)}, u32[]{:S(2)}) copy-start(bf16[2048,256]{1,0:T(8,128)(2,1)S(1)} %constant_dynamic-update-slice_fusion.7.k_ref.v_ref) | copy-start | bytes 3145732
  37.8 15.4 %all-to-all-start.1 = ((f32[8,2,1024]{2,1,0:T(2,128)}), f32[8,2,1024]{2,1,0:T(2,128)S(1)}, u32[]{:S(2)}, u32[]{:S(2)}) async-start(f32[8,2,1024]{2,1,0:T(2,128)} %attention_stats.1), calls=%async_computation.1 | async-start | bytes 131072 | tf_op jit(solution)/shard_map/all_to_all | solution.py:408
  53.2 1.2 copy-start.4
  63.1 14.8 %collective-permute-start.6 = (f32[1024,256]{1,0:T(8,128)}, f32[1024,256]{1,0:T(8,128)}, u32[]{:S(2)}, u32[]{:S(2)}) collective-permute-start(f32[1024,256]{1,0:T(8,128)} %get-tuple-element.43), channel_id=1, source_target_pairs={{0,2},{2,0},{1,3},{3,1},{4,6},{6,4},{5,7},{7,5},{8,10},{10,8},{9,1... | collective-permute-start | bytes 3145736 | tf_op jit(solution)/shard_map/ppermute | solution.py:370
  63.1 21.0 %all-to-all-start.2 = ((bf16[8,128,128]{2,1,0:T(8,128)(2,1)}), bf16[8,128,128]{2,1,0:T(8,128)(2,1)S(1)}, u32[]{:S(2)}, u32[]{:S(2)}) async-start(bf16[8,128,128]{2,1,0:T(8,128)(2,1)} %bitcast.2), calls=%async_computation.2 | async-start | bytes 524288 | tf_op jit(solution)/shard_map/all_to_all | solution.py:414
  67.9 16.2 %collective-permute-start.7 = (bf16[128,1024]{1,0:T(8,128)(2,1)S(1)}, bf16[128,1024]{1,0:T(8,128)(2,1)S(1)}, u32[]{:S(2)}, u32[]{:S(2)}) collective-permute-start(bf16[128,1024]{1,0:T(8,128)(2,1)S(1)} %copy-done.2), channel_id=1, source_target_pairs={{0,4},{2,6},{4,8},{6,10},{8,12},{10,14},{12,16},{14,18},{16,20},{1... | collective-permute-start | bytes 786440 | tf_op jit(solution)/shard_map/ppermute | solution.py:375
  71.8 9.3 %collective-permute-start.8 = (bf16[64,1024]{1,0:T(8,128)(2,1)}, bf16[64,1024]{1,0:T(8,128)(2,1)S(1)}, u32[]{:S(2)}, u32[]{:S(2)}) collective-permute-start(bf16[64,1024]{1,0:T(8,128)(2,1)} %constant_dynamic-slice_fusion), channel_id=1, source_target_pairs={{4,0},{6,2},{8,4},{10,6},{12,8},{14,10},{16,12},{18,14},{20,16},{2... | collective-permute-start | bytes 393224 | tf_op jit(solution)/shard_map/ppermute | solution.py:375
  84.1 12.1 %all-to-all-start.3 = ((bf16[8,128,256]{2,1,0:T(8,128)(2,1)}), bf16[8,128,256]{2,1,0:T(8,128)(2,1)}, u32[]{:S(2)}, u32[]{:S(2)}) async-start(bf16[8,128,256]{2,1,0:T(8,128)(2,1)} %bitcast.19), calls=%async_computation.3 | async-start | bytes 1048576 | tf_op jit(solution)/shard_map/all_to_all | solution.py:417
  88.2 2.2 %collective-permute-start.10 = (bf16[128,1024]{1,0:T(8,128)(2,1)S(1)}, bf16[128,1024]{1,0:T(8,128)(2,1)S(1)}, u32[]{:S(2)}, u32[]{:S(2)}) collective-permute-start(bf16[128,1024]{1,0:T(8,128)(2,1)S(1)} %collective-permute-done.7.refs_2_), channel_id=1, source_target_pairs={{0,2},{2,0},{1,3},{3,1},{4,6},{6,4},{5,7},{7,5},{8,10},{10,8},{9,1... | collective-permute-start | bytes 786440 | tf_op jit(solution)/shard_map/ppermute | solution.py:370
  88.3 2.1 %collective-permute-start.9 = (bf16[128,1024]{1,0:T(8,128)(2,1)S(1)}, bf16[128,1024]{1,0:T(8,128)(2,1)S(1)}, u32[]{:S(2)}, u32[]{:S(2)}) collective-permute-start(bf16[128,1024]{1,0:T(8,128)(2,1)S(1)} %copy-done.2), channel_id=1, source_target_pairs={{0,2},{2,0},{1,3},{3,1},{4,6},{6,4},{5,7},{7,5},{8,10},{10,8},{9,1... | collective-permute-start | bytes 786440 | tf_op jit(solution)/shard_map/ppermute | solution.py:370
  88.8 1.6 collective-permute-start.11
  97.3 7.2 %collective-permute-start.13 = (bf16[128,256]{1,0:T(8,128)(2,1)S(1)}, bf16[128,256]{1,0:T(8,128)(2,1)S(1)}, u32[]{:S(2)}, u32[]{:S(2)}) collective-permute-start(bf16[128,256]{1,0:T(8,128)(2,1)S(1)} %reduce_sum.34.kv_own), channel_id=1, source_target_pairs={{0,1},{1,0},{2,3},{3,2},{4,5},{5,4},{6,7},{7,6},{8,9},{9,8},{10,11... | collective-permute-start | bytes 196616 | tf_op jit(solution)/shard_map/ppermute | solution.py:370
  98.8 5.7 %collective-permute-start.12 = (bf16[128,128]{1,0:T(8,128)(2,1)S(1)}, bf16[128,128]{1,0:T(8,128)(2,1)S(1)}, u32[]{:S(2)}, u32[]{:S(2)}) collective-permute-start(bf16[128,128]{1,0:T(8,128)(2,1)S(1)} %reduce_sum.33.q_own), channel_id=1, source_target_pairs={{0,1},{1,0},{2,3},{3,2},{4,5},{5,4},{6,7},{7,6},{8,9},{9,8},{10,11... | collective-permute-start | bytes 98312 | tf_op jit(solution)/shard_map/ppermute | solution.py:370
  115.3 37.7 %copy-start = (f32[1024,128]{1,0:T(8,128)S(1)}, f32[1024,128]{1,0:T(8,128)}, u32[]{:S(2)}) copy-start(f32[1024,128]{1,0:T(8,128)} %refs_6_.1) | copy-start | bytes 1572868
  115.3 1.6 collective-permute-start.14
  117.7 28.1 %all-to-all-start.4 = ((f32[64,8,128]{2,1,0:T(8,128)}), f32[64,8,128]{2,1,0:T(8,128)S(1)}, u32[]{:S(2)}, u32[]{:S(2)}) async-start(f32[64,8,128]{2,1,0:T(8,128)} %fusion), calls=%async_computation.4 | async-start | bytes 524288 | tf_op jit(solution)/shard_map/all_to_all | solution.py:433
  127.0 18.8 %collective-permute-start.15 = (bf16[128,1024]{1,0:T(8,128)(2,1)S(1)}, bf16[128,1024]{1,0:T(8,128)(2,1)S(1)}, u32[]{:S(2)}, u32[]{:S(2)}) collective-permute-start(bf16[128,1024]{1,0:T(8,128)(2,1)S(1)} %get-tuple-element.57.refs_0_), channel_id=1, source_target_pairs={{4,0},{6,2},{8,4},{10,6},{12,8},{14,10},{16,12},{18,14},{20,16},{2... | collective-permute-start | bytes 786440 | tf_op jit(solution)/shard_map/ppermute | solution.py:375
  133.7 12.1 %collective-permute-start.17 = (bf16[128,1024]{1,0:T(8,128)(2,1)S(1)}, bf16[128,1024]{1,0:T(8,128)(2,1)S(1)}, u32[]{:S(2)}, u32[]{:S(2)}) collective-permute-start(bf16[128,1024]{1,0:T(8,128)(2,1)S(1)} %get-tuple-element.57.refs_0_), channel_id=1, source_target_pairs={{0,2},{2,0},{1,3},{3,1},{4,6},{6,4},{5,7},{7,5},{8,10},{10,8},{9,1... | collective-permute-start | bytes 786440 | tf_op jit(solution)/shard_map/ppermute | solution.py:370
  133.8 12.0 %collective-permute-start.16 = (bf16[64,1024]{1,0:T(8,128)(2,1)S(1)}, bf16[64,1024]{1,0:T(8,128)(2,1)S(1)}, u32[]{:S(2)}, u32[]{:S(2)}) collective-permute-start(bf16[64,1024]{1,0:T(8,128)(2,1)S(1)} %get-tuple-element.58), channel_id=1, source_target_pairs={{0,4},{2,6},{4,8},{6,10},{8,12},{10,14},{12,16},{14,18},{16,20},{1... | collective-permute-start | bytes 393224 | tf_op jit(solution)/shard_map/ppermute | solution.py:375
  146.6 17.8 %all-to-all-start.5 = ((f32[64,8,128]{2,1,0:T(8,128)}), f32[64,8,128]{2,1,0:T(8,128)S(1)}, u32[]{:S(2)}, u32[]{:S(2)}) async-start(f32[64,8,128]{2,1,0:T(8,128)} %broadcast_in_dim.27), calls=%async_computation.5 | async-start | bytes 524288 | tf_op jit(solution)/shard_map/all_to_all | solution.py:366
  151.2 1.8 %collective-permute-start.18 = (bf16[128,1024]{1,0:T(8,128)(2,1)S(1)}, bf16[128,1024]{1,0:T(8,128)(2,1)S(1)}, u32[]{:S(2)}, u32[]{:S(2)}) collective-permute-start(bf16[128,1024]{1,0:T(8,128)(2,1)S(1)} %collective-permute-done.15.refs_2_), channel_id=1, source_target_pairs={{0,2},{2,0},{1,3},{3,1},{4,6},{6,4},{5,7},{7,5},{8,10},{10,8},{9,1... | collective-permute-start | bytes 786440 | tf_op jit(solution)/shard_map/ppermute | solution.py:370
  151.3 1.7 %collective-permute-start.19 = (bf16[64,1024]{1,0:T(8,128)(2,1)S(1)}, bf16[64,1024]{1,0:T(8,128)(2,1)S(1)}, u32[]{:S(2)}, u32[]{:S(2)}) collective-permute-start(bf16[64,1024]{1,0:T(8,128)(2,1)S(1)} %collective-permute-done.16.refs_4_), channel_id=1, source_target_pairs={{0,2},{2,0},{1,3},{3,1},{4,6},{6,4},{5,7},{7,5},{8,10},{10,8},{9,1... | collective-permute-start | bytes 393224 | tf_op jit(solution)/shard_map/ppermute | solution.py:370
  164.4 1.5 collective-permute-start.20

commit v4 on v3

--- a/solution.py
+++ b/solution.py
@@ -19,7 +19,7 @@
 LOWEST = -1e30
 LOG2E = 1.4426950408889634
 SCALE = HD**-0.5
-QB = 256
+QB = 1024
 BF = jnp.bfloat16
 F32 = jnp.float32
 LANES = 128
@@ -238,13 +238,21 @@
     n_in, place_ref, order_ref, q_own, kv_own, q_other, kv_other, w_own, w_other, *refs
 ):
     ins = refs[:n_in]
-    pair_ref, high_ref, filt_ref, cand, grad, ext, lag = refs[n_in:]
-    cg = jnp.zeros((ROWS, LANES), F32)
-    for q_ref, kv_ref, w_ref in ((q_own, kv_own, w_own), (q_other, kv_other, w_other)):
-        cg = cg + nt(q_ref[...], w_ref[0])
-        cg = cg + nt(kv_ref[:, :HD], w_ref[1])
-        cg = cg + nt(kv_ref[:, HD:], w_ref[2])
-    grad[...] = cg.astype(BF).astype(F32)
+    pair_ref, high_ref, filt_ref, cand, projected, grad, ext, lag = refs[n_in:]
+    step = pl.program_id(0)
+
+    @pl.when(step == 0)
+    def _():
+        cg = jnp.zeros((ROWS, w_own.shape[1]), F32)
+        for q_ref, kv_ref, w_ref in ((q_own, kv_own, w_own), (q_other, kv_other, w_other)):
+            cg = cg + nt(q_ref[...], w_ref[0])
+            cg = cg + nt(kv_ref[:, :HD], w_ref[1])
+            cg = cg + nt(kv_ref[:, HD:], w_ref[2])
+        cg = cg.astype(BF).astype(F32)
+        for tile in range(w_own.shape[1] // LANES):
+            projected[tile] = cg[:, tile * LANES : (tile + 1) * LANES]
+
+    grad[...] = projected[step]
     device = device_at(place_ref)
     partner = device + 1 - 2 * place_ref[3]
     first, second = order_ref[2 * device], order_ref[2 * device + 1]
@@ -260,17 +268,18 @@
     have += low_high(order_ref, device + 2)[1:] + low_high(order_ref, partner + 2)[1:]
     extend(place_ref, order_ref, have, -2, cand, ext)
     for r in range(8):
+        totals = [None] * (TAPS // 8)
         for slot in range(2):
             rows = [grad[slot * BLK + 8 * m : slot * BLK + 8 * m + 8, :] for m in range(BLK // 8)]
             last = 2 * BLK - r
             shifted = [ext[slot, last - TAPS + 8 + 8 * n : last - TAPS + 16 + 8 * n, :] for n in range(23)]
             for a in range(TAPS // 8):
-                total = rows[0] * shifted[15 - a]
-                for m in range(1, BLK // 8):
-                    total = total + rows[m] * shifted[15 - a + m]
-                j = 8 * a + r
-                here = slice(8 * j, 8 * j + 8)
-                lag[here, :] = total if slot == 0 else lag[here, :] + total
+                for m in range(BLK // 8):
+                    term = rows[m] * shifted[15 - a + m]
+                    totals[a] = term if totals[a] is None else totals[a] + term
+        for a in range(TAPS // 8):
+            j = 8 * a + r
+            lag[8 * j : 8 * j + 8, :] = totals[a]
     taps = lag[pl.ds(0, TAPS, stride=8), :]
     for s in range(1, 8):
         taps = taps + lag[pl.ds(s, TAPS, stride=8), :]
@@ -293,13 +302,14 @@
             grid=(tiles,),
             in_specs=[whole(a) for a in (q_own, kv_own, q_other, kv_other)]
             + [
-                pl.BlockSpec((3, LANES, HD), lambda i, p, o: (0, p[4] * tiles + i, 0)),
-                pl.BlockSpec((3, LANES, HD), lambda i, p, o: (0, i, 0)),
+                pl.BlockSpec((3, channels, HD), lambda i, p, o: (0, p[4], 0)),
+                pl.BlockSpec((3, channels, HD), lambda i, p, o: (0, 0, 0)),
             ]
             + [column(a) for a in ins],
             out_specs=[block(ROWS), block(BLK), pl.BlockSpec((1, LANES, TAPS), which)],
             scratch_shapes=[
                 pltpu.VMEM((blocks, BLK, LANES), F32),
+                pltpu.VMEM((tiles, ROWS, LANES), F32),
                 pltpu.VMEM((ROWS, LANES), F32),
                 pltpu.VMEM((2, 3 * BLK, LANES), F32),
                 pltpu.VMEM((8 * TAPS, LANES), F32),

time: 169 us -> 167 us (0.988)
  Pallas kernels: 35.3 us -> 30.6 us
  starting transfers between devices: 69.1 us -> 70.9 us
    pallas_call x1, Pallas kernels: 10.8 us -> 8.82 us  [project_and_filter(): pl.pallas_call(functools.partial(filter_kernel, len(ins)), grid_spec=pltp...]
    pallas_call x1, Pallas kernels: 7.13 us -> 5.26 us  [attention_stats(): pl.pallas_call(stats_kernel, grid_spec=pltpu.PrefetchScalarGridSpec(num_s...]
    all_to_all x1, waiting for transfers between devices: 2.28 us -> 0.43 us  [local(): stats = lax.all_to_all(stats, 'z', 0, 0, tiled=True)]
    all_to_all x1, starting transfers between devices: 4.76 us -> 6.6 us  [local(): dq_parts = lax.all_to_all(dq.reshape(Z, ROWS, HD), 'z', 0, 0, tiled=True)]
    ppermute x14, waiting for transfers between devices: 15.5 us -> 17.2 us  [swap(): return lax.ppermute(x, axis, [(0, 1), (1, 0)])]
  transfers between devices with their start and end apart: 27 -> 27, of which waited for: 15 -> 15; matrix products, arithmetic and copies ran while one was open for 6% -> 6% of each run, Pallas kernels for 8% -> 7%
where the time goes in v4:
time: 167 us; the launch traced here: 164 us
  starting transfers between devices  70.9 us (42%)
  waiting for transfers between devices  45.8 us (27%)
  Pallas kernels  30.6 us (18%)
  local copies, waits for them, and re-layouts  9.39 us (6%)
  other arithmetic  4.97 us (3%)
  between operations  2.13 us (1%)
    ppermute x4, starting transfers between devices, from_ctx(): lax.ppermute(x, CTX, [(i + distance, i) for i in range(n) if 0 <= i + dis...  18.7 us
    ppermute x14, waiting for transfers between devices, swap(): return lax.ppermute(x, axis, [(0, 1), (1, 0)])  17.2 us
    ppermute x4, waiting for transfers between devices, from_ctx(): lax.ppermute(x, CTX, [(i + distance, i) for i in range(n) if 0 <= i + dis...  14.1 us
    all_to_all x1, starting transfers between devices, local(): lax.all_to_all(mine_sum.reshape(chips, channels // 2 // chips, TAPS), ('x...  9.46 us
    pallas_call x1, Pallas kernels, project_and_filter(): pl.pallas_call(functools.partial(filter_kernel, len(ins)), grid_spec=pltp...  8.82 us
    all_to_all x1, starting transfers between devices, local(): qg = lax.all_to_all(qg, 'z', 0, 0, tiled=True).reshape(NQ, 2 * HD)  8.6 us
    pallas_call x1, Pallas kernels, attention_grads(): pl.pallas_call(grads_kernel, grid_spec=pltpu.PrefetchScalarGridSpec(num_s...  7.71 us
    ppermute x14, starting transfers between devices, swap(): return lax.ppermute(x, axis, [(0, 1), (1, 0)])  7.12 us
  transfers between devices with their start and end apart: 27, of which 15 were waited for; matrix products, arithmetic and copies ran while one was open for 6% of the time, Pallas kernels for 7%

profile of v4, /device:TPU:6, one launch (start us, length us, event | category | flops | bytes accessed | tf_op | source)
XLA Modules:
  0.0 163.8 jit_solution(13225151751986652884)
XLA Ops:
  0.6 1.8 %pack.1 = (bf16[8,128,256]{2,1,0:T(8,128)(2,1)}, bf16[128,256]{1,0:T(8,128)(2,1)}) custom-call(bf16[128,128]{1,0:T(8,128)(2,1)} %q_ref.1, bf16[128,128]{1,0:T(8,128)(2,1)} %g_ref.1, bf16[128,128]{1,0:T(8,128)(2,1)} %k_ref.1, bf16[128,128]{1,0:T(8,128)(2,1)} %v_ref.1), custom_call_target="tpu_custom_call" | custom-call | tf_op jit(solution)/shard_map/pack/pallas_call | solution.py:195
  2.4 0.8 collective-permute-start
  3.3 8.6 %all-to-all-start = ((bf16[8,128,256]{2,1,0:T(8,128)(2,1)}), bf16[8,128,256]{2,1,0:T(8,128)(2,1)S(1)}, u32[]{:S(2)}, u32[]{:S(2)}) async-start(bf16[8,128,256]{2,1,0:T(8,128)(2,1)} %get-tuple-element.35), calls=%async_computation | async-start | bytes 1048576 | tf_op jit(solution)/shard_map/all_to_all | solution.py:403
  11.9 1.5 constant_dynamic-update-slice_fusion.6
  13.4 0.0 collective-permute-done
  13.4 0.7 constant_dynamic-update-slice_fusion.5
  14.0 3.0 %collective-permute-start.1 = (bf16[256,256]{1,0:T(8,128)(2,1)}, bf16[256,256]{1,0:T(8,128)(2,1)S(1)}, u32[]{:S(2)}, u32[]{:S(2)}) collective-permute-start(bf16[256,256]{1,0:T(8,128)(2,1)} %get-tuple-element.78), channel_id=1, source_target_pairs={{32,0},{64,32},{96,64},{0,96},{33,1},{65,33},{97,65},{1,97},{34,2}... | collective-permute-start | bytes 393224 | tf_op jit(solution)/shard_map/ppermute | solution.py:389
  17.1 0.9 constant_dynamic-slice_fusion.1
  18.0 0.1 dynamic_slice.10
  18.1 0.7 collective-permute-start.2
  18.7 0.6 fusion.1
  20.6 1.0 collective-permute-start.3
  21.7 1.0 collective-permute-done.1
  22.7 0.7 constant_dynamic-update-slice_fusion.4
  23.4 2.9 %collective-permute-done.2 = bf16[256,256]{1,0:T(8,128)(2,1)} collective-permute-done((bf16[256,256]{1,0:T(8,128)(2,1)}, bf16[256,256]{1,0:T(8,128)(2,1)}, u32[]{:S(2)}, u32[]{:S(2)}) %collective-permute-start.2) | collective-permute-done | bytes 131104 | tf_op jit(solution)/shard_map/ppermute | solution.py:389
  26.3 1.6 constant_dynamic-update-slice_fusion.3
  27.9 0.0 collective-permute-done.3
  27.9 0.7 constant_dynamic-update-slice_fusion.2
  28.5 0.0 collective-permute-start.4
  28.5 0.7 constant_dynamic-slice_fusion
  29.2 1.1 collective-permute-start.5
  30.3 0.3 collective-permute-done.4
  30.7 5.3 %attention_stats.1 = f32[8,2,1024]{2,1,0:T(2,128)} custom-call(s32[8]{0:T(128)S(1)} %compare_select_fusion.4.place_ref, s32[256]{0:T(256)S(1)} %copy-done.5, bf16[1024,256]{1,0:T(8,128)(2,1)S(1)} %bitcast.15, bf16[1024,256]{1,0:T(8,128)(2,1)S(1)} %bitcast.16, bf16[2048,256]{1,0:T(8,128)(2,1)S(1)} %constant_dynamic-update-slice_fusion.7.k_ref.v_ref, ...), custom_call_target="tpu_custom_call" | custom-call | flops 1073741824 | bytes 4194304 | tf_op jit(solution)/shard_map/attention_stats/pallas_call | solution.py:144
  36.0 7.1 %all-to-all-start.1 = ((f32[8,2,1024]{2,1,0:T(2,128)}), f32[8,2,1024]{2,1,0:T(2,128)S(1)}, u32[]{:S(2)}, u32[]{:S(2)}) async-start(f32[8,2,1024]{2,1,0:T(2,128)} %attention_stats.1), calls=%async_computation.1 | async-start | bytes 131072 | tf_op jit(solution)/shard_map/all_to_all | solution.py:418
  43.0 7.9 %collective-permute-done.5.w_other = bf16[3,1024,128]{2,1,0:T(8,128)(2,1)} collective-permute-done((bf16[3,1024,128]{2,1,0:T(8,128)(2,1)}, bf16[3,1024,128]{2,1,0:T(8,128)(2,1)}, u32[]{:S(2)}, u32[]{:S(2)}) %collective-permute-start.5) | collective-permute-done | bytes 786464 | tf_op jit(solution)/shard_map/ppermute | solution.py:380
  51.0 0.4 all-to-all-done.1.stat_ref
  51.4 1.2 copy-done.4
  52.6 7.7 %attention_grads.1 = (bf16[1024,128]{1,0:T(8,128)(2,1)}, f32[1024,256]{1,0:T(8,128)S(1)}, f32[1024,256]{1,0:T(8,128)}) custom-call(s32[8]{0:T(128)S(1)} %compare_select_fusion.4.place_ref, s32[256]{0:T(256)S(1)} %copy-done.5, bf16[1024,256]{1,0:T(8,128)(2,1)S(1)} %bitcast.17, bf16[1024,256]{1,0:T(8,128)(2,1)S(1)} %bitcast.18, ...), custom_call_target="tpu_custom_call" | custom-call | flops 2684354560 | bytes 4194304 | tf_op jit(solution)/shard_map/attention_grads/pallas_call | solution.py:162
  60.3 6.6 %all-to-all-start.2 = ((bf16[8,128,128]{2,1,0:T(8,128)(2,1)}), bf16[8,128,128]{2,1,0:T(8,128)(2,1)S(1)}, u32[]{:S(2)}, u32[]{:S(2)}) async-start(bf16[8,128,128]{2,1,0:T(8,128)(2,1)} %bitcast.2), calls=%async_computation.2 | async-start | bytes 524288 | tf_op jit(solution)/shard_map/all_to_all | solution.py:424
  66.9 3.9 %collective-permute-start.7 = (bf16[128,1024]{1,0:T(8,128)(2,1)S(1)}, bf16[128,1024]{1,0:T(8,128)(2,1)S(1)}, u32[]{:S(2)}, u32[]{:S(2)}) collective-permute-start(bf16[128,1024]{1,0:T(8,128)(2,1)S(1)} %copy-done.2), channel_id=1, source_target_pairs={{0,4},{2,6},{4,8},{6,10},{8,12},{10,14},{12,16},{14,18},{16,20},{1... | collective-permute-start | bytes 786440 | tf_op jit(solution)/shard_map/ppermute | solution.py:385
  70.9 6.1 %collective-permute-start.8 = (bf16[64,1024]{1,0:T(8,128)(2,1)}, bf16[64,1024]{1,0:T(8,128)(2,1)S(1)}, u32[]{:S(2)}, u32[]{:S(2)}) collective-permute-start(bf16[64,1024]{1,0:T(8,128)(2,1)} %constant_dynamic-slice_fusion), channel_id=1, source_target_pairs={{4,0},{6,2},{8,4},{10,6},{12,8},{14,10},{16,12},{18,14},{20,16},{2... | collective-permute-start | bytes 393224 | tf_op jit(solution)/shard_map/ppermute | solution.py:385
  77.0 2.1 %add_convert_fusion = bf16[1024,256]{1,0:T(8,128)(2,1)} fusion(f32[1024,256]{1,0:T(8,128)S(1)} %get-tuple-element.42, f32[1024,256]{1,0:T(8,128)} %collective-permute-done.6), kind=kLoop, calls=%fused_computation | loop fusion | flops 524288 | bytes 2621440 | tf_op jit(solution)/shard_map/convert_element_type | solution.py:425
  79.2 1.0 collective-permute-done.8.refs_4_
  80.2 3.0 %collective-permute-done.7.refs_2_ = bf16[128,1024]{1,0:T(8,128)(2,1)S(1)} collective-permute-done((bf16[128,1024]{1,0:T(8,128)(2,1)S(1)}, bf16[128,1024]{1,0:T(8,128)(2,1)S(1)}, u32[]{:S(2)}, u32[]{:S(2)}) %collective-permute-start.7) | collective-permute-done | bytes 262176 | tf_op jit(solution)/shard_map/ppermute | solution.py:385
  83.2 4.1 %all-to-all-start.3 = ((bf16[8,128,256]{2,1,0:T(8,128)(2,1)}), bf16[8,128,256]{2,1,0:T(8,128)(2,1)}, u32[]{:S(2)}, u32[]{:S(2)}) async-start(bf16[8,128,256]{2,1,0:T(8,128)(2,1)} %bitcast.19), calls=%async_computation.3 | async-start | bytes 1048576 | tf_op jit(solution)/shard_map/all_to_all | solution.py:427
  87.3 0.1 collective-permute-start.10
  87.4 0.5 collective-permute-start.9
  87.9 0.1 collective-permute-start.11
  88.0 1.5 collective-permute-done.11.refs_5_
  89.5 5.8 %all-to-all-done.3 = bf16[8,128,256]{2,1,0:T(8,128)(2,1)} async-done(((bf16[8,128,256]{2,1,0:T(8,128)(2,1)}), bf16[8,128,256]{2,1,0:T(8,128)(2,1)}, u32[]{:S(2)}, u32[]{:S(2)}) %all-to-all-start.3) | async-done | bytes 524320 | tf_op jit(solution)/shard_map/all_to_all | solution.py:427
  95.3 1.1 reduce_sum.34.kv_own
  96.4 1.4 collective-permute-start.13
  97.8 2.3 %collective-permute-start.12 = (bf16[128,128]{1,0:T(8,128)(2,1)S(1)}, bf16[128,128]{1,0:T(8,128)(2,1)S(1)}, u32[]{:S(2)}, u32[]{:S(2)}) collective-permute-start(bf16[128,128]{1,0:T(8,128)(2,1)S(1)} %reduce_sum.33.q_own), channel_id=1, source_target_pairs={{0,1},{1,0},{2,3},{3,2},{4,5},{5,4},{6,7},{7,6},{8,9},{9,8},{10,11... | collective-permute-start | bytes 98312 | tf_op jit(solution)/shard_map/ppermute | solution.py:380
  100.1 3.2 %collective-permute-done.12.q_other = bf16[128,128]{1,0:T(8,128)(2,1)S(1)} collective-permute-done((bf16[128,128]{1,0:T(8,128)(2,1)S(1)}, bf16[128,128]{1,0:T(8,128)(2,1)S(1)}, u32[]{:S(2)}, u32[]{:S(2)}) %collective-permute-start.12) | collective-permute-done | bytes 32800 | tf_op jit(solution)/shard_map/ppermute | solution.py:380
  103.3 8.8 %project_and_filter.1 = (bf16[128,1024]{1,0:T(8,128)(2,1)S(1)}, bf16[64,1024]{1,0:T(8,128)(2,1)S(1)}, f32[2,512,128]{2,1,0:T(8,128)S(1)}) custom-call(s32[8]{0:T(128)S(1)} %compare_select_fusion.4.place_ref, s32[256]{0:T(256)S(1)} %copy-done.5, bf16[128,128]{1,0:T(8,128)(2,1)S(1)} %reduce_sum.33.q_own, bf16[128,256]{1,0:T(8,128)(2,1)S(1)} %reduce_sum.34.kv_own, ...), custom_call_target="tpu_custom_call" | custom-call | flops 4294967296 | bytes 8388608 | tf_op jit(solution)/shard_map/project_and_filter/pallas_call | solution.py:298
  112.2 0.0 copy-start
  112.2 0.1 collective-permute-start.14
  112.3 1.5 collective-permute-done.14
  113.8 0.7 fusion
  114.5 9.5 %all-to-all-start.4 = ((f32[64,8,128]{2,1,0:T(8,128)}), f32[64,8,128]{2,1,0:T(8,128)S(1)}, u32[]{:S(2)}, u32[]{:S(2)}) async-start(f32[64,8,128]{2,1,0:T(8,128)} %fusion), calls=%async_computation.4 | async-start | bytes 524288 | tf_op jit(solution)/shard_map/all_to_all | solution.py:443
  124.0 6.7 %collective-permute-start.15 = (bf16[128,1024]{1,0:T(8,128)(2,1)S(1)}, bf16[128,1024]{1,0:T(8,128)(2,1)S(1)}, u32[]{:S(2)}, u32[]{:S(2)}) collective-permute-start(bf16[128,1024]{1,0:T(8,128)(2,1)S(1)} %get-tuple-element.57.refs_0_), channel_id=1, source_target_pairs={{4,0},{6,2},{8,4},{10,6},{12,8},{14,10},{16,12},{18,14},{20,16},{2... | collective-permute-start | bytes 786440 | tf_op jit(solution)/shard_map/ppermute | solution.py:385
  130.7 0.1 collective-permute-start.17
  130.8 1.9 %collective-permute-start.16 = (bf16[64,1024]{1,0:T(8,128)(2,1)S(1)}, bf16[64,1024]{1,0:T(8,128)(2,1)S(1)}, u32[]{:S(2)}, u32[]{:S(2)}) collective-permute-start(bf16[64,1024]{1,0:T(8,128)(2,1)S(1)} %get-tuple-element.58), channel_id=1, source_target_pairs={{0,4},{2,6},{4,8},{6,10},{8,12},{10,14},{12,16},{14,18},{16,20},{1... | collective-permute-start | bytes 393224 | tf_op jit(solution)/shard_map/ppermute | solution.py:385
  132.7 10.1 %collective-permute-done.16.refs_4_ = bf16[64,1024]{1,0:T(8,128)(2,1)S(1)} collective-permute-done((bf16[64,1024]{1,0:T(8,128)(2,1)S(1)}, bf16[64,1024]{1,0:T(8,128)(2,1)S(1)}, u32[]{:S(2)}, u32[]{:S(2)}) %collective-permute-start.16) | collective-permute-done | bytes 131104 | tf_op jit(solution)/shard_map/ppermute | solution.py:385
  142.8 0.1 reduce_sum.35
  142.9 0.7 broadcast_in_dim.27
  143.6 4.6 %all-to-all-start.5 = ((f32[64,8,128]{2,1,0:T(8,128)}), f32[64,8,128]{2,1,0:T(8,128)S(1)}, u32[]{:S(2)}, u32[]{:S(2)}) async-start(f32[64,8,128]{2,1,0:T(8,128)} %broadcast_in_dim.27), calls=%async_computation.5 | async-start | bytes 524288 | tf_op jit(solution)/shard_map/all_to_all | solution.py:376
  148.2 0.1 collective-permute-start.18
  148.3 0.5 collective-permute-start.19
  148.8 1.2 collective-permute-done.19.refs_5_
  150.0 7.0 %input_conv.1 = bf16[128,1024]{1,0:T(8,128)(2,1)} custom-call(s32[8]{0:T(128)S(1)} %compare_select_fusion.4.place_ref, s32[256]{0:T(256)S(1)} %copy-done.5, bf16[128,1024]{1,0:T(8,128)(2,1)S(1)} %get-tuple-element.57.refs_0_, bf16[128,1024]{1,0:T(8,128)(2,1)S(1)} %collective-permute-done.17.refs_1_, bf16[128,1024]{1,0:T(8,128)(2,1)S(1)} %collective-permute-done.15.refs_2_, ...), custom_call_target="tpu_custom_call" | custom-call | flops 1048576 | bytes 1048576 | tf_op jit(solution)/shard_map/input_conv/pallas_call | solution.py:355
  157.0 4.4 %all-to-all-done.5 = f32[64,8,128]{2,1,0:T(8,128)S(1)} async-done(((f32[64,8,128]{2,1,0:T(8,128)}), f32[64,8,128]{2,1,0:T(8,128)S(1)}, u32[]{:S(2)}, u32[]{:S(2)}) %all-to-all-start.5) | async-done | bytes 262176 | tf_op jit(solution)/shard_map/all_to_all | solution.py:376
  161.4 1.5 collective-permute-done.20
  162.9 0.8 pad_maximum_fusion
  (27 shorter events, 0.2 us)
Async XLA Ops:
  0.6 16.4 %copy-start.1 = (bf16[3,2048,128]{2,1,0:T(8,128)(2,1)S(1)}, bf16[3,2048,128]{2,1,0:T(8,128)(2,1)}, u32[]{:S(2)}) copy-start(bf16[3,2048,128]{2,1,0:T(8,128)(2,1)} %w_own.1) | copy-start | bytes 4718596
  2.4 10.9 %collective-permute-start = (bf16[128,256]{1,0:T(8,128)(2,1)}, bf16[128,256]{1,0:T(8,128)(2,1)S(1)}, u32[]{:S(2)}, u32[]{:S(2)}) collective-permute-start(bf16[128,256]{1,0:T(8,128)(2,1)} %get-tuple-element.36), channel_id=1, source_target_pairs={{0,128},{128,0},{1,129},{129,1},{2,130},{130,2},{3,131},{131,3},{4... | collective-permute-start | bytes 196616 | tf_op jit(solution)/shard_map/ppermute | solution.py:380
  3.3 14.7 %copy-start.5 = (s32[256]{0:T(256)S(1)}, s32[256]{0:T(256)}, u32[]{:S(2)}) copy-start(s32[256]{0:T(256)} %order_ref.7) | copy-start | bytes 3076
  3.3 27.4 %all-to-all-start = ((bf16[8,128,256]{2,1,0:T(8,128)(2,1)}), bf16[8,128,256]{2,1,0:T(8,128)(2,1)S(1)}, u32[]{:S(2)}, u32[]{:S(2)}) async-start(bf16[8,128,256]{2,1,0:T(8,128)(2,1)} %get-tuple-element.35), calls=%async_computation | async-start | bytes 1048576 | tf_op jit(solution)/shard_map/all_to_all | solution.py:403
  13.4 15.2 %copy-start.2 = (bf16[128,1024]{1,0:T(8,128)(2,1)S(1)}, bf16[128,1024]{1,0:T(8,128)(2,1)}, u32[]{:S(2)}) copy-start(bf16[128,1024]{1,0:T(8,128)(2,1)} %refs_0_.1) | copy-start | bytes 786436
  14.0 8.7 %collective-permute-start.1 = (bf16[256,256]{1,0:T(8,128)(2,1)}, bf16[256,256]{1,0:T(8,128)(2,1)S(1)}, u32[]{:S(2)}, u32[]{:S(2)}) collective-permute-start(bf16[256,256]{1,0:T(8,128)(2,1)} %get-tuple-element.78), channel_id=1, source_target_pairs={{32,0},{64,32},{96,64},{0,96},{33,1},{65,33},{97,65},{1,97},{34,2}... | collective-permute-start | bytes 393224 | tf_op jit(solution)/shard_map/ppermute | solution.py:389
  18.1 8.2 %collective-permute-start.2 = (bf16[256,256]{1,0:T(8,128)(2,1)}, bf16[256,256]{1,0:T(8,128)(2,1)}, u32[]{:S(2)}, u32[]{:S(2)}) collective-permute-start(bf16[256,256]{1,0:T(8,128)(2,1)} %get-tuple-element.78), channel_id=1, source_target_pairs={{64,0},{96,32},{0,64},{32,96},{65,1},{97,33},{1,65},{33,97},{66,2}... | collective-permute-start | bytes 393224 | tf_op jit(solution)/shard_map/ppermute | solution.py:389
  20.6 7.2 %collective-permute-start.3 = (bf16[256,256]{1,0:T(8,128)(2,1)}, bf16[256,256]{1,0:T(8,128)(2,1)S(1)}, u32[]{:S(2)}, u32[]{:S(2)}) collective-permute-start(bf16[256,256]{1,0:T(8,128)(2,1)} %get-tuple-element.78), channel_id=1, source_target_pairs={{96,0},{0,32},{32,64},{64,96},{97,1},{1,33},{33,65},{65,97},{98,2}... | collective-permute-start | bytes 393224 | tf_op jit(solution)/shard_map/ppermute | solution.py:389
  28.5 2.1 %collective-permute-start.4 = (bf16[1024,256]{1,0:T(8,128)(2,1)}, bf16[1024,256]{1,0:T(8,128)(2,1)S(1)}, u32[]{:S(2)}, u32[]{:S(2)}) collective-permute-start(bf16[1024,256]{1,0:T(8,128)(2,1)} %get-tuple-element.70), channel_id=1, source_target_pairs={{0,2},{2,0},{1,3},{3,1},{4,6},{6,4},{5,7},{7,5},{8,10},{10,8},{9,1... | collective-permute-start | bytes 1572872 | tf_op jit(solution)/shard_map/ppermute | solution.py:380
  29.2 21.8 %collective-permute-start.5 = (bf16[3,1024,128]{2,1,0:T(8,128)(2,1)}, bf16[3,1024,128]{2,1,0:T(8,128)(2,1)}, u32[]{:S(2)}, u32[]{:S(2)}) collective-permute-start(bf16[3,1024,128]{2,1,0:T(8,128)(2,1)} %constant_dynamic-slice_fusion.1), channel_id=1, source_target_pairs={{0,1},{1,0},{2,3},{3,2},{4,5},{5,4},{6,7},{7,6},{8,9},{9,8},{10,11... | collective-permute-start | bytes 2359304 | tf_op jit(solution)/shard_map/ppermute | solution.py:380
  30.7 5.3 %copy-start.3 = (bf16[2048,256]{1,0:T(8,128)(2,1)}, bf16[2048,256]{1,0:T(8,128)(2,1)S(1)}, u32[]{:S(2)}) copy-start(bf16[2048,256]{1,0:T(8,128)(2,1)S(1)} %constant_dynamic-update-slice_fusion.7.k_ref.v_ref) | copy-start | bytes 3145732
  36.0 15.4 %all-to-all-start.1 = ((f32[8,2,1024]{2,1,0:T(2,128)}), f32[8,2,1024]{2,1,0:T(2,128)S(1)}, u32[]{:S(2)}, u32[]{:S(2)}) async-start(f32[8,2,1024]{2,1,0:T(2,128)} %attention_stats.1), calls=%async_computation.1 | async-start | bytes 131072 | tf_op jit(solution)/shard_map/all_to_all | solution.py:418
  51.4 1.2 copy-start.4
  60.3 16.7 %collective-permute-start.6 = (f32[1024,256]{1,0:T(8,128)}, f32[1024,256]{1,0:T(8,128)}, u32[]{:S(2)}, u32[]{:S(2)}) collective-permute-start(f32[1024,256]{1,0:T(8,128)} %get-tuple-element.43), channel_id=1, source_target_pairs={{0,2},{2,0},{1,3},{3,1},{4,6},{6,4},{5,7},{7,5},{8,10},{10,8},{9,1... | collective-permute-start | bytes 3145736 | tf_op jit(solution)/shard_map/ppermute | solution.py:380
  60.3 22.8 %all-to-all-start.2 = ((bf16[8,128,128]{2,1,0:T(8,128)(2,1)}), bf16[8,128,128]{2,1,0:T(8,128)(2,1)S(1)}, u32[]{:S(2)}, u32[]{:S(2)}) async-start(bf16[8,128,128]{2,1,0:T(8,128)(2,1)} %bitcast.2), calls=%async_computation.2 | async-start | bytes 524288 | tf_op jit(solution)/shard_map/all_to_all | solution.py:424
  66.9 16.2 %collective-permute-start.7 = (bf16[128,1024]{1,0:T(8,128)(2,1)S(1)}, bf16[128,1024]{1,0:T(8,128)(2,1)S(1)}, u32[]{:S(2)}, u32[]{:S(2)}) collective-permute-start(bf16[128,1024]{1,0:T(8,128)(2,1)S(1)} %copy-done.2), channel_id=1, source_target_pairs={{0,4},{2,6},{4,8},{6,10},{8,12},{10,14},{12,16},{14,18},{16,20},{1... | collective-permute-start | bytes 786440 | tf_op jit(solution)/shard_map/ppermute | solution.py:385
  70.9 9.3 %collective-permute-start.8 = (bf16[64,1024]{1,0:T(8,128)(2,1)}, bf16[64,1024]{1,0:T(8,128)(2,1)S(1)}, u32[]{:S(2)}, u32[]{:S(2)}) collective-permute-start(bf16[64,1024]{1,0:T(8,128)(2,1)} %constant_dynamic-slice_fusion), channel_id=1, source_target_pairs={{4,0},{6,2},{8,4},{10,6},{12,8},{14,10},{16,12},{18,14},{20,16},{2... | collective-permute-start | bytes 393224 | tf_op jit(solution)/shard_map/ppermute | solution.py:385
  83.2 12.1 %all-to-all-start.3 = ((bf16[8,128,256]{2,1,0:T(8,128)(2,1)}), bf16[8,128,256]{2,1,0:T(8,128)(2,1)}, u32[]{:S(2)}, u32[]{:S(2)}) async-start(bf16[8,128,256]{2,1,0:T(8,128)(2,1)} %bitcast.19), calls=%async_computation.3 | async-start | bytes 1048576 | tf_op jit(solution)/shard_map/all_to_all | solution.py:427
  87.3 2.2 %collective-permute-start.10 = (bf16[128,1024]{1,0:T(8,128)(2,1)S(1)}, bf16[128,1024]{1,0:T(8,128)(2,1)S(1)}, u32[]{:S(2)}, u32[]{:S(2)}) collective-permute-start(bf16[128,1024]{1,0:T(8,128)(2,1)S(1)} %collective-permute-done.7.refs_2_), channel_id=1, source_target_pairs={{0,2},{2,0},{1,3},{3,1},{4,6},{6,4},{5,7},{7,5},{8,10},{10,8},{9,1... | collective-permute-start | bytes 786440 | tf_op jit(solution)/shard_map/ppermute | solution.py:380
  87.4 2.1 %collective-permute-start.9 = (bf16[128,1024]{1,0:T(8,128)(2,1)S(1)}, bf16[128,1024]{1,0:T(8,128)(2,1)S(1)}, u32[]{:S(2)}, u32[]{:S(2)}) collective-permute-start(bf16[128,1024]{1,0:T(8,128)(2,1)S(1)} %copy-done.2), channel_id=1, source_target_pairs={{0,2},{2,0},{1,3},{3,1},{4,6},{6,4},{5,7},{7,5},{8,10},{10,8},{9,1... | collective-permute-start | bytes 786440 | tf_op jit(solution)/shard_map/ppermute | solution.py:380
  87.9 1.6 collective-permute-start.11
  96.4 6.9 %collective-permute-start.13 = (bf16[128,256]{1,0:T(8,128)(2,1)S(1)}, bf16[128,256]{1,0:T(8,128)(2,1)S(1)}, u32[]{:S(2)}, u32[]{:S(2)}) collective-permute-start(bf16[128,256]{1,0:T(8,128)(2,1)S(1)} %reduce_sum.34.kv_own), channel_id=1, source_target_pairs={{0,1},{1,0},{2,3},{3,2},{4,5},{5,4},{6,7},{7,6},{8,9},{9,8},{10,11... | collective-permute-start | bytes 196616 | tf_op jit(solution)/shard_map/ppermute | solution.py:380
  97.8 5.5 %collective-permute-start.12 = (bf16[128,128]{1,0:T(8,128)(2,1)S(1)}, bf16[128,128]{1,0:T(8,128)(2,1)S(1)}, u32[]{:S(2)}, u32[]{:S(2)}) collective-permute-start(bf16[128,128]{1,0:T(8,128)(2,1)S(1)} %reduce_sum.33.q_own), channel_id=1, source_target_pairs={{0,1},{1,0},{2,3},{3,2},{4,5},{5,4},{6,7},{7,6},{8,9},{9,8},{10,11... | collective-permute-start | bytes 98312 | tf_op jit(solution)/shard_map/ppermute | solution.py:380
  112.2 37.9 %copy-start = (f32[1024,128]{1,0:T(8,128)S(1)}, f32[1024,128]{1,0:T(8,128)}, u32[]{:S(2)}) copy-start(f32[1024,128]{1,0:T(8,128)} %refs_6_.1) | copy-start | bytes 1572868
  112.2 1.6 collective-permute-start.14
  114.5 28.3 %all-to-all-start.4 = ((f32[64,8,128]{2,1,0:T(8,128)}), f32[64,8,128]{2,1,0:T(8,128)S(1)}, u32[]{:S(2)}, u32[]{:S(2)}) async-start(f32[64,8,128]{2,1,0:T(8,128)} %fusion), calls=%async_computation.4 | async-start | bytes 524288 | tf_op jit(solution)/shard_map/all_to_all | solution.py:443
  124.0 18.8 %collective-permute-start.15 = (bf16[128,1024]{1,0:T(8,128)(2,1)S(1)}, bf16[128,1024]{1,0:T(8,128)(2,1)S(1)}, u32[]{:S(2)}, u32[]{:S(2)}) collective-permute-start(bf16[128,1024]{1,0:T(8,128)(2,1)S(1)} %get-tuple-element.57.refs_0_), channel_id=1, source_target_pairs={{4,0},{6,2},{8,4},{10,6},{12,8},{14,10},{16,12},{18,14},{20,16},{2... | collective-permute-start | bytes 786440 | tf_op jit(solution)/shard_map/ppermute | solution.py:385
  130.7 12.1 %collective-permute-start.17 = (bf16[128,1024]{1,0:T(8,128)(2,1)S(1)}, bf16[128,1024]{1,0:T(8,128)(2,1)S(1)}, u32[]{:S(2)}, u32[]{:S(2)}) collective-permute-start(bf16[128,1024]{1,0:T(8,128)(2,1)S(1)} %get-tuple-element.57.refs_0_), channel_id=1, source_target_pairs={{0,2},{2,0},{1,3},{3,1},{4,6},{6,4},{5,7},{7,5},{8,10},{10,8},{9,1... | collective-permute-start | bytes 786440 | tf_op jit(solution)/shard_map/ppermute | solution.py:380
  130.8 12.0 %collective-permute-start.16 = (bf16[64,1024]{1,0:T(8,128)(2,1)S(1)}, bf16[64,1024]{1,0:T(8,128)(2,1)S(1)}, u32[]{:S(2)}, u32[]{:S(2)}) collective-permute-start(bf16[64,1024]{1,0:T(8,128)(2,1)S(1)} %get-tuple-element.58), channel_id=1, source_target_pairs={{0,4},{2,6},{4,8},{6,10},{8,12},{10,14},{12,16},{14,18},{16,20},{1... | collective-permute-start | bytes 393224 | tf_op jit(solution)/shard_map/ppermute | solution.py:385
  143.6 17.8 %all-to-all-start.5 = ((f32[64,8,128]{2,1,0:T(8,128)}), f32[64,8,128]{2,1,0:T(8,128)S(1)}, u32[]{:S(2)}, u32[]{:S(2)}) async-start(f32[64,8,128]{2,1,0:T(8,128)} %broadcast_in_dim.27), calls=%async_computation.5 | async-start | bytes 524288 | tf_op jit(solution)/shard_map/all_to_all | solution.py:376
  148.2 1.8 %collective-permute-start.18 = (bf16[128,1024]{1,0:T(8,128)(2,1)S(1)}, bf16[128,1024]{1,0:T(8,128)(2,1)S(1)}, u32[]{:S(2)}, u32[]{:S(2)}) collective-permute-start(bf16[128,1024]{1,0:T(8,128)(2,1)S(1)} %collective-permute-done.15.refs_2_), channel_id=1, source_target_pairs={{0,2},{2,0},{1,3},{3,1},{4,6},{6,4},{5,7},{7,5},{8,10},{10,8},{9,1... | collective-permute-start | bytes 786440 | tf_op jit(solution)/shard_map/ppermute | solution.py:380
  148.3 1.7 %collective-permute-start.19 = (bf16[64,1024]{1,0:T(8,128)(2,1)S(1)}, bf16[64,1024]{1,0:T(8,128)(2,1)S(1)}, u32[]{:S(2)}, u32[]{:S(2)}) collective-permute-start(bf16[64,1024]{1,0:T(8,128)(2,1)S(1)} %collective-permute-done.16.refs_4_), channel_id=1, source_target_pairs={{0,2},{2,0},{1,3},{3,1},{4,6},{6,4},{5,7},{7,5},{8,10},{10,8},{9,1... | collective-permute-start | bytes 393224 | tf_op jit(solution)/shard_map/ppermute | solution.py:380
  161.4 1.5 collective-permute-start.20

commit v5 on v4

--- a/solution.py
+++ b/solution.py
@@ -151,7 +151,7 @@
             scratch_shapes=[pltpu.VMEM((NK, LANES), jnp.int32)],
         ),
         out_shape=jax.ShapeDtypeStruct((Z, 2, NQ), F32),
-        compiler_params=pltpu.CompilerParams(vmem_limit_bytes=40 << 20),
+        compiler_params=pltpu.CompilerParams(vmem_limit_bytes=56 << 20),
         cost_estimate=pl.CostEstimate(flops=4 * NQ * NK * HD, bytes_accessed=4 << 20, transcendentals=NQ * NK),
         name="attention_stats",
     )(place, order, qg, qg, kv, kv)
@@ -177,7 +177,7 @@
             jax.ShapeDtypeStruct((NK // 2, 2 * HD), F32),
             jax.ShapeDtypeStruct((NK // 2, 2 * HD), F32),
         ],
-        compiler_params=pltpu.CompilerParams(vmem_limit_bytes=40 << 20),
+        compiler_params=pltpu.CompilerParams(vmem_limit_bytes=56 << 20),
         cost_estimate=pl.CostEstimate(flops=10 * NQ * NK * HD, bytes_accessed=4 << 20, transcendentals=NQ * NK),
         name="attention_grads",
     )(place, order, qg, qg, kv, kv, stats)
@@ -320,7 +320,7 @@
             jax.ShapeDtypeStruct((BLK, channels), BF),
             jax.ShapeDtypeStruct((2, channels // 2, TAPS), F32),
         ],
-        compiler_params=pltpu.CompilerParams(vmem_limit_bytes=40 << 20),
+        compiler_params=pltpu.CompilerParams(vmem_limit_bytes=56 << 20),
         cost_estimate=pl.CostEstimate(flops=4 << 30, bytes_accessed=8 << 20, transcendentals=0),
         name="project_and_filter",
     )(place, order, q_own, kv_own, q_other, kv_other, weight, w_other, *ins)
@@ -366,7 +366,7 @@
             ],
         ),
         out_shape=jax.ShapeDtypeStruct((ROWS, channels), BF),
-        compiler_params=pltpu.CompilerParams(vmem_limit_bytes=40 << 20),
+        compiler_params=pltpu.CompilerParams(vmem_limit_bytes=56 << 20),
         cost_estimate=pl.CostEstimate(flops=1 << 20, bytes_accessed=1 << 20, transcendentals=0),
         name="input_conv",
     )(place, order, *grads, taps)

time: 167 us -> 170 us (1.018)
  Pallas kernels: 30.6 us -> 35.8 us
  starting transfers between devices: 70.9 us -> 66.6 us
  local copies, waits for them, and re-layouts: 9.39 us -> 11.7 us
    all_to_all x1, waiting for transfers between devices: 0.43 us -> 3.93 us  [local(): stats = lax.all_to_all(stats, 'z', 0, 0, tiled=True)]
    all_to_all x1, starting transfers between devices: 6.6 us -> 3.42 us  [local(): dq_parts = lax.all_to_all(dq.reshape(Z, ROWS, HD), 'z', 0, 0, tiled=True)]
    all_to_all x1, waiting for transfers between devices: 4.39 us -> 1.57 us  [to_all(): lax.all_to_all(jnp.broadcast_to(x[None], (count,) + x.shape), axes, 0, 0,...]
    ppermute x14, waiting for transfers between devices: 17.2 us -> 14.9 us  [swap(): return lax.ppermute(x, axis, [(0, 1), (1, 0)])]
    unnamed x16 -> x48, local copies, waits for them, and re-layouts: 5.67 us -> 7.61 us
    pallas_call x1, Pallas kernels: 7.71 us -> 9.43 us  [attention_grads(): pl.pallas_call(grads_kernel, grid_spec=pltpu.PrefetchScalarGridSpec(num_s...]
  transfers between devices with their start and end apart: 27 -> 27, of which waited for: 15 -> 16; matrix products, arithmetic and copies ran while one was open for 6% -> 5% of each run, Pallas kernels for 7% -> 9%
where the time goes in v5:
time: 170 us; the launch traced here: 167 us
  starting transfers between devices  66.6 us (39%)
  waiting for transfers between devices  45.2 us (27%)
  Pallas kernels  35.8 us (21%)
  local copies, waits for them, and re-layouts  11.7 us (7%)
  other arithmetic  5.46 us (3%)
  between operations  2.31 us (1%)
    ppermute x4, starting transfers between devices, from_ctx(): lax.ppermute(x, CTX, [(i + distance, i) for i in range(n) if 0 <= i + dis...  18.7 us
    ppermute x14, waiting for transfers between devices, swap(): return lax.ppermute(x, axis, [(0, 1), (1, 0)])  14.9 us
    ppermute x4, waiting for transfers between devices, from_ctx(): lax.ppermute(x, CTX, [(i + distance, i) for i in range(n) if 0 <= i + dis...  14.2 us
    pallas_call x1, Pallas kernels, project_and_filter(): pl.pallas_call(functools.partial(filter_kernel, len(ins)), grid_spec=pltp...  9.76 us
    pallas_call x1, Pallas kernels, attention_grads(): pl.pallas_call(grads_kernel, grid_spec=pltpu.PrefetchScalarGridSpec(num_s...  9.43 us
    all_to_all x1, starting transfers between devices, local(): lax.all_to_all(mine_sum.reshape(chips, channels // 2 // chips, TAPS), ('x...  9.01 us
    all_to_all x1, starting transfers between devices, local(): qg = lax.all_to_all(qg, 'z', 0, 0, tiled=True).reshape(NQ, 2 * HD)  8.6 us
    pallas_call x1, Pallas kernels, input_conv(): pl.pallas_call(functools.partial(conv_kernel, len(grads)), grid_spec=pltp...  8.43 us
  transfers between devices with their start and end apart: 27, of which 16 were waited for; matrix products, arithmetic and copies ran while one was open for 5% of the time, Pallas kernels for 9%

profile of v5, /device:TPU:6, one launch (start us, length us, event | category | flops | bytes accessed | tf_op | source)
XLA Modules:
  0.0 167.1 jit_solution(2745026206250201536)
XLA Ops:
  0.6 1.8 %pack.1 = (bf16[8,128,256]{2,1,0:T(8,128)(2,1)}, bf16[128,256]{1,0:T(8,128)(2,1)}) custom-call(bf16[128,128]{1,0:T(8,128)(2,1)} %q_ref.1, bf16[128,128]{1,0:T(8,128)(2,1)} %g_ref.1, bf16[128,128]{1,0:T(8,128)(2,1)} %k_ref.1, bf16[128,128]{1,0:T(8,128)(2,1)} %v_ref.1), custom_call_target="tpu_custom_call" | custom-call | tf_op jit(solution)/shard_map/pack/pallas_call | solution.py:195
  2.4 0.8 collective-permute-start
  3.3 8.6 %all-to-all-start = ((bf16[8,128,256]{2,1,0:T(8,128)(2,1)}), bf16[8,128,256]{2,1,0:T(8,128)(2,1)S(1)}, u32[]{:S(2)}, u32[]{:S(2)}) async-start(bf16[8,128,256]{2,1,0:T(8,128)(2,1)} %get-tuple-element.35), calls=%async_computation | async-start | bytes 1048576 | tf_op jit(solution)/shard_map/all_to_all | solution.py:403
  11.9 1.5 constant_dynamic-update-slice_fusion.6
  13.4 0.7 constant_dynamic-update-slice_fusion.5
  14.1 3.0 %collective-permute-start.1 = (bf16[256,256]{1,0:T(8,128)(2,1)S(1)}, bf16[256,256]{1,0:T(8,128)(2,1)S(1)}, u32[]{:S(2)}, u32[]{:S(2)}) collective-permute-start(bf16[256,256]{1,0:T(8,128)(2,1)S(1)} %get-tuple-element.78), channel_id=1, source_target_pairs={{32,0},{64,32},{96,64},{0,96},{33,1},{65,33},{97,65},{1,97},{34,2}... | collective-permute-start | bytes 393224 | tf_op jit(solution)/shard_map/ppermute | solution.py:389
  17.2 0.1 dynamic_slice.10
  17.3 0.7 collective-permute-start.2
  17.9 0.6 fusion.1
  19.8 1.0 collective-permute-start.3
  20.9 1.2 collective-permute-done.1
  22.1 0.7 constant_dynamic-update-slice_fusion.4
  22.8 2.3 %collective-permute-done.2 = bf16[256,256]{1,0:T(8,128)(2,1)S(1)} collective-permute-done((bf16[256,256]{1,0:T(8,128)(2,1)S(1)}, bf16[256,256]{1,0:T(8,128)(2,1)S(1)}, u32[]{:S(2)}, u32[]{:S(2)}) %collective-permute-start.2) | collective-permute-done | bytes 131104 | tf_op jit(solution)/shard_map/ppermute | solution.py:389
  25.1 0.7 constant_dynamic-update-slice_fusion.3
  25.8 0.7 collective-permute-done.3
  26.6 0.7 constant_dynamic-update-slice_fusion.2
  27.3 1.2 collective-permute-start.5
  28.5 0.6 compare_select_fusion.4.place_ref
  29.1 0.3 collective-permute-done.4
  29.4 0.8 constant_dynamic-update-slice_fusion.7.k_ref.v_ref
  30.3 0.8 copy-done
  31.1 6.4 %attention_stats.1 = f32[8,2,1024]{2,1,0:T(2,128)} custom-call(s32[8]{0:T(128)} %compare_select_fusion.4.place_ref, s32[256]{0:T(256)} %order_ref.7, bf16[1024,256]{1,0:T(8,128)(2,1)} %bitcast.16, bf16[1024,256]{1,0:T(8,128)(2,1)} %bitcast.17, bf16[2048,256]{1,0:T(8,128)(2,1)} %constant_dynamic-update-slice_fusion.7.k_ref.v_ref, ...), custom_call_target="tpu_custom_call" | custom-call | flops 1073741824 | bytes 4194304 | tf_op jit(solution)/shard_map/attention_stats/pallas_call | solution.py:144
  37.4 7.0 %all-to-all-start.1 = ((f32[8,2,1024]{2,1,0:T(2,128)}), f32[8,2,1024]{2,1,0:T(2,128)S(1)}, u32[]{:S(2)}, u32[]{:S(2)}) async-start(f32[8,2,1024]{2,1,0:T(2,128)} %attention_stats.1), calls=%async_computation.1 | async-start | bytes 131072 | tf_op jit(solution)/shard_map/all_to_all | solution.py:418
  44.4 4.4 %collective-permute-done.5.w_other = bf16[3,1024,128]{2,1,0:T(8,128)(2,1)S(1)} collective-permute-done((bf16[3,1024,128]{2,1,0:T(8,128)(2,1)S(1)}, bf16[3,1024,128]{2,1,0:T(8,128)(2,1)S(1)}, u32[]{:S(2)}, u32[]{:S(2)}) %collective-permute-start.5) | collective-permute-done | bytes 786464 | tf_op jit(solution)/shard_map/ppermute | solution.py:380
  48.9 3.9 %all-to-all-done.1.stat_ref = f32[8,2,1024]{2,1,0:T(2,128)S(1)} async-done(((f32[8,2,1024]{2,1,0:T(2,128)}), f32[8,2,1024]{2,1,0:T(2,128)S(1)}, u32[]{:S(2)}, u32[]{:S(2)}) %all-to-all-start.1) | async-done | bytes 65568 | tf_op jit(solution)/shard_map/all_to_all | solution.py:418
  52.8 0.6 copy-done.9
  53.4 9.4 %attention_grads.1 = (bf16[1024,128]{1,0:T(8,128)(2,1)}, f32[1024,256]{1,0:T(8,128)}, f32[1024,256]{1,0:T(8,128)}) custom-call(s32[8]{0:T(128)} %compare_select_fusion.4.place_ref, s32[256]{0:T(256)} %order_ref.7, bf16[1024,256]{1,0:T(8,128)(2,1)} %bitcast.18, bf16[1024,256]{1,0:T(8,128)(2,1)} %bitcast.19, ...), custom_call_target="tpu_custom_call" | custom-call | flops 2684354560 | bytes 4194304 | tf_op jit(solution)/shard_map/attention_grads/pallas_call | solution.py:162
  62.9 3.4 %all-to-all-start.2 = ((bf16[8,128,128]{2,1,0:T(8,128)(2,1)}), bf16[8,128,128]{2,1,0:T(8,128)(2,1)S(1)}, u32[]{:S(2)}, u32[]{:S(2)}) async-start(bf16[8,128,128]{2,1,0:T(8,128)(2,1)} %bitcast.20), calls=%async_computation.2 | async-start | bytes 524288 | tf_op jit(solution)/shard_map/all_to_all | solution.py:424
  66.3 3.8 %collective-permute-start.7 = (bf16[128,1024]{1,0:T(8,128)(2,1)S(1)}, bf16[128,1024]{1,0:T(8,128)(2,1)S(1)}, u32[]{:S(2)}, u32[]{:S(2)}) collective-permute-start(bf16[128,1024]{1,0:T(8,128)(2,1)S(1)} %copy-done.8), channel_id=1, source_target_pairs={{0,4},{2,6},{4,8},{6,10},{8,12},{10,14},{12,16},{14,18},{16,20},{1... | collective-permute-start | bytes 786440 | tf_op jit(solution)/shard_map/ppermute | solution.py:385
  70.1 6.2 %collective-permute-start.8 = (bf16[64,1024]{1,0:T(8,128)(2,1)S(1)}, bf16[64,1024]{1,0:T(8,128)(2,1)S(1)}, u32[]{:S(2)}, u32[]{:S(2)}) collective-permute-start(bf16[64,1024]{1,0:T(8,128)(2,1)S(1)} %constant_dynamic-slice_fusion), channel_id=1, source_target_pairs={{4,0},{6,2},{8,4},{10,6},{12,8},{14,10},{16,12},{18,14},{20,16},{2... | collective-permute-start | bytes 393224 | tf_op jit(solution)/shard_map/ppermute | solution.py:385
  76.4 2.1 %add_convert_fusion = bf16[1024,256]{1,0:T(8,128)(2,1)} fusion(f32[1024,256]{1,0:T(8,128)} %get-tuple-element.42, f32[1024,256]{1,0:T(8,128)S(1)} %collective-permute-done.6), kind=kLoop, calls=%fused_computation | loop fusion | flops 524288 | bytes 2621440 | tf_op jit(solution)/shard_map/convert_element_type | solution.py:425
  78.5 1.0 collective-permute-done.8.refs_4_
  79.5 3.2 %collective-permute-done.7.refs_2_ = bf16[128,1024]{1,0:T(8,128)(2,1)S(1)} collective-permute-done((bf16[128,1024]{1,0:T(8,128)(2,1)S(1)}, bf16[128,1024]{1,0:T(8,128)(2,1)S(1)}, u32[]{:S(2)}, u32[]{:S(2)}) %collective-permute-start.7) | collective-permute-done | bytes 262176 | tf_op jit(solution)/shard_map/ppermute | solution.py:385
  82.7 3.5 %all-to-all-start.3 = ((bf16[8,128,256]{2,1,0:T(8,128)(2,1)}), bf16[8,128,256]{2,1,0:T(8,128)(2,1)S(1)}, u32[]{:S(2)}, u32[]{:S(2)}) async-start(bf16[8,128,256]{2,1,0:T(8,128)(2,1)} %bitcast.3), calls=%async_computation.3 | async-start | bytes 1048576 | tf_op jit(solution)/shard_map/all_to_all | solution.py:427
  86.2 0.5 collective-permute-start.9
  86.7 0.1 collective-permute-start.11
  86.8 1.5 collective-permute-done.11.refs_5_
  88.3 6.4 %all-to-all-done.3 = bf16[8,128,256]{2,1,0:T(8,128)(2,1)S(1)} async-done(((bf16[8,128,256]{2,1,0:T(8,128)(2,1)}), bf16[8,128,256]{2,1,0:T(8,128)(2,1)S(1)}, u32[]{:S(2)}, u32[]{:S(2)}) %all-to-all-start.3) | async-done | bytes 524320 | tf_op jit(solution)/shard_map/all_to_all | solution.py:427
  94.8 2.6 %collective-permute-start.13 = (bf16[128,256]{1,0:T(8,128)(2,1)S(1)}, bf16[128,256]{1,0:T(8,128)(2,1)S(1)}, u32[]{:S(2)}, u32[]{:S(2)}) collective-permute-start(bf16[128,256]{1,0:T(8,128)(2,1)S(1)} %reduce_sum.34.kv_own), channel_id=1, source_target_pairs={{0,1},{1,0},{2,3},{3,2},{4,5},{5,4},{6,7},{7,6},{8,9},{9,8},{10,11... | collective-permute-start | bytes 196616 | tf_op jit(solution)/shard_map/ppermute | solution.py:380
  97.4 1.1 collective-permute-start.12
  98.5 4.4 %collective-permute-done.12.q_other = bf16[128,128]{1,0:T(8,128)(2,1)S(1)} collective-permute-done((bf16[128,128]{1,0:T(8,128)(2,1)S(1)}, bf16[128,128]{1,0:T(8,128)(2,1)S(1)}, u32[]{:S(2)}, u32[]{:S(2)}) %collective-permute-start.12) | collective-permute-done | bytes 32800 | tf_op jit(solution)/shard_map/ppermute | solution.py:380
  103.0 0.5 copy-done.21
  103.5 0.6 copy-done.20
  104.2 9.8 %project_and_filter.1 = (bf16[128,1024]{1,0:T(8,128)(2,1)}, bf16[64,1024]{1,0:T(8,128)(2,1)}, f32[2,512,128]{2,1,0:T(8,128)}) custom-call(s32[8]{0:T(128)} %compare_select_fusion.4.place_ref, s32[256]{0:T(256)} %order_ref.7, bf16[128,128]{1,0:T(8,128)(2,1)} %copy-done.11, bf16[128,256]{1,0:T(8,128)(2,1)} %copy-done.10, bf16[128,128]{1,0:T(8,128)(2,1)} %copy-done.21, ...), custom_call_target="tpu_custom_call" | custom-call | flops 4294967296 | bytes 8388608 | tf_op jit(solution)/shard_map/project_and_filter/pallas_call | solution.py:298
  113.9 1.0 slice_bitcast_fusion
  115.0 0.1 collective-permute-start.14
  115.1 1.5 collective-permute-done.14
  116.6 1.7 %fusion = f32[64,8,128]{2,1,0:T(8,128)} fusion(f32[512,128]{1,0:T(8,128)S(1)} %collective-permute-done.14, f32[2,512,128]{2,1,0:T(8,128)} %get-tuple-element.56), kind=kLoop, calls=%fused_computation.3 | loop fusion | flops 65536 | bytes 786432 | tf_op jit(solution)/shard_map/reshape | solution.py:444
  118.3 9.0 %all-to-all-start.4 = ((f32[64,8,128]{2,1,0:T(8,128)}), f32[64,8,128]{2,1,0:T(8,128)S(1)}, u32[]{:S(2)}, u32[]{:S(2)}) async-start(f32[64,8,128]{2,1,0:T(8,128)} %fusion), calls=%async_computation.4 | async-start | bytes 524288 | tf_op jit(solution)/shard_map/all_to_all | solution.py:443
  127.3 6.7 %collective-permute-start.15 = (bf16[128,1024]{1,0:T(8,128)(2,1)S(1)}, bf16[128,1024]{1,0:T(8,128)(2,1)S(1)}, u32[]{:S(2)}, u32[]{:S(2)}) collective-permute-start(bf16[128,1024]{1,0:T(8,128)(2,1)S(1)} %copy-done.2), channel_id=1, source_target_pairs={{4,0},{6,2},{8,4},{10,6},{12,8},{14,10},{16,12},{18,14},{20,16},{2... | collective-permute-start | bytes 786440 | tf_op jit(solution)/shard_map/ppermute | solution.py:385
  134.0 0.1 collective-permute-start.17
  134.1 1.9 %collective-permute-start.16 = (bf16[64,1024]{1,0:T(8,128)(2,1)S(1)}, bf16[64,1024]{1,0:T(8,128)(2,1)S(1)}, u32[]{:S(2)}, u32[]{:S(2)}) collective-permute-start(bf16[64,1024]{1,0:T(8,128)(2,1)S(1)} %copy-done.19), channel_id=1, source_target_pairs={{0,4},{2,6},{4,8},{6,10},{8,12},{10,14},{12,16},{14,18},{16,20},{1... | collective-permute-start | bytes 393224 | tf_op jit(solution)/shard_map/ppermute | solution.py:385
  136.0 10.1 %collective-permute-done.16.refs_4_ = bf16[64,1024]{1,0:T(8,128)(2,1)S(1)} collective-permute-done((bf16[64,1024]{1,0:T(8,128)(2,1)S(1)}, bf16[64,1024]{1,0:T(8,128)(2,1)S(1)}, u32[]{:S(2)}, u32[]{:S(2)}) %collective-permute-start.16) | collective-permute-done | bytes 131104 | tf_op jit(solution)/shard_map/ppermute | solution.py:385
  146.2 0.8 broadcast_in_dim.27
  147.0 4.5 %all-to-all-start.5 = ((f32[64,8,128]{2,1,0:T(8,128)}), f32[64,8,128]{2,1,0:T(8,128)S(1)}, u32[]{:S(2)}, u32[]{:S(2)}) async-start(f32[64,8,128]{2,1,0:T(8,128)} %broadcast_in_dim.27), calls=%async_computation.5 | async-start | bytes 524288 | tf_op jit(solution)/shard_map/all_to_all | solution.py:376
  151.6 0.1 collective-permute-start.18
  151.7 0.5 collective-permute-start.19
  152.2 1.2 collective-permute-done.19.refs_5_
  153.4 0.6 copy-done.7
  154.0 0.7 copy-done.5
  154.7 8.4 %input_conv.1 = bf16[128,1024]{1,0:T(8,128)(2,1)} custom-call(s32[8]{0:T(128)} %compare_select_fusion.4.place_ref, s32[256]{0:T(256)} %order_ref.7, bf16[128,1024]{1,0:T(8,128)(2,1)} %get-tuple-element.57.refs_0_, bf16[128,1024]{1,0:T(8,128)(2,1)} %copy-done.4, bf16[128,1024]{1,0:T(8,128)(2,1)} %copy-done.3, bf16[128,1024]{1,0:T(8,128)(2,1)} %copy-done.5, ...), custom_call_target="tpu_custom_call" | custom-call | flops 1048576 | bytes 1048576 | tf_op jit(solution)/shard_map/input_conv/pallas_call | solution.py:355
  163.2 1.6 all-to-all-done.5
  164.7 1.5 collective-permute-done.20
  166.3 0.8 pad_maximum_fusion
  (59 shorter events, 0.4 us)
Async XLA Ops:
  0.6 16.5 %copy-start.1 = (bf16[3,2048,128]{2,1,0:T(8,128)(2,1)S(1)}, bf16[3,2048,128]{2,1,0:T(8,128)(2,1)}, u32[]{:S(2)}) copy-start(bf16[3,2048,128]{2,1,0:T(8,128)(2,1)} %w_own.1) | copy-start | bytes 4718596
  2.4 10.9 %collective-permute-start = (bf16[128,256]{1,0:T(8,128)(2,1)}, bf16[128,256]{1,0:T(8,128)(2,1)S(1)}, u32[]{:S(2)}, u32[]{:S(2)}) collective-permute-start(bf16[128,256]{1,0:T(8,128)(2,1)} %get-tuple-element.36), channel_id=1, source_target_pairs={{0,128},{128,0},{1,129},{129,1},{2,130},{130,2},{3,131},{131,3},{4... | collective-permute-start | bytes 196616 | tf_op jit(solution)/shard_map/ppermute | solution.py:380
  3.3 13.9 %copy-start.12 = (s32[256]{0:T(256)S(1)}, s32[256]{0:T(256)}, u32[]{:S(2)}) copy-start(s32[256]{0:T(256)} %order_ref.7) | copy-start | bytes 3076
  3.3 27.0 %all-to-all-start = ((bf16[8,128,256]{2,1,0:T(8,128)(2,1)}), bf16[8,128,256]{2,1,0:T(8,128)(2,1)S(1)}, u32[]{:S(2)}, u32[]{:S(2)}) async-start(bf16[8,128,256]{2,1,0:T(8,128)(2,1)} %get-tuple-element.35), calls=%async_computation | async-start | bytes 1048576 | tf_op jit(solution)/shard_map/all_to_all | solution.py:403
  13.4 13.9 %copy-start.8 = (bf16[128,1024]{1,0:T(8,128)(2,1)S(1)}, bf16[128,1024]{1,0:T(8,128)(2,1)}, u32[]{:S(2)}) copy-start(bf16[128,1024]{1,0:T(8,128)(2,1)} %refs_0_.1) | copy-start | bytes 786436
  14.1 8.1 %collective-permute-start.1 = (bf16[256,256]{1,0:T(8,128)(2,1)S(1)}, bf16[256,256]{1,0:T(8,128)(2,1)S(1)}, u32[]{:S(2)}, u32[]{:S(2)}) collective-permute-start(bf16[256,256]{1,0:T(8,128)(2,1)S(1)} %get-tuple-element.78), channel_id=1, source_target_pairs={{32,0},{64,32},{96,64},{0,96},{33,1},{65,33},{97,65},{1,97},{34,2}... | collective-permute-start | bytes 393224 | tf_op jit(solution)/shard_map/ppermute | solution.py:389
  17.3 7.9 %collective-permute-start.2 = (bf16[256,256]{1,0:T(8,128)(2,1)S(1)}, bf16[256,256]{1,0:T(8,128)(2,1)S(1)}, u32[]{:S(2)}, u32[]{:S(2)}) collective-permute-start(bf16[256,256]{1,0:T(8,128)(2,1)S(1)} %get-tuple-element.78), channel_id=1, source_target_pairs={{64,0},{96,32},{0,64},{32,96},{65,1},{97,33},{1,65},{33,97},{66,2}... | collective-permute-start | bytes 393224 | tf_op jit(solution)/shard_map/ppermute | solution.py:389
  19.8 6.7 %collective-permute-start.3 = (bf16[256,256]{1,0:T(8,128)(2,1)S(1)}, bf16[256,256]{1,0:T(8,128)(2,1)S(1)}, u32[]{:S(2)}, u32[]{:S(2)}) collective-permute-start(bf16[256,256]{1,0:T(8,128)(2,1)S(1)} %get-tuple-element.78), channel_id=1, source_target_pairs={{96,0},{0,32},{32,64},{64,96},{97,1},{1,33},{33,65},{65,97},{98,2}... | collective-permute-start | bytes 393224 | tf_op jit(solution)/shard_map/ppermute | solution.py:389
  27.3 2.1 %collective-permute-start.4 = (bf16[1024,256]{1,0:T(8,128)(2,1)}, bf16[1024,256]{1,0:T(8,128)(2,1)S(1)}, u32[]{:S(2)}, u32[]{:S(2)}) collective-permute-start(bf16[1024,256]{1,0:T(8,128)(2,1)} %get-tuple-element.70), channel_id=1, source_target_pairs={{0,2},{2,0},{1,3},{3,1},{4,6},{6,4},{5,7},{7,5},{8,10},{10,8},{9,1... | collective-permute-start | bytes 1572872 | tf_op jit(solution)/shard_map/ppermute | solution.py:380
  27.3 21.5 %collective-permute-start.5 = (bf16[3,1024,128]{2,1,0:T(8,128)(2,1)S(1)}, bf16[3,1024,128]{2,1,0:T(8,128)(2,1)S(1)}, u32[]{:S(2)}, u32[]{:S(2)}) collective-permute-start(bf16[3,1024,128]{2,1,0:T(8,128)(2,1)S(1)} %constant_dynamic-slice_fusion.1), channel_id=1, source_target_pairs={{0,1},{1,0},{2,3},{3,2},{4,5},{5,4},{6,7},{7,6},{8,9},{9,8},{10,11... | collective-permute-start | bytes 2359304 | tf_op jit(solution)/shard_map/ppermute | solution.py:380
  30.3 0.8 copy-start
  37.4 15.4 %all-to-all-start.1 = ((f32[8,2,1024]{2,1,0:T(2,128)}), f32[8,2,1024]{2,1,0:T(2,128)S(1)}, u32[]{:S(2)}, u32[]{:S(2)}) async-start(f32[8,2,1024]{2,1,0:T(2,128)} %attention_stats.1), calls=%async_computation.1 | async-start | bytes 131072 | tf_op jit(solution)/shard_map/all_to_all | solution.py:418
  48.9 14.0 %copy-start.13 = (bf16[3,1024,128]{2,1,0:T(8,128)(2,1)}, bf16[3,1024,128]{2,1,0:T(8,128)(2,1)S(1)}, u32[]{:S(2)}) copy-start(bf16[3,1024,128]{2,1,0:T(8,128)(2,1)S(1)} %collective-permute-done.5.w_other) | copy-start | bytes 2359300
  52.8 0.6 copy-start.9
  62.9 13.5 %collective-permute-start.6 = (f32[1024,256]{1,0:T(8,128)}, f32[1024,256]{1,0:T(8,128)S(1)}, u32[]{:S(2)}, u32[]{:S(2)}) collective-permute-start(f32[1024,256]{1,0:T(8,128)} %get-tuple-element.43), channel_id=1, source_target_pairs={{0,2},{2,0},{1,3},{3,1},{4,6},{6,4},{5,7},{7,5},{8,10},{10,8},{9,1... | collective-permute-start | bytes 3145736 | tf_op jit(solution)/shard_map/ppermute | solution.py:380
  62.9 19.8 %all-to-all-start.2 = ((bf16[8,128,128]{2,1,0:T(8,128)(2,1)}), bf16[8,128,128]{2,1,0:T(8,128)(2,1)S(1)}, u32[]{:S(2)}, u32[]{:S(2)}) async-start(bf16[8,128,128]{2,1,0:T(8,128)(2,1)} %bitcast.20), calls=%async_computation.2 | async-start | bytes 524288 | tf_op jit(solution)/shard_map/all_to_all | solution.py:424
  66.3 16.4 %collective-permute-start.7 = (bf16[128,1024]{1,0:T(8,128)(2,1)S(1)}, bf16[128,1024]{1,0:T(8,128)(2,1)S(1)}, u32[]{:S(2)}, u32[]{:S(2)}) collective-permute-start(bf16[128,1024]{1,0:T(8,128)(2,1)S(1)} %copy-done.8), channel_id=1, source_target_pairs={{0,4},{2,6},{4,8},{6,10},{8,12},{10,14},{12,16},{14,18},{16,20},{1... | collective-permute-start | bytes 786440 | tf_op jit(solution)/shard_map/ppermute | solution.py:385
  70.1 9.4 %collective-permute-start.8 = (bf16[64,1024]{1,0:T(8,128)(2,1)S(1)}, bf16[64,1024]{1,0:T(8,128)(2,1)S(1)}, u32[]{:S(2)}, u32[]{:S(2)}) collective-permute-start(bf16[64,1024]{1,0:T(8,128)(2,1)S(1)} %constant_dynamic-slice_fusion), channel_id=1, source_target_pairs={{4,0},{6,2},{8,4},{10,6},{12,8},{14,10},{16,12},{18,14},{20,16},{2... | collective-permute-start | bytes 393224 | tf_op jit(solution)/shard_map/ppermute | solution.py:385
  79.5 23.4 %copy-start.17 = (bf16[64,1024]{1,0:T(8,128)(2,1)}, bf16[64,1024]{1,0:T(8,128)(2,1)S(1)}, u32[]{:S(2)}) copy-start(bf16[64,1024]{1,0:T(8,128)(2,1)S(1)} %collective-permute-done.8.refs_4_) | copy-start | bytes 393220
  82.7 20.3 %copy-start.14 = (bf16[128,1024]{1,0:T(8,128)(2,1)}, bf16[128,1024]{1,0:T(8,128)(2,1)S(1)}, u32[]{:S(2)}) copy-start(bf16[128,1024]{1,0:T(8,128)(2,1)S(1)} %collective-permute-done.7.refs_2_) | copy-start | bytes 786436
  82.7 12.0 %all-to-all-start.3 = ((bf16[8,128,256]{2,1,0:T(8,128)(2,1)}), bf16[8,128,256]{2,1,0:T(8,128)(2,1)S(1)}, u32[]{:S(2)}, u32[]{:S(2)}) async-start(bf16[8,128,256]{2,1,0:T(8,128)(2,1)} %bitcast.3), calls=%async_computation.3 | async-start | bytes 1048576 | tf_op jit(solution)/shard_map/all_to_all | solution.py:427
  86.2 2.1 %collective-permute-start.10 = (bf16[128,1024]{1,0:T(8,128)(2,1)S(1)}, bf16[128,1024]{1,0:T(8,128)(2,1)S(1)}, u32[]{:S(2)}, u32[]{:S(2)}) collective-permute-start(bf16[128,1024]{1,0:T(8,128)(2,1)S(1)} %collective-permute-done.7.refs_2_), channel_id=1, source_target_pairs={{0,2},{2,0},{1,3},{3,1},{4,6},{6,4},{5,7},{7,5},{8,10},{10,8},{9,1... | collective-permute-start | bytes 786440 | tf_op jit(solution)/shard_map/ppermute | solution.py:380
  86.2 2.1 %collective-permute-start.9 = (bf16[128,1024]{1,0:T(8,128)(2,1)S(1)}, bf16[128,1024]{1,0:T(8,128)(2,1)S(1)}, u32[]{:S(2)}, u32[]{:S(2)}) collective-permute-start(bf16[128,1024]{1,0:T(8,128)(2,1)S(1)} %copy-done.8), channel_id=1, source_target_pairs={{0,2},{2,0},{1,3},{3,1},{4,6},{6,4},{5,7},{7,5},{8,10},{10,8},{9,1... | collective-permute-start | bytes 786440 | tf_op jit(solution)/shard_map/ppermute | solution.py:380
  86.7 1.6 collective-permute-start.11
  88.3 14.6 %copy-start.18 = (bf16[64,1024]{1,0:T(8,128)(2,1)}, bf16[64,1024]{1,0:T(8,128)(2,1)S(1)}, u32[]{:S(2)}) copy-start(bf16[64,1024]{1,0:T(8,128)(2,1)S(1)} %collective-permute-done.11.refs_5_) | copy-start | bytes 393220
  88.3 14.6 %copy-start.15 = (bf16[128,1024]{1,0:T(8,128)(2,1)}, bf16[128,1024]{1,0:T(8,128)(2,1)S(1)}, u32[]{:S(2)}) copy-start(bf16[128,1024]{1,0:T(8,128)(2,1)S(1)} %collective-permute-done.10.refs_3_) | copy-start | bytes 786436
  88.3 14.6 %copy-start.16 = (bf16[128,1024]{1,0:T(8,128)(2,1)}, bf16[128,1024]{1,0:T(8,128)(2,1)S(1)}, u32[]{:S(2)}) copy-start(bf16[128,1024]{1,0:T(8,128)(2,1)S(1)} %collective-permute-done.9.refs_1_) | copy-start | bytes 786436
  94.8 8.2 %copy-start.10 = (bf16[128,256]{1,0:T(8,128)(2,1)}, bf16[128,256]{1,0:T(8,128)(2,1)S(1)}, u32[]{:S(2)}) copy-start(bf16[128,256]{1,0:T(8,128)(2,1)S(1)} %reduce_sum.34.kv_own) | copy-start | bytes 196612
  94.8 8.1 %collective-permute-start.13 = (bf16[128,256]{1,0:T(8,128)(2,1)S(1)}, bf16[128,256]{1,0:T(8,128)(2,1)S(1)}, u32[]{:S(2)}, u32[]{:S(2)}) collective-permute-start(bf16[128,256]{1,0:T(8,128)(2,1)S(1)} %reduce_sum.34.kv_own), channel_id=1, source_target_pairs={{0,1},{1,0},{2,3},{3,2},{4,5},{5,4},{6,7},{7,6},{8,9},{9,8},{10,11... | collective-permute-start | bytes 196616 | tf_op jit(solution)/shard_map/ppermute | solution.py:380
  97.4 5.6 %copy-start.11 = (bf16[128,128]{1,0:T(8,128)(2,1)}, bf16[128,128]{1,0:T(8,128)(2,1)S(1)}, u32[]{:S(2)}) copy-start(bf16[128,128]{1,0:T(8,128)(2,1)S(1)} %reduce_sum.33.q_own) | copy-start | bytes 98308
  97.4 5.5 %collective-permute-start.12 = (bf16[128,128]{1,0:T(8,128)(2,1)S(1)}, bf16[128,128]{1,0:T(8,128)(2,1)S(1)}, u32[]{:S(2)}, u32[]{:S(2)}) collective-permute-start(bf16[128,128]{1,0:T(8,128)(2,1)S(1)} %reduce_sum.33.q_own), channel_id=1, source_target_pairs={{0,1},{1,0},{2,3},{3,2},{4,5},{5,4},{6,7},{7,6},{8,9},{9,8},{10,11... | collective-permute-start | bytes 98312 | tf_op jit(solution)/shard_map/ppermute | solution.py:380
  102.9 0.6 copy-start.21
  103.5 0.6 copy-start.20
  113.9 13.4 %copy-start.2 = (bf16[128,1024]{1,0:T(8,128)(2,1)S(1)}, bf16[128,1024]{1,0:T(8,128)(2,1)}, u32[]{:S(2)}) copy-start(bf16[128,1024]{1,0:T(8,128)(2,1)} %get-tuple-element.57.refs_0_) | copy-start | bytes 786436
  113.9 20.2 %copy-start.19 = (bf16[64,1024]{1,0:T(8,128)(2,1)S(1)}, bf16[64,1024]{1,0:T(8,128)(2,1)}, u32[]{:S(2)}) copy-start(bf16[64,1024]{1,0:T(8,128)(2,1)} %get-tuple-element.58) | copy-start | bytes 393220
  115.0 1.6 collective-permute-start.14
  118.3 27.9 %all-to-all-start.4 = ((f32[64,8,128]{2,1,0:T(8,128)}), f32[64,8,128]{2,1,0:T(8,128)S(1)}, u32[]{:S(2)}, u32[]{:S(2)}) async-start(f32[64,8,128]{2,1,0:T(8,128)} %fusion), calls=%async_computation.4 | async-start | bytes 524288 | tf_op jit(solution)/shard_map/all_to_all | solution.py:443
  127.3 18.8 %collective-permute-start.15 = (bf16[128,1024]{1,0:T(8,128)(2,1)S(1)}, bf16[128,1024]{1,0:T(8,128)(2,1)S(1)}, u32[]{:S(2)}, u32[]{:S(2)}) collective-permute-start(bf16[128,1024]{1,0:T(8,128)(2,1)S(1)} %copy-done.2), channel_id=1, source_target_pairs={{4,0},{6,2},{8,4},{10,6},{12,8},{14,10},{16,12},{18,14},{20,16},{2... | collective-permute-start | bytes 786440 | tf_op jit(solution)/shard_map/ppermute | solution.py:385
  134.0 12.1 %collective-permute-start.17 = (bf16[128,1024]{1,0:T(8,128)(2,1)S(1)}, bf16[128,1024]{1,0:T(8,128)(2,1)S(1)}, u32[]{:S(2)}, u32[]{:S(2)}) collective-permute-start(bf16[128,1024]{1,0:T(8,128)(2,1)S(1)} %copy-done.2), channel_id=1, source_target_pairs={{0,2},{2,0},{1,3},{3,1},{4,6},{6,4},{5,7},{7,5},{8,10},{10,8},{9,1... | collective-permute-start | bytes 786440 | tf_op jit(solution)/shard_map/ppermute | solution.py:380
  134.1 12.0 %collective-permute-start.16 = (bf16[64,1024]{1,0:T(8,128)(2,1)S(1)}, bf16[64,1024]{1,0:T(8,128)(2,1)S(1)}, u32[]{:S(2)}, u32[]{:S(2)}) collective-permute-start(bf16[64,1024]{1,0:T(8,128)(2,1)S(1)} %copy-done.19), channel_id=1, source_target_pairs={{0,4},{2,6},{4,8},{6,10},{8,12},{10,14},{12,16},{14,18},{16,20},{1... | collective-permute-start | bytes 393224 | tf_op jit(solution)/shard_map/ppermute | solution.py:385
  146.1 7.3 %copy-start.6 = (bf16[64,1024]{1,0:T(8,128)(2,1)}, bf16[64,1024]{1,0:T(8,128)(2,1)S(1)}, u32[]{:S(2)}) copy-start(bf16[64,1024]{1,0:T(8,128)(2,1)S(1)} %collective-permute-done.16.refs_4_) | copy-start | bytes 393220
  146.1 7.3 %copy-start.3 = (bf16[128,1024]{1,0:T(8,128)(2,1)}, bf16[128,1024]{1,0:T(8,128)(2,1)S(1)}, u32[]{:S(2)}) copy-start(bf16[128,1024]{1,0:T(8,128)(2,1)S(1)} %collective-permute-done.15.refs_2_) | copy-start | bytes 786436
  146.1 7.3 %copy-start.4 = (bf16[128,1024]{1,0:T(8,128)(2,1)}, bf16[128,1024]{1,0:T(8,128)(2,1)S(1)}, u32[]{:S(2)}) copy-start(bf16[128,1024]{1,0:T(8,128)(2,1)S(1)} %collective-permute-done.17.refs_1_) | copy-start | bytes 786436
  147.0 17.7 %all-to-all-start.5 = ((f32[64,8,128]{2,1,0:T(8,128)}), f32[64,8,128]{2,1,0:T(8,128)S(1)}, u32[]{:S(2)}, u32[]{:S(2)}) async-start(f32[64,8,128]{2,1,0:T(8,128)} %broadcast_in_dim.27), calls=%async_computation.5 | async-start | bytes 524288 | tf_op jit(solution)/shard_map/all_to_all | solution.py:376
  151.6 1.8 %collective-permute-start.18 = (bf16[128,1024]{1,0:T(8,128)(2,1)S(1)}, bf16[128,1024]{1,0:T(8,128)(2,1)S(1)}, u32[]{:S(2)}, u32[]{:S(2)}) collective-permute-start(bf16[128,1024]{1,0:T(8,128)(2,1)S(1)} %collective-permute-done.15.refs_2_), channel_id=1, source_target_pairs={{0,2},{2,0},{1,3},{3,1},{4,6},{6,4},{5,7},{7,5},{8,10},{10,8},{9,1... | collective-permute-start | bytes 786440 | tf_op jit(solution)/shard_map/ppermute | solution.py:380
  151.7 1.7 %collective-permute-start.19 = (bf16[64,1024]{1,0:T(8,128)(2,1)S(1)}, bf16[64,1024]{1,0:T(8,128)(2,1)S(1)}, u32[]{:S(2)}, u32[]{:S(2)}) collective-permute-start(bf16[64,1024]{1,0:T(8,128)(2,1)S(1)} %collective-permute-done.16.refs_4_), channel_id=1, source_target_pairs={{0,2},{2,0},{1,3},{3,1},{4,6},{6,4},{5,7},{7,5},{8,10},{10,8},{9,1... | collective-permute-start | bytes 393224 | tf_op jit(solution)/shard_map/ppermute | solution.py:380
  153.4 0.7 copy-start.7
  154.0 0.7 copy-start.5
  164.7 1.5 collective-permute-start.20
